TPU v7x, 32 devices: a whole 2x2x4 slice. The times are simulated.
32 devices in a mesh: dp: 4 (over y, x), mp: 8 (over z, core).
Axes of the slice: x: 2, y: 2, z: 4, core: 2. Of those that a mesh axis runs over, the one named last changes fastest.
Arguments:
- inputs: bfloat16 [8192, 2048], P(('dp', 'mp')), may hold values from -6 to 6
- cotangent: bfloat16 [8192, 2048], P(('dp', 'mp')), may hold values from -6 to 6
- widths: int32 [4], P('dp'), may hold values from 0 to 3, as said below
- norm_gain: float32 [2048], replicated, may hold values from 0.5 to 1.5
- in_weight: bfloat16 [2048, 8512], P('mp'), may hold values from -0.125 to 0.125
- conv_weight: float32 [4, 4352], replicated, may hold values from -3 to 3
- conv_bias: float32 [4352], replicated, may hold values from -3 to 3
- step_bias: float32 [64], replicated, may hold values from -4 to -0.5
- rate_log: float32 [64], replicated, may hold values from -4.6 to -0.7
- skip_gain: float32 [64], replicated, may hold values from 0.5 to 1.5
- out_gain: float32 [4096], replicated, may hold values from 0.5 to 1.5
- out_weight: bfloat16 [4096, 2048], P('mp'), may hold values from -0.09375 to 0.09375
Outputs:
- outputs: bfloat16 [8192, 2048], P(('dp', 'mp'))
- input_grad: bfloat16 [8192, 2048], P(('dp', 'mp'))
- norm_gain_grad: float32 [2048], replicated
- in_weight_grad: float32 [2048, 8512], P('mp')
- conv_weight_grad: float32 [4, 4352], replicated
- conv_bias_grad: float32 [4352], replicated
- step_bias_grad: float32 [64], replicated
- rate_log_grad: float32 [64], replicated
- skip_gain_grad: float32 [64], replicated
- out_gain_grad: float32 [4096], replicated
- out_weight_grad: float32 [4096, 2048], P('mp')
Inputs may be any that keep to these rules, and one draw needn't show every extreme that they name: `widths`: each index of dp holds 1 sequence in a row, and at least one of them has width index 3.
All inputs are finite; a program needn't handle non-finite values.
Results may differ from a plain program's by a relative error of at most 0.01.
Values may be sent and summed in bfloat16 or wider, within the bound.
No kernel may reach another device: no remote copies, remote signals or barrier semaphores. Data moves between devices by JAX's collectives and lax.ppermute only.
A program may use at most 320 MiB of HBM per device.

v0:
```python
import jax
import jax.numpy as jnp
from jax import lax
from jax.sharding import PartitionSpec as P

STRETCH = 256
SEQ = 2048
INNER = 4096


EPS = 1e-05
HIGH = lax.Precision.HIGHEST


def conv_act(extended, conv_weight, conv_bias):
    conv_span = conv_weight.shape[0]
    length = extended.shape[0] - conv_span + 1
    summed = conv_bias[None, :] + extended[0:length] * conv_weight[0][None, :]
    for offset in range(1, conv_span):
        summed = summed + extended[offset : offset + length] * conv_weight[offset][None, :]
    return jax.nn.silu(summed)


def prepare(
    extended, step_raw, conv_weight, conv_bias, step_bias, rate_log, head_mask, inner_width
):
    conv_out = conv_act(extended, conv_weight, conv_bias)
    length = conv_out.shape[0]
    head_count = step_raw.shape[1]
    state_dim = (conv_out.shape[1] - inner_width) // 2
    values = (
        conv_out[:, :inner_width].reshape(length, head_count, inner_width // head_count)
        * head_mask[None, :, None]
    )
    b_coef = conv_out[:, inner_width : inner_width + state_dim]
    c_coef = conv_out[:, inner_width + state_dim :]
    step_size = jax.nn.softplus(step_raw + step_bias[None, :])
    decay_rate = -jnp.exp(rate_log)[None, :] * step_size
    scaled = values * step_size[:, :, None]
    return (values, scaled, b_coef, c_coef, decay_rate)


def stretch_step(carry_state, block_parts):
    scaled, b_coef, c_coef, decay_rate = block_parts
    cumulative = jnp.cumsum(decay_rate, axis=0)
    block_len = decay_rate.shape[0]
    causal = lax.broadcasted_iota(jnp.int32, (block_len, block_len), 0) >= lax.broadcasted_iota(
        jnp.int32, (block_len, block_len), 1
    )
    gap_logs = jnp.where(causal[:, :, None], cumulative[:, None, :] - cumulative[None, :, :], -1e30)
    scores = jnp.dot(c_coef, b_coef.T, precision=HIGH)
    mixing = scores[:, :, None] * jnp.exp(gap_logs)
    within = jnp.einsum("lsh,shp->lhp", mixing, scaled, precision=HIGH)
    carried = (
        jnp.einsum("ln,hpn->lhp", c_coef, carry_state, precision=HIGH)
        * jnp.exp(cumulative)[:, :, None]
    )
    tail_logs = jnp.exp(cumulative[-1][None, :] - cumulative)
    fresh_state = jnp.einsum("sh,shp,sn->hpn", tail_logs, scaled, b_coef, precision=HIGH)
    new_state = carry_state * jnp.exp(cumulative[-1])[:, None, None] + fresh_state
    return (new_state, within + carried)


def run_stretches(scaled, b_coef, c_coef, decay_rate, carry_state):
    length = scaled.shape[0]
    head_count = scaled.shape[1]
    head_dim = scaled.shape[2]
    block_count = length // STRETCH
    block_parts = (
        scaled.reshape(block_count, STRETCH, head_count, head_dim),
        b_coef.reshape(block_count, STRETCH, b_coef.shape[1]),
        c_coef.reshape(block_count, STRETCH, c_coef.shape[1]),
        decay_rate.reshape(block_count, STRETCH, head_count),
    )
    final_state, outputs = lax.scan(jax.checkpoint(stretch_step), carry_state, block_parts)
    return (final_state, outputs.reshape(length, head_count, head_dim))


def width_mask(width_index, first_head, local_heads, head_count):
    active_heads = head_count // 8 * jnp.left_shift(jnp.int32(1), width_index)
    return (first_head + jnp.arange(local_heads, dtype=jnp.int32) < active_heads).astype(
        jnp.float32
    )


def local_params(conv_weight, conv_bias, step_bias, rate_log, skip_gain, inner_width):
    head_count = step_bias.shape[0]
    local_heads = head_count // lax.axis_size("mp")
    head_dim = inner_width // head_count
    first_head = lax.axis_index("mp") * local_heads
    first_chan = first_head * head_dim
    conv_local = jnp.concatenate(
        [
            lax.dynamic_slice_in_dim(conv_weight, first_chan, local_heads * head_dim, 1),
            conv_weight[:, inner_width:],
        ],
        axis=1,
    )
    bias_local = jnp.concatenate(
        [
            lax.dynamic_slice_in_dim(conv_bias, first_chan, local_heads * head_dim, 0),
            conv_bias[inner_width:],
        ],
        axis=0,
    )
    local_weights = (
        conv_local,
        bias_local,
        lax.dynamic_slice_in_dim(step_bias, first_head, local_heads, 0),
        lax.dynamic_slice_in_dim(rate_log, first_head, local_heads, 0),
        lax.dynamic_slice_in_dim(skip_gain, first_head, local_heads, 0),
    )
    return (local_weights, first_head)


def head_mixer(seq_values, seq_steps, seq_coef, local_weights, seq_mask):
    conv_local, bias_local, step_local, rate_local, skip_local = local_weights
    inner_local = seq_values.shape[1]
    joined = jnp.concatenate([seq_values, seq_coef], axis=1)
    extended = jnp.concatenate(
        [jnp.zeros((conv_local.shape[0] - 1, joined.shape[1]), jnp.float32), joined], axis=0
    )
    values, scaled, b_coef, c_coef, decay_rate = prepare(
        extended, seq_steps, conv_local, bias_local, step_local, rate_local, seq_mask, inner_local
    )
    start_state = jnp.zeros((values.shape[1], values.shape[2], b_coef.shape[1]), jnp.float32)
    _, mixed = run_stretches(scaled, b_coef, c_coef, decay_rate, start_state)
    return (mixed + skip_local[None, :, None] * values).reshape(seq_values.shape[0], inner_local)


def heads_forward(conv_input, step_raw, widths, local_weights, first_head, inner_width):
    tok_count = conv_input.shape[0]
    head_count = step_raw.shape[1]
    head_dim = inner_width // head_count
    mp_size = lax.axis_size("mp")
    local_heads = head_count // mp_size
    per_token = conv_input[:, :inner_width].reshape(tok_count, head_count, head_dim)
    shared = jnp.broadcast_to(
        conv_input[:, None, inner_width:], (tok_count, mp_size, conv_input.shape[1] - inner_width)
    )
    got_values, got_steps, got_coef = (
        lax.all_to_all(per_token, "mp", split_axis=1, concat_axis=0, tiled=True),
        lax.all_to_all(step_raw, "mp", split_axis=1, concat_axis=0, tiled=True),
        lax.all_to_all(shared, "mp", split_axis=1, concat_axis=0, tiled=True),
    )
    seq_count = widths.shape[0]
    seq_len = got_values.shape[0] // seq_count
    seq_inputs = (
        got_values.reshape(seq_count, seq_len, local_heads * head_dim),
        got_steps.reshape(seq_count, seq_len, local_heads),
        got_coef.reshape(seq_count, seq_len, got_coef.shape[2]),
        widths,
    )

    def forward_one(seq_item):
        seq_values, seq_steps, seq_coef, width_index = seq_item
        seq_mask = width_mask(width_index, first_head, local_heads, head_count)

        def forward_compute(unused):
            return head_mixer(
                seq_values.astype(jnp.float32),
                seq_steps.astype(jnp.float32),
                seq_coef.astype(jnp.float32),
                local_weights,
                seq_mask,
            )

        def forward_skipped(unused):
            return jnp.zeros((seq_len, local_heads * head_dim), jnp.float32)

        return lax.cond(jnp.max(seq_mask) > 0, forward_compute, forward_skipped, 0).astype(
            jnp.bfloat16
        )

    mixed_seqs = lax.map(forward_one, seq_inputs)
    mixed_heads = mixed_seqs.reshape(seq_count * seq_len, local_heads, head_dim)
    back_tokens = lax.all_to_all(mixed_heads, "mp", split_axis=0, concat_axis=1, tiled=True)
    return (back_tokens.reshape(tok_count, inner_width), seq_inputs)


def heads_backward(
    d_mixed, seq_inputs, local_weights, first_head, inner_width, head_count, conv_width
):
    tok_count = d_mixed.shape[0]
    head_dim = inner_width // head_count
    local_heads = local_weights[2].shape[0]
    got_grad = lax.all_to_all(
        d_mixed.reshape(tok_count, head_count, head_dim),
        "mp",
        split_axis=1,
        concat_axis=0,
        tiled=True,
    )
    seq_count = seq_inputs[3].shape[0]
    seq_len = got_grad.shape[0] // seq_count
    seq_grads = got_grad.reshape(seq_count, seq_len, local_heads * head_dim)

    def backward_one(seq_item):
        seq_values, seq_steps, seq_coef, width_index, seq_dy = seq_item
        seq_mask = width_mask(width_index, first_head, local_heads, head_count)

        def backward_compute(unused):
            _, pullback = jax.vjp(
                lambda part_v, part_s, part_c, part_w: head_mixer(
                    part_v, part_s, part_c, part_w, seq_mask
                ),
                seq_values.astype(jnp.float32),
                seq_steps.astype(jnp.float32),
                seq_coef.astype(jnp.float32),
                local_weights,
            )
            return pullback(seq_dy.astype(jnp.float32))

        def backward_skipped(unused):
            return (
                jnp.zeros(seq_values.shape, jnp.float32),
                jnp.zeros(seq_steps.shape, jnp.float32),
                jnp.zeros(seq_coef.shape, jnp.float32),
                jax.tree.map(jnp.zeros_like, local_weights),
            )

        return lax.cond(jnp.max(seq_mask) > 0, backward_compute, backward_skipped, 0)

    d_values, d_steps, d_coef, d_local = lax.map(backward_one, seq_inputs + (seq_grads,))
    d_local = jax.tree.map(lambda piece: jnp.sum(piece, axis=0), d_local)
    group_tokens = seq_count * seq_len
    send_values = d_values.reshape(group_tokens, local_heads, head_dim).astype(jnp.bfloat16)
    send_steps = d_steps.reshape(group_tokens, local_heads).astype(jnp.bfloat16)
    back_values, back_steps = (
        lax.all_to_all(send_values, "mp", split_axis=0, concat_axis=1, tiled=True),
        lax.all_to_all(send_steps, "mp", split_axis=0, concat_axis=1, tiled=True),
    )
    coef_grad = lax.psum_scatter(
        d_coef.reshape(group_tokens, d_coef.shape[2]), "mp", scatter_dimension=0, tiled=True
    )
    d_conv_input = jnp.concatenate(
        [back_values.reshape(tok_count, inner_width), coef_grad.astype(jnp.bfloat16)], axis=1
    )
    conv_local_grad, bias_local_grad, step_local_grad, rate_local_grad, skip_local_grad = d_local
    local_chan = local_heads * head_dim
    first_chan = first_head * head_dim
    conv_weight_grad = jnp.zeros((conv_local_grad.shape[0], conv_width), jnp.float32)
    conv_weight_grad = lax.dynamic_update_slice_in_dim(
        conv_weight_grad, conv_local_grad[:, :local_chan], first_chan, 1
    )
    conv_weight_grad = conv_weight_grad.at[:, inner_width:].set(conv_local_grad[:, local_chan:])
    conv_bias_grad = jnp.zeros((conv_width,), jnp.float32)
    conv_bias_grad = lax.dynamic_update_slice_in_dim(
        conv_bias_grad, bias_local_grad[:local_chan], first_chan, 0
    )
    conv_bias_grad = conv_bias_grad.at[inner_width:].set(bias_local_grad[local_chan:])
    head_zeros = jnp.zeros((head_count,), jnp.float32)
    step_bias_grad = lax.dynamic_update_slice_in_dim(head_zeros, step_local_grad, first_head, 0)
    rate_log_grad = lax.dynamic_update_slice_in_dim(head_zeros, rate_local_grad, first_head, 0)
    skip_gain_grad = lax.dynamic_update_slice_in_dim(head_zeros, skip_local_grad, first_head, 0)
    return (
        d_conv_input,
        back_steps,
        (conv_weight_grad, conv_bias_grad, step_bias_grad, rate_log_grad, skip_gain_grad),
    )


def on_device(
    inputs,
    cotangent,
    widths,
    norm_gain,
    in_weight,
    conv_weight,
    conv_bias,
    step_bias,
    rate_log,
    skip_gain,
    out_gain,
    out_weight,
):
    inner_width = INNER
    head_count = step_bias.shape[0]
    head_dim = inner_width // head_count
    conv_width = conv_bias.shape[0]
    tok_count = inputs.shape[0]
    pieces = SEQ // tok_count
    mp_place = lax.axis_index("mp")
    width_index = lax.dynamic_index_in_dim(widths, mp_place // pieces, 0, keepdims=False)
    active_heads = head_count // 8 * jnp.left_shift(jnp.int32(1), width_index)
    head_mask = (jnp.arange(head_count, dtype=jnp.int32) < active_heads).astype(jnp.float32)
    chan_mask = jnp.repeat(head_mask, head_dim)
    active_count = (active_heads * head_dim).astype(jnp.float32)
    in_full, out_full = (
        lax.all_gather(in_weight, "mp", axis=0, tiled=True),
        lax.all_gather(out_weight, "mp", axis=0, tiled=True),
    )
    inputs_f = inputs.astype(jnp.float32)
    mean_sq = jnp.mean(inputs_f * inputs_f, axis=-1, keepdims=True)
    rms_scale = lax.rsqrt(mean_sq + EPS)
    normed = inputs_f * rms_scale
    hidden = (normed * norm_gain[None, :]).astype(jnp.bfloat16)
    projected = jnp.dot(hidden, in_full, preferred_element_type=jnp.float32).astype(jnp.bfloat16)
    gate_z = projected[:, :inner_width].astype(jnp.float32)
    conv_input = projected[:, inner_width : inner_width + conv_width]
    step_raw = projected[:, inner_width + conv_width :]
    local_weights, first_head = local_params(
        conv_weight, conv_bias, step_bias, rate_log, skip_gain, inner_width
    )
    mixed, seq_inputs = heads_forward(
        conv_input, step_raw, widths, local_weights, first_head, inner_width
    )
    y_f = mixed.astype(jnp.float32)
    silu_z = jax.nn.silu(gate_z)
    gated = y_f * silu_z
    mean_g = jnp.sum(gated * gated * chan_mask[None, :], axis=-1, keepdims=True) / active_count
    out_root = lax.rsqrt(mean_g + EPS)
    normed_out = (gated * out_root * out_gain[None, :] * chan_mask[None, :]).astype(jnp.bfloat16)
    outputs = (inputs_f + jnp.dot(normed_out, out_full, preferred_element_type=jnp.float32)).astype(
        jnp.bfloat16
    )
    row_block = normed_out
    out_weight_grad = lax.psum_scatter(
        lax.dot_general(
            row_block, cotangent, (((0,), (0,)), ((), ())), preferred_element_type=jnp.float32
        ),
        "mp",
        scatter_dimension=0,
        tiled=True,
    )
    d_normed = lax.dot_general(
        cotangent, out_full, (((1,), (1,)), ((), ())), preferred_element_type=jnp.float32
    )
    out_gain_grad = jnp.sum(d_normed * gated * out_root * chan_mask[None, :], axis=0)
    upstream = d_normed * out_gain[None, :] * chan_mask[None, :]
    inner_dot = jnp.sum(upstream * gated, axis=-1, keepdims=True)
    d_gated = (
        out_root * upstream
        - out_root * out_root * out_root * chan_mask[None, :] * gated * inner_dot / active_count
    )
    d_y = (d_gated * silu_z).astype(jnp.bfloat16)
    gate_sigmoid = jax.nn.sigmoid(gate_z)
    d_gate_z = d_gated * y_f * gate_sigmoid * (1.0 + gate_z * (1.0 - gate_sigmoid))
    d_conv_input, d_steps, mixer_grads = heads_backward(
        d_y, seq_inputs, local_weights, first_head, inner_width, head_count, conv_width
    )
    d_proj = jnp.concatenate([d_gate_z.astype(jnp.bfloat16), d_conv_input, d_steps], axis=1)
    row_block = hidden
    in_weight_grad = lax.psum_scatter(
        lax.dot_general(
            row_block, d_proj, (((0,), (0,)), ((), ())), preferred_element_type=jnp.float32
        ),
        "mp",
        scatter_dimension=0,
        tiled=True,
    )
    d_hidden = lax.dot_general(
        d_proj, in_full, (((1,), (1,)), ((), ())), preferred_element_type=jnp.float32
    )
    norm_gain_grad = jnp.sum(d_hidden * normed, axis=0)
    d_normed_in = d_hidden * norm_gain[None, :]
    input_back = rms_scale * (
        d_normed_in - normed * jnp.mean(d_normed_in * normed, axis=-1, keepdims=True)
    )
    input_grad = (cotangent.astype(jnp.float32) + input_back).astype(jnp.bfloat16)
    conv_weight_grad, conv_bias_grad, step_bias_grad, rate_log_grad, skip_gain_grad = mixer_grads
    partial_sums = lax.psum(
        (
            norm_gain_grad,
            conv_weight_grad,
            conv_bias_grad,
            step_bias_grad,
            rate_log_grad,
            skip_gain_grad,
            out_gain_grad,
        ),
        "mp",
    )
    totals = lax.psum(
        (
            in_weight_grad,
            out_weight_grad,
            partial_sums[0],
            partial_sums[1],
            partial_sums[2],
            partial_sums[3],
            partial_sums[4],
            partial_sums[5],
            partial_sums[6],
        ),
        "dp",
    )
    return (
        outputs,
        input_grad,
        totals[2],
        totals[0],
        totals[3],
        totals[4],
        totals[5],
        totals[6],
        totals[7],
        totals[8],
        totals[1],
    )


def solution(mesh):
    placed = (
        P(("dp", "mp"), None),
        P(("dp", "mp"), None),
        P("dp"),
        P(),
        P("mp", None),
        P(),
        P(),
        P(),
        P(),
        P(),
        P(),
        P("mp", None),
    )
    return jax.shard_map(
        on_device,
        mesh=mesh,
        in_specs=placed,
        out_specs=(
            P(("dp", "mp"), None),
            P(("dp", "mp"), None),
            P(),
            P("mp", None),
            P(),
            P(),
            P(),
            P(),
            P(),
            P(),
            P("mp", None),
        ),
        check_vma=False,
    )
```

profile of v0, /device:TPU:0, one launch (start us, length us, event | category | flops | bytes accessed | tf_op | source)
XLA Modules:
  0.0 2633.1 jit_solution(14063386649731044326)
XLA Ops:
  9.0 307.1 %all-gather.3.cloned.1.call-done = bf16[2048,8512]{0,1:T(8,128)(2,1)} async-done(((bf16[256,8512]{0,1:T(8,128)(2,1)}), bf16[2048,8512]{0,1:T(8,128)(2,1)}) %all-gather.3.cloned.1.call-update) | async-done | bytes 34865168 | tf_op jit(solution)/shard_map/all_gather | solution.py:290
  316.1 17.8 convolution_convert_fusion
  344.9 48.2 %all-to-all-done.1 = bf16[256,8,256]{0,2,1:T(8,128)(2,1)S(1)} async-done(((bf16[256,8,256]{0,2,1:T(8,128)(2,1)}), bf16[256,8,256]{0,2,1:T(8,128)(2,1)S(1)}, u32[]{:S(2)}, u32[]{:S(2)}) %all-to-all-start.1) | async-done | bytes 1048608 | tf_op jit(solution)/shard_map/all_to_all | solution.py:144
  400.4 101.8 %all-to-all-done = bf16[256,64,64]{0,2,1:T(8,128)(2,1)S(1)} async-done(((bf16[256,64,64]{0,2,1:T(8,128)(2,1)}), bf16[256,64,64]{0,2,1:T(8,128)(2,1)S(1)}, u32[]{:S(2)}, u32[]{:S(2)}) %all-to-all-start) | async-done | bytes 2097184 | tf_op jit(solution)/shard_map/all_to_all | solution.py:142
  512.2 226.9 %conditional.2 = (bf16[2048,512]{0,1:T(8,128)(2,1)}) conditional(s32[]{:T(128)} %convert_element_type.108, () %tuple.78, (f32[768]{0:T(1024)S(1)}, bf16[2048,512]{0,1:T(8,128)(2,1)S(1)}, bf16[2048,256]{1,0:T(8,128)(2,1)}, f32[4,768]{1,0:T(4,128)S(1)}, f32[8]{0:T(128)S(1)}, /*index=5*/bf16[2048,8]{0,1:T(8,128)(2,1)S(1)}, f32[8]{0:T(128)S(1)}, ...), branch_computations={%region_2.3_spmd, %region_3.8_spmd} | conditional | flops 940132352 | bytes 114156712 | solution.py:171
  539.4 191.0 %while.70 = (s32[]{:T(128)}, f32[8,64,128]{2,1,0:T(8,128)S(1)}, f32[8,256,8,64]{1,0,3,2:T(8,128)}, f32[8,256,8]{1,2,0:T(8,128)S(1)}, f32[8,256,8,64]{1,0,3,2:T(8...) while((s32[]{:T(128)}, f32[8,64,128]{2,1,0:T(8,128)S(1)}, ...), condition=%wide.region_7.7_spmd.clone, body=%wide.region_4.6_spmd.clone.sunk | while | flops 908527616 | bytes 7833396 | solution.py:75
  574.4 12.7 dynamic_update_slice.113
  598.3 12.7 dynamic_update_slice.113
  622.2 12.7 dynamic_update_slice.113
  756.9 48.9 %all-to-all-done.3 = bf16[8,2,65536]{2,1,0:T(2,128)(2,1)} async-done(((bf16[8,2,65536]{2,1,0:T(2,128)(2,1)}), bf16[8,2,65536]{2,1,0:T(2,128)(2,1)}, u32[]{:S(2)}, u32[]{:S(2)}) %all-to-all-start.3) | async-done | bytes 2097184 | tf_op jit(solution)/shard_map/all_to_all | solution.py:177
  829.3 13.5 multiply_reduce_fusion.10
  853.3 49.0 %all-to-all-done.4 = bf16[256,64,64]{0,2,1:T(8,128)(2,1)} async-done(((bf16[256,64,64]{0,2,1:T(8,128)(2,1)}), bf16[256,64,64]{0,2,1:T(8,128)(2,1)}, u32[]{:S(2)}, u32[]{:S(2)}) %all-to-all-start.4) | async-done | bytes 2097184 | tf_op jit(solution)/shard_map/all_to_all | solution.py:187
  902.3 373.8 %conditional.3 = (bf16[2048,512]{0,1:T(8,128)(2,1)}, bf16[2048,8]{0,1:T(8,128)(2,1)}, f32[2048,256]{0,1:T(8,128)}, f32[8]{0:T(128)S(1)}, f32[8]{0:T(128)S(1)}, /...) conditional(s32[]{:T(128)} %convert_element_type.108, () %tuple.80, ...), branch_computations={%region_10.11_spmd, %region_11.38_spmd} | conditional | flops 2415493376 | bytes 388250048 | solution.py:222
  937.6 29.1 %while.71 = (s32[]{:T(128)}, f32[8,64,128]{2,1,0:T(8,128)S(1)}, f32[8,8,64,128]{3,2,1,0:T(8,128)}, f32[8,256,8]{1,2,0:T(8,128)S(1)}, f32[8,256,8,64]{1,3,2,0:T(8...) while((s32[]{:T(128)}, f32[8,64,128]{2,1,0:T(8,128)S(1)}, ...), condition=%wide.region_15.15_spmd.clone, body=%wide.region_12.14_spmd.clone.sunk | while | flops 201984032 | bytes 1779999 | solution.py:75
  971.3 257.1 %while.72 = (s32[]{:T(128)}, f32[8,64,128]{2,1,0:T(8,128)S(1)}, f32[8,256,8,64]{1,0,3,2:T(8,128)}, f32[8,256,128]{2,1,0:T(8,128)}, f32[8,256,128]{2,1,0:T(8,128)...) while((s32[]{:T(128)}, f32[8,64,128]{2,1,0:T(8,128)S(1)}, ...), condition=%wide.region_27.27_spmd.clone, body=%wide.region_16.26_spmd.clone.sunk | while | flops 2122334208 | bytes 17361508 | solution.py:75
  1276.9 15.2 fusion.115
  1305.4 54.0 %all_to_all.101 = bf16[8,2,65536]{2,1,0:T(2,128)(2,1)S(1)} all-to-all(bf16[8,2,65536]{2,1,0:T(2,128)(2,1)} %reshape.501), channel_id=1, replica_groups=mesh['dp'=4,'mp'=8] {'mp'}, dimensions={0} | all-to-all | bytes 4194304 | tf_op jit(solution)/shard_map/all_to_all | solution.py:230
  1374.1 30.4 %fusion.109 = f32[2048,8512]{0,1:T(8,128)} fusion(bf16[256,64]{0,1:T(8,128)(2,1)S(1)} %bitcast.384, bf16[256,256]{0,1:T(8,128)(2,1)S(1)} %convert_element_type.127, bf16[256,4096]{0,1:T(8,128)(2,1)} %bitcast.362, bf16[256,4096]{0,1:T(8,128)(2,1)S(1)} %copy-done.14, bf16[256,2048]{1,0:T(8,128)(2,1)S(1)} %copy-done.10, f32[2048]{0:T(1024)S(1)} %copy-done.22, ...), kind=kOutput, calls=%fused_computation.213 | convolution fusion | flops 8945008640 | bytes 75146240 | tf_op jit(solution)/shard_map/dot_general | solution.py:345
  1404.8 293.7 %reduce-scatter.8.cloned.1.call-done = f32[512,2048]{1,0:T(8,128)} async-done(((f32[4096,2048]{1,0:T(8,128)}), f32[512,2048]{1,0:T(8,128)}) %reduce-scatter.8.cloned.1.call-update) | async-done | bytes 4194320 | tf_op jit(solution)/shard_map/reduce_scatter | solution.py:318
  1698.5 665.4 %reduce-scatter.6.cloned.1.call-done = f32[256,8512]{0,1:T(8,128)} async-done(((f32[2048,8512]{0,1:T(8,128)}), f32[256,8512]{0,1:T(8,128)}) %reduce-scatter.6.cloned.1.call-update) | async-done | bytes 8716304 | tf_op jit(solution)/shard_map/reduce_scatter | solution.py:344
  2377.4 18.4 fusion.107
  2395.9 26.4 %all-reduce.15 = (f32[2048]{0:T(1024)S(1)}, f32[4352]{0:T(1024)S(1)}, f32[64]{0:T(128)S(1)}, f32[64]{0:T(128)S(1)}, f32[64]{0:T(128)S(1)}, /*index=5*/f32[4096]{0:T(1024)S(1)}) all-reduce(f32[2048]{0:T(1024)S(1)} %get-tuple-element.907, f32[4352]{0:T(1024)S(1)} %constant_dynamic-update-slice_fusion, ...), channel_id=1, replica_groups=mesh['dp'=4,'mp'=8] {'mp'}, use_global_device_ids=true, to_apply=%region_41.42 | all-reduce | flops 10688 | bytes 85504 | tf_op jit(solution)/shard_map/psum | solution.py:362
  2422.2 18.9 all-reduce.16
  2444.7 171.6 %all-reduce.23.cloned.1.call-done = (f32[256,8512]{0,1:T(8,128)}, f32[4,4352]{1,0:T(4,128)}, f32[512,2048]{1,0:T(8,128)}) async-done(((f32[256,8512]{0,1:T(8,128)}, f32[4,4352]{1,0:T(4,128)}, f32[512,2048]{1,0:T(8,128)}), (f32[256,8512]{0,1:T(8,128)}, f32[4,4352]{1,0:T(4,128)}, f32[512,2048]{1,0:T(8,128)})) %all-reduce.23.cloned.1.call-update) | async-done | bytes 12980240 | tf_op jit(solution)/shard_map/psum | solution.py:374
  (724 shorter events, 695.1 us)
Async XLA Ops:
  7.2 308.9 %copy-start.21 = (f32[2048]{0:T(1024)S(1)}, f32[2048]{0:T(1024)}, u32[]{:S(2)}) copy-start(f32[2048]{0:T(1024)} %param.29) | copy-start | bytes 24580
  7.2 308.9 %all-gather.3.cloned.1.call-start = ((), (), s32[]{:S(2)}) async-start(), calls=%async_computation.10 | async-start | bytes 39223296 | tf_op jit(solution)/shard_map/all_gather | solution.py:290
  7.9 821.3 %all-gather.5.cloned.1.call-start = ((), (), s32[]{:S(2)}) async-start(), calls=%async_computation.11 | async-start | bytes 18874368 | tf_op jit(solution)/shard_map/all_gather | solution.py:291
  9.0 324.9 %copy-start.25 = (f32[256]{0:T(256)}, f32[256]{0:T(256)S(1)}, u32[]{:S(2)}) copy-start(f32[256]{0:T(256)S(1)} %add_rsqrt_fusion.1) | copy-start | bytes 3076
  337.1 56.1 %all-to-all-start.1 = ((bf16[256,8,256]{0,2,1:T(8,128)(2,1)}), bf16[256,8,256]{0,2,1:T(8,128)(2,1)S(1)}, u32[]{:S(2)}, u32[]{:S(2)}) async-start(bf16[256,8,256]{0,2,1:T(8,128)(2,1)} %broadcast_in_dim.199), calls=%async_computation.1 | async-start | bytes 2097152 | tf_op jit(solution)/shard_map/all_to_all | solution.py:144
  341.8 55.7 %copy-start.28 = (f32[64]{0:T(128)S(1)}, f32[64]{0:T(128)}, u32[]{:S(2)}) copy-start(f32[64]{0:T(128)} %param.33) | copy-start | bytes 772
  341.8 55.8 %copy-start.29 = (f32[64]{0:T(128)S(1)}, f32[64]{0:T(128)}, u32[]{:S(2)}) copy-start(f32[64]{0:T(128)} %param.34) | copy-start | bytes 772
  341.8 55.8 %copy-start.30 = (f32[64]{0:T(128)S(1)}, f32[64]{0:T(128)}, u32[]{:S(2)}) copy-start(f32[64]{0:T(128)} %param.35) | copy-start | bytes 772
  341.8 57.2 %copy-start.27 = (f32[4352]{0:T(1024)S(1)}, f32[4352]{0:T(1024)}, u32[]{:S(2)}) copy-start(f32[4352]{0:T(1024)} %param.32) | copy-start | bytes 52228
  341.8 57.2 %copy-start.24 = (f32[4,4352]{1,0:T(4,128)S(1)}, f32[4,4352]{1,0:T(4,128)}, u32[]{:S(2)}) copy-start(f32[4,4352]{1,0:T(4,128)} %param.31) | copy-start | bytes 208900
  341.8 57.2 %slice-start.3 = ((f32[4,4352]{1,0:T(4,128)}), f32[4,256]{1,0:T(4,128)S(1)}, s32[]{:S(2)}) async-start(f32[4,4352]{1,0:T(4,128)} %param.31), calls=%async_computation.20 | async-start | bytes 8192 | tf_op jit(solution)/shard_map/slice | solution.py:95
  341.8 163.8 %slice-start.4 = ((f32[4352]{0:T(1024)}), f32[256]{0:T(256)S(1)}, s32[]{:S(2)}) async-start(f32[4352]{0:T(1024)} %param.32), calls=%async_computation.21 | async-start | bytes 2048 | tf_op jit(solution)/shard_map/slice | solution.py:102
  393.2 109.1 %all-to-all-start = ((bf16[256,64,64]{0,2,1:T(8,128)(2,1)}), bf16[256,64,64]{0,2,1:T(8,128)(2,1)S(1)}, u32[]{:S(2)}, u32[]{:S(2)}) async-start(bf16[256,64,64]{0,2,1:T(8,128)(2,1)} %bitcast.367), calls=%async_computation | async-start | bytes 4194304 | tf_op jit(solution)/shard_map/all_to_all | solution.py:142
  502.3 9.9 all-to-all-start.2
  752.3 53.4 %all-to-all-start.3 = ((bf16[8,2,65536]{2,1,0:T(2,128)(2,1)}), bf16[8,2,65536]{2,1,0:T(2,128)(2,1)}, u32[]{:S(2)}, u32[]{:S(2)}) async-start(bf16[8,2,65536]{2,1,0:T(2,128)(2,1)} %reshape.499), calls=%async_computation.3 | async-start | bytes 4194304 | tf_op jit(solution)/shard_map/all_to_all | solution.py:177
  848.9 53.4 %all-to-all-start.4 = ((bf16[256,64,64]{0,2,1:T(8,128)(2,1)}), bf16[256,64,64]{0,2,1:T(8,128)(2,1)}, u32[]{:S(2)}, u32[]{:S(2)}) async-start(bf16[256,64,64]{0,2,1:T(8,128)(2,1)} %bitcast.364), calls=%async_computation.4 | async-start | bytes 4194304 | tf_op jit(solution)/shard_map/all_to_all | solution.py:187
  853.2 519.8 %reduce-scatter.4.cloned.1.call-start = ((), (), s32[]{:S(2)}) async-start(), calls=%async_computation.12 | async-start | bytes 2359296 | tf_op jit(solution)/shard_map/reduce_scatter | solution.py:233
  910.1 14.1 copy-start.3
  1276.1 128.7 %all-reduce.21.cloned.1.call-start = ((), (), s32[]{:S(2)}) async-start(), calls=%async_computation.14 | async-start | bytes 139264 | tf_op jit(solution)/shard_map/psum | solution.py:362
  1276.9 421.7 %reduce-scatter.8.cloned.1.call-start = ((), (), s32[]{:S(2)}) async-start(), calls=%async_computation.15 | async-start | bytes 37748736 | tf_op jit(solution)/shard_map/reduce_scatter | solution.py:318
  1359.4 14.6 all-to-all-start.6
  1362.8 1001.1 %reduce-scatter.6.cloned.1.call-start = ((), (), s32[]{:S(2)}) async-start(), calls=%async_computation.13 | async-start | bytes 78446592 | tf_op jit(solution)/shard_map/reduce_scatter | solution.py:344
  1404.5 1211.8 %all-reduce.23.cloned.1.call-start = ((), (), s32[]{:S(2)}) async-start(), calls=%async_computation.16 | async-start | bytes 25960448 | tf_op jit(solution)/shard_map/psum | solution.py:374
  2377.4 18.4 copy-start.23
  (25 other events, 138.8 us)
Sparse Core Ops, SparseCore 0:
  9.6 306.3 all-gather.2
  317.7 218.1 all-gather.4
  1276.2 34.5 reduce-scatter.3
  1313.6 55.0 all-reduce.20
  1371.0 327.4 reduce-scatter.7
  1700.8 663.0 reduce-scatter.5
  2368.4 247.8 all-reduce.22
where the time goes:
time: 2650 us; the launch traced here: 2630 us
  waiting for transfers between devices  1690 us (64%)
  local copies, waits for them, and re-layouts  397 us (15%)
  matrix products  265 us (10%)
  other arithmetic  137 us (5%)
  blocking collectives  99.2 us (4%)
    reduce_scatter x1, waiting for transfers between devices, on_device(): lax.psum_scatter(lax.dot_general(row_block, d_proj, (((0,), (0,)), ((), (...  665 us
    all_gather x1, waiting for transfers between devices, on_device(): lax.all_gather(in_weight, 'mp', axis=0, tiled=True)  307 us
    reduce_scatter x1, waiting for transfers between devices, on_device(): lax.psum_scatter(lax.dot_general(row_block, cotangent, (((0,), (0,)), (()...  294 us
    dynamic_update_slice x32, local copies, waits for them, and re-layouts, run_stretches(): lax.scan(jax.checkpoint(stretch_step), carry_state, block_parts)  212 us
    psum x1, waiting for transfers between devices, on_device(): lax.psum((in_weight_grad, out_weight_grad, partial_sums[0], partial_sums[...  172 us
    all_to_all x1, waiting for transfers between devices, heads_forward(): lax.all_to_all(per_token, 'mp', split_axis=1, concat_axis=0, tiled=True)  102 us
    dot_general x24, matrix products, stretch_step(): within = jnp.einsum('lsh,shp->lhp', mixing, scaled, precision=HIGH)  56.8 us
    all_to_all x1, blocking collectives, heads_backward(): lax.all_to_all(send_values, 'mp', split_axis=0, concat_axis=1, tiled=True)  54 us
  transfers between devices with their start and end apart: 13, of which 9 were waited for; matrix products, arithmetic and copies ran while one was open for 15% of the time, Pallas kernels for 0%

commit v1 on v0

v1 whole, which is shorter than its diff:
```python
import jax
import jax.numpy as jnp
from jax import lax
from jax.experimental import pallas as pl
from jax.experimental.pallas import tpu as pltpu
from jax.sharding import PartitionSpec as P

SEQ = 2048
BLOCK = 256
EPS = 1e-05
LANES = 128
VMEM = 56 * 2**20

F32 = jnp.float32
BF16 = jnp.bfloat16
NN = (((1,), (0,)), ((), ()))
NT = (((1,), (1,)), ((), ()))
TN = (((0,), (0,)), ((), ()))


def mm(left, right, dims=NN):
    return lax.dot_general(left, right, dims, preferred_element_type=F32)


def halves(value):
    high = value.astype(BF16)
    return high, (value - high.astype(F32)).astype(BF16)


def mm3(left, right, dims=NN):
    return mm(left[0], right[0], dims) + (mm(left[0], right[1], dims) + mm(left[1], right[0], dims))


def mm_exact(ones, value, dims=NN):
    first, rest = value.astype(BF16), None
    rest = value - first.astype(F32)
    second = rest.astype(BF16)
    third = (rest - second.astype(F32)).astype(BF16)
    return mm(ones, first, dims) + (mm(ones, second, dims) + mm(ones, third, dims))


def spread(per_head, width):
    rows = per_head.shape[0]
    low_half = lax.broadcasted_iota(jnp.int32, (rows, LANES), 1) < LANES // 2
    parts = []
    for pair in range(width // LANES):
        parts.append(
            jnp.where(
                low_half, per_head[:, 2 * pair : 2 * pair + 1], per_head[:, 2 * pair + 1 : 2 * pair + 2]
            )
        )
    return parts[0] if len(parts) == 1 else jnp.concatenate(parts, axis=1)


def head_ones(width):
    chan = lax.broadcasted_iota(jnp.int32, (width, LANES), 0)
    head = lax.broadcasted_iota(jnp.int32, (width, LANES), 1)
    return (chan // (LANES // 2) == head).astype(BF16)


def head_sum(per_chan, ones):
    high, low = halves(per_chan)
    return mm(high, ones) + mm(low, ones)


def conv_block(ext_ref, taps_ref, width):
    span = 4
    pre = taps_ref[span : span + 1, :] + ext_ref[5 : 5 + BLOCK, :] * taps_ref[0:1, :]
    for tap in range(1, span):
        pre = pre + ext_ref[5 + tap : 5 + tap + BLOCK, :] * taps_ref[tap : tap + 1, :]
    return pre


def step_rates(step_raw, heads_ref):
    biased = step_raw + heads_ref[0:1, :]
    step_size = jnp.maximum(biased, 0.0) + jnp.log1p(jnp.exp(-jnp.abs(biased)))
    decay = heads_ref[1:2, :] * step_size
    return biased, step_size, decay


def triangle(keep):
    row = lax.broadcasted_iota(jnp.int32, (BLOCK, BLOCK), 0)
    col = lax.broadcasted_iota(jnp.int32, (BLOCK, BLOCK), 1)
    return keep(row, col)


def forward_kernel(
    mask_ref, hidden_ref, weight_ref, taps_ref, heads_ref, skip_ref,
    proj_ref, y_ref, state_ref, square_ref,
    ext, state, *, state_dim, width,
):
    joint = 2 * state_dim + width

    @pl.when(pl.program_id(1) == 0)
    def _():
        ext[0:8, :] = jnp.zeros((8, joint), F32)
        state[...] = jnp.zeros_like(state)

    projected = mm(hidden_ref[...], weight_ref[...]).astype(BF16)
    proj_ref[...] = projected
    ext[8 : 8 + BLOCK, :] = projected[:, :joint].astype(F32)
    pre = conv_block(ext, taps_ref, joint)
    ext[0:8, :] = ext[BLOCK : BLOCK + 8, :]
    conv_out = pre * jax.nn.sigmoid(pre)
    values = conv_out[:, 2 * state_dim :] * mask_ref[0]
    b_coef = halves(conv_out[:, :state_dim])
    c_coef = halves(conv_out[:, state_dim : 2 * state_dim])
    _, step_size, decay = step_rates(projected[:, joint + width :].astype(F32), heads_ref)
    causal = triangle(lambda row, col: row >= col)
    cumulative = mm_exact(causal.astype(BF16), decay)
    across = cumulative.T
    last = cumulative[BLOCK - 1 : BLOCK, :]
    scaled = values * spread(step_size, width)
    scaled_parts = halves(scaled)
    scores = mm3(c_coef, b_coef, NT)
    low_half = lax.broadcasted_iota(jnp.int32, (BLOCK, LANES), 1) < LANES // 2
    old = state[...]
    state_ref[0] = old
    mixed = spread(jnp.exp(cumulative), width) * mm3(c_coef, halves(old))
    within = []
    for pair in range(width // LANES):
        lanes = slice(pair * LANES, (pair + 1) * LANES)
        rhs = (scaled_parts[0][:, lanes], scaled_parts[1][:, lanes])
        sides = []
        for head in (2 * pair, 2 * pair + 1):
            gap = jnp.where(causal, cumulative[:, head : head + 1] - across[head : head + 1, :], -1e30)
            sides.append(mm3(halves(scores * jnp.exp(gap)), rhs))
        within.append(jnp.where(low_half, sides[0], sides[1]))
    mixed = mixed + (within[0] if len(within) == 1 else jnp.concatenate(within, axis=1))
    tail = halves(scaled * spread(jnp.exp(last - cumulative), width))
    state[...] = old * spread(jnp.exp(last), width) + mm3(b_coef, tail, TN)
    y_low = (mixed + skip_ref[0:1, :] * values).astype(BF16)
    y_ref[...] = y_low
    gate = projected[:, joint : joint + width].astype(F32)
    gated = y_low.astype(F32) * (gate * jax.nn.sigmoid(gate))
    square = halves(gated * gated * mask_ref[0])
    ones = jnp.ones((8, width), BF16)
    square_ref[0] = mm(ones, square[0], NT) + mm(ones, square[1], NT)


def backward_kernel(
    mask_ref, joint_ref, before_ref, raw_ref, dy_ref, dgate_ref, state_ref, taps_ref, heads_ref, skip_ref,
    dproj_ref, conv_grad_ref, head_grad_ref,
    ext, dext, dstate, rows, *, state_dim, width, blocks,
):
    joint = 2 * state_dim + width
    place = blocks - 1 - pl.program_id(1)

    @pl.when((pl.program_id(0) == 0) & (pl.program_id(1) == 0))
    def _():
        conv_grad_ref[...] = jnp.zeros_like(conv_grad_ref)
        head_grad_ref[...] = jnp.zeros_like(head_grad_ref)
        rows[...] = jnp.zeros_like(rows)

    @pl.when(pl.program_id(1) == 0)
    def _():
        dext[0:8, :] = jnp.zeros((8, joint), F32)
        dstate[...] = jnp.zeros_like(dstate)

    before = before_ref[...].astype(F32)[8:16, :]
    ext[0:8, :] = jnp.where(place > 0, before, 0.0)
    ext[8 : 8 + BLOCK, :] = joint_ref[...].astype(F32)
    pre = conv_block(ext, taps_ref, joint)
    sig = jax.nn.sigmoid(pre)
    conv_out = pre * sig
    mask = mask_ref[0]
    values = conv_out[:, 2 * state_dim :] * mask
    b_coef = halves(conv_out[:, :state_dim])
    c_coef = halves(conv_out[:, state_dim : 2 * state_dim])
    biased, step_size, decay = step_rates(raw_ref[...].astype(F32), heads_ref)
    later = triangle(lambda row, col: col >= row)
    cumulative = mm_exact(triangle(lambda row, col: row >= col).astype(BF16), decay)
    across = cumulative.T
    last = cumulative[BLOCK - 1 : BLOCK, :]
    step_chan = spread(step_size, width)
    scaled = values * step_chan
    scaled_parts = halves(scaled)
    dy_low = dy_ref[...]
    dy = dy_low.astype(F32)
    scores = mm3(b_coef, c_coef, NT)
    low_half = lax.broadcasted_iota(jnp.int32, (BLOCK, LANES), 1) < LANES // 2
    lane = lax.broadcasted_iota(jnp.int32, (BLOCK, LANES), 1)
    d_scores = jnp.zeros((BLOCK, BLOCK), F32)
    from_rows = jnp.zeros((BLOCK, LANES), F32)
    d_within = []
    for pair in range(width // LANES):
        lanes = slice(pair * LANES, (pair + 1) * LANES)
        dy_pair = dy_low[:, lanes]
        dy_twice = jnp.concatenate([dy_pair, dy_pair], axis=1)
        sides = []
        for side in range(2):
            head = 2 * pair + side
            own = low_half if side == 0 else jnp.logical_not(low_half)
            left = jnp.concatenate(
                [jnp.where(own, part[:, lanes], jnp.zeros((), BF16)) for part in scaled_parts], axis=1
            )
            d_mixing = mm(left, dy_twice, NT)
            gap = jnp.where(later, across[head : head + 1, :] - cumulative[:, head : head + 1], -1e30)
            weight = jnp.exp(gap)
            mixing = scores * weight
            d_scores = d_scores + d_mixing * weight
            product = d_mixing * mixing
            rows[head : head + 1, :] = jnp.sum(product, axis=0, keepdims=True)
            from_rows = jnp.where(lane == head, jnp.sum(product, axis=1, keepdims=True), from_rows)
            parts = halves(mixing)
            sides.append(mm(parts[0], dy_pair) + mm(parts[1], dy_pair))
        d_within.append(jnp.where(low_half, sides[0], sides[1]))
    ones = head_ones(width)
    old = state_ref[0]
    old_parts = halves(old)
    grown = dstate[...]
    grown_parts = halves(grown)
    ey = spread(jnp.exp(cumulative), width) * dy
    ey_parts = halves(ey)
    tail_chan = spread(jnp.exp(last - cumulative), width)
    tail = scaled * tail_chan
    tail_parts = halves(tail)
    last_chan = spread(jnp.exp(last), width)
    into_state = mm3(b_coef, grown_parts)
    d_scaled = (d_within[0] if len(d_within) == 1 else jnp.concatenate(d_within, axis=1)) + tail_chan * into_state
    d_parts = halves(d_scores)
    d_c = mm3(d_parts, b_coef, TN) + mm3(ey_parts, old_parts, NT)
    d_b = mm3(d_parts, c_coef) + mm3(tail_parts, grown_parts, NT)
    end_terms = head_sum(ey * mm3(c_coef, old_parts), ones)
    start_terms = head_sum(tail * into_state, ones)
    kept = jnp.sum(last_chan * grown * old, axis=0, keepdims=True)
    skip_part = jnp.sum(dy * values, axis=0, keepdims=True)
    kept_heads = mm_exact_left(jnp.concatenate([kept, skip_part, jnp.zeros((6, width), F32)], axis=0), ones)
    dstate[...] = last_chan * grown + mm3(c_coef, ey_parts, TN)
    gaps = rows[...].T - from_rows + end_terms
    d_decay = (
        mm_exact(later.astype(BF16), gaps)
        + mm_exact(triangle(lambda row, col: col < row).astype(BF16), start_terms)
        + kept_heads[0:1, :]
    )
    d_step = head_sum(d_scaled * values, ones) + d_decay * heads_ref[1:2, :]
    d_raw = d_step * jax.nn.sigmoid(biased)
    head_grad_ref[0:1, :] += jnp.sum(d_raw, axis=0, keepdims=True)
    head_grad_ref[1:2, :] += jnp.sum(d_decay * decay, axis=0, keepdims=True)
    head_grad_ref[2:3, :] += kept_heads[1:2, :]
    d_values = (d_scaled * step_chan + skip_ref[0:1, :] * dy) * mask
    d_conv = jnp.concatenate([d_b, d_c, d_values], axis=1)
    d_pre = d_conv * (sig * (1.0 + pre * (1.0 - sig)))
    for tap in range(4):
        conv_grad_ref[tap : tap + 1, :] += jnp.sum(d_pre * ext[5 + tap : 5 + tap + BLOCK, :], axis=0, keepdims=True)
    conv_grad_ref[4:5, :] += jnp.sum(d_pre, axis=0, keepdims=True)
    dext[BLOCK : BLOCK + 8, :] = dext[0:8, :]
    dext[0:BLOCK, :] = d_pre
    d_in = dext[3 : 3 + BLOCK, :] * taps_ref[0:1, :]
    for tap in range(1, 4):
        d_in = d_in + dext[3 - tap : 3 - tap + BLOCK, :] * taps_ref[tap : tap + 1, :]
    dproj_ref[:, :joint] = d_in.astype(BF16)
    dproj_ref[:, joint : joint + width] = dgate_ref[...]
    dproj_ref[:, joint + width :] = d_raw.astype(BF16)


def mm_exact_left(value, ones):
    first = value.astype(BF16)
    rest = value - first.astype(F32)
    second = rest.astype(BF16)
    third = (rest - second.astype(F32)).astype(BF16)
    return mm(first, ones) + (mm(second, ones) + mm(third, ones))


def mixer_forward(mask, hidden, weight, taps, heads, skip, state_dim, width):
    seqs = mask.shape[0]
    tokens, depth = hidden.shape
    blocks = tokens // seqs // BLOCK
    columns = weight.shape[1]
    joint = 2 * state_dim + width
    row = lambda s, c: (s * blocks + c, 0)
    whole = lambda s, c: (0, 0)
    return pl.pallas_call(
        lambda *refs: forward_kernel(*refs, state_dim=state_dim, width=width),
        grid=(seqs, blocks),
        in_specs=[
            pl.BlockSpec((1, 1, width), lambda s, c: (s, 0, 0)),
            pl.BlockSpec((BLOCK, depth), row),
            pl.BlockSpec((depth, columns), whole),
            pl.BlockSpec((8, joint), whole),
            pl.BlockSpec((8, LANES), whole),
            pl.BlockSpec((8, width), whole),
        ],
        out_specs=[
            pl.BlockSpec((BLOCK, columns), row),
            pl.BlockSpec((BLOCK, width), row),
            pl.BlockSpec((1, state_dim, width), lambda s, c: (s * blocks + c, 0, 0)),
            pl.BlockSpec((1, 8, BLOCK), lambda s, c: (s * blocks + c, 0, 0)),
        ],
        out_shape=[
            jax.ShapeDtypeStruct((tokens, columns), BF16),
            jax.ShapeDtypeStruct((tokens, width), BF16),
            jax.ShapeDtypeStruct((seqs * blocks, state_dim, width), F32),
            jax.ShapeDtypeStruct((seqs * blocks, 8, BLOCK), F32),
        ],
        scratch_shapes=[
            pltpu.VMEM((BLOCK + 8, joint), F32),
            pltpu.VMEM((state_dim, width), F32),
        ],
        compiler_params=pltpu.CompilerParams(
            dimension_semantics=("arbitrary", "arbitrary"), vmem_limit_bytes=VMEM
        ),
        name="mixer_forward",
    )(mask, hidden, weight, taps, heads, skip)


def mixer_backward(mask, projected, d_y, d_gate, states, taps, heads, skip, state_dim, width):
    seqs = mask.shape[0]
    tokens, columns = projected.shape
    blocks = tokens // seqs // BLOCK
    joint = 2 * state_dim + width
    place = lambda s, c: s * blocks + blocks - 1 - c
    row = lambda s, c: (place(s, c), 0)
    whole = lambda s, c: (0, 0)
    return pl.pallas_call(
        lambda *refs: backward_kernel(*refs, state_dim=state_dim, width=width, blocks=blocks),
        grid=(seqs, blocks),
        in_specs=[
            pl.BlockSpec((1, 1, width), lambda s, c: (s, 0, 0)),
            pl.BlockSpec((BLOCK, joint), row),
            pl.BlockSpec((16, joint), lambda s, c: (jnp.maximum(place(s, c) * (BLOCK // 16) - 1, 0), 0)),
            pl.BlockSpec((BLOCK, LANES), lambda s, c: (place(s, c), (joint + width) // LANES)),
            pl.BlockSpec((BLOCK, width), row),
            pl.BlockSpec((BLOCK, width), row),
            pl.BlockSpec((1, state_dim, width), lambda s, c: (place(s, c), 0, 0)),
            pl.BlockSpec((8, joint), whole),
            pl.BlockSpec((8, LANES), whole),
            pl.BlockSpec((8, width), whole),
        ],
        out_specs=[
            pl.BlockSpec((BLOCK, columns), row),
            pl.BlockSpec((8, joint), whole),
            pl.BlockSpec((8, LANES), whole),
        ],
        out_shape=[
            jax.ShapeDtypeStruct((tokens, columns), BF16),
            jax.ShapeDtypeStruct((8, joint), F32),
            jax.ShapeDtypeStruct((8, LANES), F32),
        ],
        scratch_shapes=[
            pltpu.VMEM((BLOCK + 8, joint), F32),
            pltpu.VMEM((BLOCK + 8, joint), F32),
            pltpu.VMEM((state_dim, width), F32),
            pltpu.VMEM((LANES, BLOCK), F32),
        ],
        compiler_params=pltpu.CompilerParams(
            dimension_semantics=("arbitrary", "arbitrary"), vmem_limit_bytes=VMEM
        ),
        name="mixer_backward",
    )(mask, projected, projected, projected, d_y, d_gate, states, taps, heads, skip)


def pad_last(array, size):
    extra = size - array.shape[-1]
    if extra == 0:
        return array
    return jnp.pad(array, [(0, 0)] * (array.ndim - 1) + [(0, extra)])


def pad_rows(array, size):
    return jnp.pad(array, [(0, size - array.shape[0]), (0, 0)])


def on_device(
    inputs, cotangent, widths, norm_gain, in_weight, conv_weight, conv_bias, step_bias, rate_log,
    skip_gain, out_gain, out_weight,
):
    mp, dp = lax.axis_size("mp"), lax.axis_size("dp")
    mp_place, dp_place = lax.axis_index("mp"), lax.axis_index("dp")
    heads, inner, channels = step_bias.shape[0], out_gain.shape[0], conv_bias.shape[0]
    head_dim, state_dim = inner // heads, (channels - inner) // 2
    own_heads = heads // mp
    own = own_heads * head_dim
    width = -(-own // LANES) * LANES
    joint = 2 * state_dim + width
    columns = joint + width + LANES
    tokens, depth = inputs.shape
    rows = depth // mp
    part = rows // dp
    seqs = widths.shape[0]
    all_tokens = tokens * mp

    slab = lax.dynamic_slice_in_dim(in_weight, dp_place * part, part, 0)
    by_place = lambda piece, size: pad_last(
        piece.reshape(part, mp, piece.shape[1] // mp).transpose(1, 0, 2), size
    )
    send = jnp.concatenate(
        [
            jnp.broadcast_to(slab[None, :, 2 * inner : 2 * inner + 2 * state_dim], (mp, part, 2 * state_dim)),
            by_place(slab[:, inner : 2 * inner], width),
            by_place(slab[:, :inner], width),
            by_place(slab[:, inner + channels :], LANES),
        ],
        axis=2,
    )
    got = lax.all_to_all(send, "mp", split_axis=0, concat_axis=0, tiled=True)
    weight = lax.all_gather(got.reshape(mp * part, columns), "dp", axis=0, tiled=True)

    reorder = lambda array: array.reshape(-1, mp, dp, part).transpose(0, 2, 1, 3).reshape(-1, depth)
    restore = lambda array: array.reshape(-1, dp, mp, part).transpose(0, 2, 1, 3).reshape(-1, depth)
    inputs_f = inputs.astype(F32)
    rms_scale = lax.rsqrt(jnp.mean(inputs_f * inputs_f, axis=-1, keepdims=True) + EPS)
    normed = inputs_f * rms_scale
    hidden_own = reorder((normed * norm_gain[None, :]).astype(BF16))
    hidden = lax.all_gather(hidden_own, "mp", axis=0, tiled=True)
    cot_all = lax.all_gather(cotangent, "mp", axis=0, tiled=True)

    first_chan, first_head = mp_place * own, mp_place * own_heads
    cut = lambda array, first, size: lax.dynamic_slice_in_dim(array, first, size, array.ndim - 1)
    taps_all = jnp.concatenate([conv_weight, conv_bias[None, :]], axis=0)
    taps = pad_rows(
        jnp.concatenate([taps_all[:, inner:], pad_last(cut(taps_all, first_chan, own), width)], axis=1), 8
    )
    head_rows = jnp.stack([step_bias, -jnp.exp(rate_log)])
    head_params = pad_rows(pad_last(cut(head_rows, first_head, own_heads), LANES), 8)
    skip = jnp.repeat(cut(skip_gain, first_head, own_heads), head_dim)[None, :]
    skip = pad_rows(pad_last(skip, width), 8)
    active_heads = heads // 8 * jnp.left_shift(jnp.int32(1), widths)
    head_mask = (first_head + jnp.arange(own_heads, dtype=jnp.int32))[None, :] < active_heads[:, None]
    chan_mask = jnp.repeat(head_mask.astype(F32), head_dim, axis=1)
    mask = pad_last(chan_mask, width)[:, None, :]
    per_token = lambda array: jnp.repeat(array, all_tokens // seqs, axis=0)
    mask_tok = chan_mask if seqs == 1 else per_token(chan_mask)
    active_count = (active_heads * head_dim).astype(F32)[:, None]
    if seqs > 1:
        active_count = per_token(active_count)

    projected, y_all, states, squares = mixer_forward(
        mask, hidden, weight, taps, head_params, skip, state_dim, width
    )
    total_square = lax.psum(squares[:, 0, :].reshape(all_tokens), "mp")[:, None]
    gate = projected[:, joint : joint + own].astype(F32)
    y_f = y_all[:, :own].astype(F32)
    gate_sig = jax.nn.sigmoid(gate)
    silu_z = gate * gate_sig
    gated = y_f * silu_z
    gain = cut(out_gain, first_chan, own)[None, :]
    out_root = lax.rsqrt(total_square / active_count + EPS)
    normed_out = (gated * out_root * gain * mask_tok).astype(BF16)
    share = jnp.dot(normed_out, out_weight, preferred_element_type=F32).astype(BF16)
    summed = lax.psum_scatter(share, "mp", scatter_dimension=0, tiled=True)
    outputs = (inputs_f + summed.astype(F32)).astype(BF16)

    d_normed = mm(cot_all, out_weight, NT)
    upstream = d_normed * gain * mask_tok
    inner_dot = lax.psum(jnp.sum(upstream * gated, axis=-1), "mp")[:, None]
    out_weight_grad = lax.psum(mm(normed_out, cot_all, TN), "dp")
    out_gain_grad = jnp.sum(d_normed * gated * out_root * mask_tok, axis=0)
    d_gated = out_root * upstream - out_root * out_root * out_root * mask_tok * gated * inner_dot / active_count
    d_y = pad_last((d_gated * silu_z).astype(BF16), width)
    d_gate = pad_last((d_gated * y_f * gate_sig * (1.0 + gate * (1.0 - gate_sig))).astype(BF16), width)
    d_proj, conv_grads, head_grads = mixer_backward(
        mask, projected, d_y, d_gate, states, taps, head_params, skip, state_dim, width
    )

    d_share = mm(d_proj, weight, NT).astype(BF16)
    d_hidden = lax.psum_scatter(d_share, "mp", scatter_dimension=0, tiled=True)
    d_hidden = restore(d_hidden.astype(F32))
    norm_gain_grad = jnp.sum(d_hidden * normed, axis=0)
    d_normed_in = d_hidden * norm_gain[None, :]
    input_back = rms_scale * (d_normed_in - normed * jnp.mean(d_normed_in * normed, axis=-1, keepdims=True))
    input_grad = (cotangent.astype(F32) + input_back).astype(BF16)

    weight_part = mm(hidden, d_proj, TN)
    mine = lax.psum_scatter(weight_part, "dp", scatter_dimension=0, tiled=True)
    blocks = lax.all_to_all(mine.reshape(mp, part, columns), "mp", split_axis=0, concat_axis=0, tiled=True)
    flat = lambda piece: piece.transpose(1, 0, 2).reshape(part, -1)
    grad_rows = jnp.concatenate(
        [
            flat(blocks[:, :, joint : joint + own]),
            flat(blocks[:, :, 2 * state_dim : 2 * state_dim + own]),
            jnp.sum(blocks[:, :, : 2 * state_dim], axis=0),
            flat(blocks[:, :, joint + width : joint + width + own_heads]),
        ],
        axis=1,
    )
    in_weight_grad = lax.all_gather(grad_rows, "dp", axis=0, tiled=True)

    def place_in(array, first, size):
        return lax.dynamic_update_slice_in_dim(
            jnp.zeros(array.shape[:-1] + (size,), F32), array, first, array.ndim - 1
        )

    conv_own = place_in(conv_grads[:5, 2 * state_dim : 2 * state_dim + own], first_chan, inner)
    conv_full = jnp.concatenate([conv_own, conv_grads[:5, : 2 * state_dim]], axis=1)
    head_full = place_in(head_grads[:3, :own_heads], first_head, heads)
    gain_full = place_in(out_gain_grad, first_chan, inner)
    conv_total, head_total, gain_total, norm_total = lax.psum(
        (conv_full, head_full, gain_full, norm_gain_grad), ("dp", "mp")
    )
    return (
        outputs,
        input_grad,
        norm_total,
        in_weight_grad,
        conv_total[:4],
        conv_total[4],
        head_total[0],
        head_total[1],
        head_total[2],
        gain_total,
        out_weight_grad,
    )


def solution(mesh):
    rows = P(("dp", "mp"), None)
    return jax.shard_map(
        on_device,
        mesh=mesh,
        in_specs=(rows, rows, P("dp"), P(), P("mp", None), P(), P(), P(), P(), P(), P(), P("mp", None)),
        out_specs=(rows, rows, P(), P("mp", None), P(), P(), P(), P(), P(), P(), P("mp", None)),
        check_vma=False,
    )
```

time: 2650 us -> 1050 us (0.40)
  waiting for transfers between devices: 1690 us -> 601 us
  local copies, waits for them, and re-layouts: 397 us -> 52 us
  matrix products: 265 us -> 71.2 us
  other arithmetic: 137 us -> 25.2 us
  Pallas kernels: 0 us -> 89.4 us
  blocking collectives: 99.2 us -> 183 us
    reduce_scatter x3, waiting for transfers between devices: 959 us -> 210 us  [the longest x1 91.6 us: on_device(): d_hidden = lax.psum_scatter(d_share, 'mp', scatter_dimension=0, tiled=True)]
    all_to_all x6 -> x0, waiting for transfers between devices: 251 us -> none  [the longest x1 102 us: heads_forward(): lax.all_to_all(per_token, 'mp', split_axis=1, concat_axis=0, tiled=True)]
    dynamic_update_slice x37 -> x3, local copies, waits for them, and re-layouts: 213 us -> 0.33 us  [place_in(): lax.dynamic_update_slice_in_dim(jnp.zeros(array.shape[:-1] + (size,), F32...]
    dot_general x126 -> x5, matrix products: 265 us -> 71.2 us  [the longest x4 60 us: mm(): return lax.dot_general(left, right, dims, preferred_element_type=F32)]
    pallas_call x0 -> x2, Pallas kernels: none -> 89.4 us  [the longest x1 50.6 us: mixer_backward(): pl.pallas_call(lambda *refs: backward_kernel(*refs, state_dim=state_dim,...]
    all_to_all x1 -> x2, blocking collectives: 54 us -> 114 us  [the longest x1 72.5 us: on_device(): lax.all_to_all(mine.reshape(mp, part, columns), 'mp', split_axis=0, conca...]
    all_gather x2 -> x4, waiting for transfers between devices: 307 us -> 250 us  [the longest x1 86.5 us: on_device(): in_weight_grad = lax.all_gather(grad_rows, 'dp', axis=0, tiled=True)]
    another operation x90 -> x2, other arithmetic: 36.4 us -> 0.01 us  [on_device(): head_rows = jnp.stack([step_bias, -jnp.exp(rate_log)])]
  transfers between devices with their start and end apart: 13 -> 9, of which waited for: 9 -> 9; matrix products, arithmetic and copies ran while one was open for 15% -> 9% of each run, Pallas kernels for 0% -> 4%
where the time goes in v1:
time: 1050 us; the launch traced here: 1040 us
  waiting for transfers between devices  601 us (57%)
  blocking collectives  183 us (17%)
  Pallas kernels  89.4 us (9%)
  matrix products  71.2 us (7%)
  local copies, waits for them, and re-layouts  52 us (5%)
  other arithmetic  25.2 us (2%)
  between operations  15.2 us (1%)
    psum x1, waiting for transfers between devices, on_device(): out_weight_grad = lax.psum(mm(normed_out, cot_all, TN), 'dp')  98.5 us
    reduce_scatter x1, waiting for transfers between devices, on_device(): d_hidden = lax.psum_scatter(d_share, 'mp', scatter_dimension=0, tiled=True)  91.6 us
    all_gather x1, waiting for transfers between devices, on_device(): in_weight_grad = lax.all_gather(grad_rows, 'dp', axis=0, tiled=True)  86.5 us
    all_gather x1, waiting for transfers between devices, on_device(): hidden = lax.all_gather(hidden_own, 'mp', axis=0, tiled=True)  84.3 us
    reduce_scatter x1, waiting for transfers between devices, on_device(): mine = lax.psum_scatter(weight_part, 'dp', scatter_dimension=0, tiled=True)  79.2 us
    all_to_all x1, blocking collectives, on_device(): lax.all_to_all(mine.reshape(mp, part, columns), 'mp', split_axis=0, conca...  72.5 us
    dot_general x4, matrix products, mm(): return lax.dot_general(left, right, dims, preferred_element_type=F32)  60 us
    all_gather x1, waiting for transfers between devices, on_device(): lax.all_gather(got.reshape(mp * part, columns), 'dp', axis=0, tiled=True)  50.9 us
  transfers between devices with their start and end apart: 9, of which 9 were waited for; matrix products, arithmetic and copies ran while one was open for 9% of the time, Pallas kernels for 4%

profile of v1, /device:TPU:0, one launch (start us, length us, event | category | flops | bytes accessed | tf_op | source)
XLA Modules:
  0.0 1038.0 jit_solution(16550395050283879363)
XLA Ops:
  17.5 41.3 %all_to_all.10 = bf16[8,64,1408]{2,1,0:T(8,128)(2,1)} all-to-all(bf16[8,64,1408]{2,1,0:T(8,128)(2,1)S(1)} %fusion.21), channel_id=1, replica_groups=mesh['dp'=4,'mp'=8] {'mp'}, dimensions={0} | all-to-all | bytes 2883584 | tf_op jit(solution)/shard_map/all_to_all | solution.py:396
  72.8 50.9 %all-gather.7.cloned.1.call-done.refs_2_ = bf16[2048,1408]{1,0:T(8,128)(2,1)} async-done(((bf16[512,1408]{1,0:T(8,128)(2,1)}), bf16[2048,1408]{1,0:T(8,128)(2,1)}) %all-gather.7.cloned.1.call-update) | async-done | bytes 5767184 | tf_op jit(solution)/shard_map/all_gather | solution.py:397
  123.7 84.3 %all-gather.5.cloned.1.call-done.refs_1_ = bf16[2048,2048]{1,0:T(8,128)(2,1)} async-done(((bf16[256,2048]{1,0:T(8,128)(2,1)}), bf16[2048,2048]{1,0:T(8,128)(2,1)}) %all-gather.5.cloned.1.call-update) | async-done | bytes 8388624 | tf_op jit(solution)/shard_map/all_gather | solution.py:405
  207.9 38.8 %mixer_forward.1 = (bf16[2048,1408]{1,0:T(8,128)(2,1)}, bf16[2048,512]{1,0:T(8,128)(2,1)}, f32[8,128,512]{2,1,0:T(8,128)}, f32[8,8,256]{2,1,0:T(8,128)}) custom-call(f32[1,1,512]{2,1,0:T(1,128)} %broadcast_in_dim.19.refs_0_, bf16[2048,2048]{1,0:T(8,128)(2,1)} %all-gather.5.cloned.1.call-done.refs_1_, ...), custom_call_target="tpu_custom_call" | custom-call | tf_op jit(solution)/shard_map/mixer_forward/pallas_call | solution.py:273
  247.6 15.1 %psum.49 = f32[2048]{0:T(1024)S(1)} all-reduce(f32[2048]{0:T(1024)S(1)} %bitcast.62), channel_id=1, replica_groups=mesh['dp'=4,'mp'=8] {'mp'}, use_global_device_ids=true, to_apply=%region_1.2 | all-reduce | flops 2048 | bytes 16384 | tf_op jit(solution)/shard_map/psum | solution.py:431
  262.7 28.0 %all-gather.9.cloned.1.call-done = bf16[2048,2048]{1,0:T(8,128)(2,1)} async-done(((bf16[256,2048]{1,0:T(8,128)(2,1)}), bf16[2048,2048]{1,0:T(8,128)(2,1)}) %all-gather.9.cloned.1.call-update) | async-done | bytes 8388624 | tf_op jit(solution)/shard_map/all_gather | solution.py:406
  290.8 10.6 %multiply_reduce_fusion = (f32[512]{0:T(512)S(1)}, f32[2048]{0:T(1024)S(1)}, f32[2048,512]{1,0:T(8,128)}) fusion(f32[512]{0:T(512)S(1)} %broadcast_in_dim.43, f32[2048]{0:T(1024)S(1)} %get-tuple-element.79, bf16[2048,1408]{1,0:T(8,128)(2,1)} %get-tuple-element.19.refs_1_.refs_2_.refs_3_, bf16[2048,512]{1,0:T(8,128)(2,1)} %get-tuple-element.18, ...), kind=kOutput, calls=%fused_computation.14 | convolution fusion | flops 4310693376 | bytes 18896896 | tf_op jit(solution)/shard_map/dot_general | solution.py:22
  301.4 14.4 %psum.50 = f32[2048]{0:T(1024)S(1)} all-reduce(f32[2048]{0:T(1024)S(1)} %get-tuple-element.70), channel_id=1, replica_groups=mesh['dp'=4,'mp'=8] {'mp'}, use_global_device_ids=true, to_apply=%region_4.5 | all-reduce | flops 2048 | bytes 16384 | tf_op jit(solution)/shard_map/psum | solution.py:446
  315.7 7.2 fusion.2
  327.3 50.6 %mixer_backward.1 = (bf16[2048,1408]{1,0:T(8,128)(2,1)}, f32[8,768]{1,0:T(8,128)}, f32[8,128]{1,0:T(8,128)}) custom-call(f32[1,1,512]{2,1,0:T(1,128)} %broadcast_in_dim.19.refs_0_, bf16[2048,1408]{1,0:T(8,128)(2,1)} %get-tuple-element.19.refs_1_.refs_2_.refs_3_, bf16[2048,1408]{1,0:T(8,128)(2,1)} %get-tuple-element.19.refs_1_.refs_2_.refs_3_, ...), custom_call_target="tpu_custom_call" | custom-call | tf_op jit(solution)/shard_map/mixer_backward/pallas_call | solution.py:315
  377.9 18.7 %fusion.26 = f32[2048,1408]{1,0:T(8,128)} fusion(bf16[2048,2048]{1,0:T(8,128)(2,1)} %all-gather.5.cloned.1.call-done.refs_1_, bf16[2048,1408]{1,0:T(8,128)(2,1)} %get-tuple-element.22), kind=kOutput, calls=%fused_computation.69 | convolution fusion | flops 11811160064 | bytes 25690112 | tf_op jit(solution)/shard_map/dot_general | solution.py:22
  398.3 18.5 %convolution_convert_fusion = bf16[2048,2048]{1,0:T(8,128)(2,1)} fusion(bf16[2048,1408]{1,0:T(8,128)(2,1)} %get-tuple-element.22, bf16[2048,1408]{1,0:T(8,128)(2,1)} %all-gather.7.cloned.1.call-done.refs_2_), kind=kOutput, calls=%fused_computation | convolution fusion | flops 11815354368 | bytes 19922944 | tf_op jit(solution)/shard_map/dot_general | solution.py:22
  416.9 11.2 %convolution_convert_fusion.1 = bf16[2048,2048]{1,0:T(8,128)(2,1)} fusion(bf16[512,2048]{1,0:T(8,128)(2,1)S(1)} %copy-done, f32[512]{0:T(512)S(1)} %broadcast_in_dim.43, f32[512]{0:T(512)S(1)} %dynamic_slice.19, f32[2048]{0:T(1024)S(1)} %get-tuple-element.79, bf16[2048,512]{1,0:T(8,128)(2,1)} %get-tuple-element.18, ...), kind=kOutput, calls=%fused_computation.1 | convolution fusion | flops 4310695936 | bytes 14692352 | tf_op jit(solution)/shard_map/dot_general | solution.py:440
  428.2 79.2 %reduce-scatter.8.cloned.1.call-done = f32[512,1408]{1,0:T(8,128)} async-done(((f32[2048,1408]{1,0:T(8,128)}), f32[512,1408]{1,0:T(8,128)}) %reduce-scatter.8.cloned.1.call-update) | async-done | bytes 2883600 | tf_op jit(solution)/shard_map/reduce_scatter | solution.py:465
  507.4 72.5 %all_to_all.11 = f32[8,64,1408]{2,1,0:T(8,128)S(1)} all-to-all(f32[8,64,1408]{2,1,0:T(8,128)} %bitcast.57), channel_id=1, replica_groups=mesh['dp'=4,'mp'=8] {'mp'}, dimensions={0} | all-to-all | bytes 5767168 | tf_op jit(solution)/shard_map/all_to_all | solution.py:466
  586.5 12.2 %fusion.24 = f32[512,2048]{1,0:T(8,128)} fusion(bf16[2048,2048]{1,0:T(8,128)(2,1)} %all-gather.9.cloned.1.call-done, f32[512]{0:T(512)S(1)} %broadcast_in_dim.43, f32[512]{0:T(512)S(1)} %dynamic_slice.19, f32[2048]{0:T(1024)S(1)} %get-tuple-element.79, bf16[2048,512]{1,0:T(8,128)(2,1)} %get-tuple-element.18, ...), kind=kOutput, calls=%fused_computation.67 | convolution fusion | flops 4306501632 | bytes 16789504 | tf_op jit(solution)/shard_map/dot_general | solution.py:22
  599.8 41.7 %all-reduce.9.cloned.1.call-done = f32[5,4352]{1,0:T(8,128)} async-done(((f32[5,4352]{1,0:T(8,128)}), f32[5,4352]{1,0:T(8,128)}) %all-reduce.9.cloned.1.call-update) | async-done | bytes 87056 | tf_op jit(solution)/shard_map/psum | solution.py:488
  644.6 91.6 %reduce-scatter.6.cloned.1.call-done = bf16[256,2048]{1,0:T(8,128)(2,1)} async-done(((bf16[2048,2048]{1,0:T(8,128)(2,1)}), bf16[256,2048]{1,0:T(8,128)(2,1)}) %reduce-scatter.6.cloned.1.call-update) | async-done | bytes 1048592 | tf_op jit(solution)/shard_map/reduce_scatter | solution.py:457
  747.6 40.0 %all-reduce.5 = (f32[2048]{0:T(1024)}, f32[3,64]{1,0:T(4,128)S(1)}, f32[4096]{0:T(1024)}) all-reduce(f32[2048]{0:T(1024)S(1)} %get-tuple-element.71, f32[3,64]{1,0:T(4,128)S(1)} %dynamic_update_slice.10, f32[4096]{0:T(1024)S(1)} %dynamic_update_slice.11), channel_id=1, replica_groups=mesh['dp'=4,'mp'=8] {'dp','mp'}, use_global_device_ids=true, to_apply=%region_8.9 | all-reduce | flops 6336 | bytes 50688 | tf_op jit(solution)/shard_map/psum | solution.py:488
  788.1 39.4 %reduce-scatter.4.cloned.1.call-done = bf16[256,2048]{1,0:T(8,128)(2,1)} async-done(((bf16[2048,2048]{1,0:T(8,128)(2,1)}), bf16[256,2048]{1,0:T(8,128)(2,1)}) %reduce-scatter.4.cloned.1.call-update) | async-done | bytes 1048592 | tf_op jit(solution)/shard_map/reduce_scatter | solution.py:441
  832.1 86.5 %all-gather.11.cloned.1.call-done = f32[256,8512]{1,0:T(8,128)} async-done(((f32[64,8512]{1,0:T(8,128)}), f32[256,8512]{1,0:T(8,128)}) %all-gather.11.cloned.1.call-update) | async-done | bytes 8716304 | tf_op jit(solution)/shard_map/all_gather | solution.py:477
  918.6 9.2 copy.107
  927.8 98.5 %all-reduce.11.cloned.1.call-done = f32[512,2048]{1,0:T(8,128)} async-done(((f32[512,2048]{1,0:T(8,128)}), f32[512,2048]{1,0:T(8,128)}) %all-reduce.11.cloned.1.call-update) | async-done | bytes 4194320 | tf_op jit(solution)/shard_map/psum | solution.py:447
  1026.4 4.7 copy.117
  (101 shorter events, 57.7 us)
Async XLA Ops:
  7.2 283.6 %copy-start = (bf16[512,2048]{1,0:T(8,128)(2,1)S(1)}, bf16[512,2048]{1,0:T(8,128)(2,1)}, u32[]{:S(2)}) copy-start(bf16[512,2048]{1,0:T(8,128)(2,1)} %param.23) | copy-start | bytes 6291460
  7.2 116.5 %all-gather.7.cloned.1.call-start = ((), (), s32[]{:S(2)}) async-start(), calls=%async_computation.6 | async-start | bytes 7208960 | tf_op jit(solution)/shard_map/all_gather | solution.py:397
  13.7 45.1 %copy-start.1 = (bf16[256,2048]{1,0:T(8,128)(2,1)S(1)}, bf16[256,2048]{1,0:T(8,128)(2,1)}, u32[]{:S(2)}) copy-start(bf16[256,2048]{1,0:T(8,128)(2,1)} %param.12) | copy-start | bytes 3145732
  16.2 43.0 %copy-start.4 = (f32[2048]{0:T(1024)S(1)}, f32[2048]{0:T(1024)}, u32[]{:S(2)}) copy-start(f32[2048]{0:T(1024)} %param.15) | copy-start | bytes 24580
  58.8 149.2 %all-gather.5.cloned.1.call-start = ((), (), s32[]{:S(2)}) async-start(), calls=%async_computation.5 | async-start | bytes 9437184 | tf_op jit(solution)/shard_map/all_gather | solution.py:405
  60.4 9.3 copy-start.9
  60.4 9.5 copy-start.10
  60.4 9.6 copy-start.8
  60.4 10.9 %copy-start.6 = (f32[4352]{0:T(1024)S(1)}, f32[4352]{0:T(1024)}, u32[]{:S(2)}) copy-start(f32[4352]{0:T(1024)} %param.18) | copy-start | bytes 52228
  60.4 11.6 %copy-start.3 = (f32[4,4352]{1,0:T(4,128)S(1)}, f32[4,4352]{1,0:T(4,128)}, u32[]{:S(2)}) copy-start(f32[4,4352]{1,0:T(4,128)} %param.17) | copy-start | bytes 208900
  67.5 223.3 %all-gather.9.cloned.1.call-start = ((), (), s32[]{:S(2)}) async-start(), calls=%async_computation.8 | async-start | bytes 9437184 | tf_op jit(solution)/shard_map/all_gather | solution.py:406
  68.2 439.2 %reduce-scatter.8.cloned.1.call-start = ((), (), s32[]{:S(2)}) async-start(), calls=%async_computation.10 | async-start | bytes 14417920 | tf_op jit(solution)/shard_map/reduce_scatter | solution.py:465
  396.6 0.7 copy-start.5
  396.6 244.8 %all-reduce.9.cloned.1.call-start = ((), (), s32[]{:S(2)}) async-start(), calls=%async_computation.12 | async-start | bytes 278528 | tf_op jit(solution)/shard_map/psum | solution.py:488
  398.1 338.1 %reduce-scatter.6.cloned.1.call-start = ((), (), s32[]{:S(2)}) async-start(), calls=%async_computation.9 | async-start | bytes 9437184 | tf_op jit(solution)/shard_map/reduce_scatter | solution.py:457
  416.9 410.7 %reduce-scatter.4.cloned.1.call-start = ((), (), s32[]{:S(2)}) async-start(), calls=%async_computation.7 | async-start | bytes 9437184 | tf_op jit(solution)/shard_map/reduce_scatter | solution.py:441
  428.2 490.5 %all-gather.11.cloned.1.call-start = ((), (), s32[]{:S(2)}) async-start(), calls=%async_computation.11 | async-start | bytes 10977280 | tf_op jit(solution)/shard_map/all_gather | solution.py:477
  579.9 1.6 copy-start.2
  586.2 440.1 %all-reduce.11.cloned.1.call-start = ((), (), s32[]{:S(2)}) async-start(), calls=%async_computation.13 | async-start | bytes 8388608 | tf_op jit(solution)/shard_map/psum | solution.py:447
  598.8 0.7 copy-start.7
Sparse Core Ops, SparseCore 0:
  58.9 64.7 all-gather.6
  125.8 82.0 all-gather.4
  209.5 81.1 all-gather.8
  396.8 110.5 reduce-scatter.7
  513.3 128.0 all-reduce.8
  644.2 91.9 reduce-scatter.5
  738.5 89.0 reduce-scatter.3
  829.4 89.2 all-gather.10
  922.5 103.8 all-reduce.10

commit v2 on v1

--- a/solution.py
+++ b/solution.py
@@ -10,6 +10,7 @@
 EPS = 1e-05
 LANES = 128
 VMEM = 56 * 2**20
+FREE = pl.CostEstimate(flops=1, bytes_accessed=1, transcendentals=0)
 
 F32 = jnp.float32
 BF16 = jnp.bfloat16
@@ -63,7 +64,7 @@
     return mm(high, ones) + mm(low, ones)
 
 
-def conv_block(ext_ref, taps_ref, width):
+def conv_block(ext_ref, taps_ref):
     span = 4
     pre = taps_ref[span : span + 1, :] + ext_ref[5 : 5 + BLOCK, :] * taps_ref[0:1, :]
     for tap in range(1, span):
@@ -86,7 +87,7 @@
 
 def forward_kernel(
     mask_ref, hidden_ref, weight_ref, taps_ref, heads_ref, skip_ref,
-    proj_ref, y_ref, state_ref, square_ref,
+    proj_ref, y_ref, state_ref, square_ref, pre_ref,
     ext, state, *, state_dim, width,
 ):
     joint = 2 * state_dim + width
@@ -98,8 +99,9 @@
 
     projected = mm(hidden_ref[...], weight_ref[...]).astype(BF16)
     proj_ref[...] = projected
-    ext[8 : 8 + BLOCK, :] = projected[:, :joint].astype(F32)
-    pre = conv_block(ext, taps_ref, joint)
+    ext[8 : 8 + BLOCK, :] = projected[:, width : width + joint].astype(F32)
+    pre = conv_block(ext, taps_ref)
+    pre_ref[...] = pre
     ext[0:8, :] = ext[BLOCK : BLOCK + 8, :]
     conv_out = pre * jax.nn.sigmoid(pre)
     values = conv_out[:, 2 * state_dim :] * mask_ref[0]
@@ -131,7 +133,7 @@
     state[...] = old * spread(jnp.exp(last), width) + mm3(b_coef, tail, TN)
     y_low = (mixed + skip_ref[0:1, :] * values).astype(BF16)
     y_ref[...] = y_low
-    gate = projected[:, joint : joint + width].astype(F32)
+    gate = projected[:, :width].astype(F32)
     gated = y_low.astype(F32) * (gate * jax.nn.sigmoid(gate))
     square = halves(gated * gated * mask_ref[0])
     ones = jnp.ones((8, width), BF16)
@@ -139,17 +141,17 @@
 
 
 def backward_kernel(
-    mask_ref, joint_ref, before_ref, raw_ref, dy_ref, dgate_ref, state_ref, taps_ref, heads_ref, skip_ref,
-    dproj_ref, conv_grad_ref, head_grad_ref,
-    ext, dext, dstate, rows, *, state_dim, width, blocks,
+    gain_ref, proj_ref, pre_ref, y_ref, d_normed_ref, tokens_ref, state_ref, taps_ref, heads_ref, skip_ref,
+    dproj_ref, conv_grad_ref, head_grad_ref, gain_grad_ref,
+    dext, dstate, rows, *, state_dim, width,
 ):
     joint = 2 * state_dim + width
-    place = blocks - 1 - pl.program_id(1)
 
     @pl.when((pl.program_id(0) == 0) & (pl.program_id(1) == 0))
     def _():
         conv_grad_ref[...] = jnp.zeros_like(conv_grad_ref)
         head_grad_ref[...] = jnp.zeros_like(head_grad_ref)
+        gain_grad_ref[...] = jnp.zeros_like(gain_grad_ref)
         rows[...] = jnp.zeros_like(rows)
 
     @pl.when(pl.program_id(1) == 0)
@@ -157,17 +159,29 @@
         dext[0:8, :] = jnp.zeros((8, joint), F32)
         dstate[...] = jnp.zeros_like(dstate)
 
-    before = before_ref[...].astype(F32)[8:16, :]
-    ext[0:8, :] = jnp.where(place > 0, before, 0.0)
-    ext[8 : 8 + BLOCK, :] = joint_ref[...].astype(F32)
-    pre = conv_block(ext, taps_ref, joint)
+    per_token = tokens_ref[0].T
+    count = gain_ref[0, 2:3, 0:1]
+    root = lax.rsqrt(per_token[:, 0:1] / count + EPS)
+    pull = root * root * per_token[:, 1:2] / count
+    gate = proj_ref[:, :width].astype(F32)
+    y = y_ref[...].astype(F32)
+    gate_sig = jax.nn.sigmoid(gate)
+    silu = gate * gate_sig
+    normed_gated = y * silu * root * gain_ref[0, 1:2, :]
+    d_normed = d_normed_ref[...]
+    gain_grad_ref[0:1, :] += jnp.sum(d_normed * normed_gated, axis=0, keepdims=True)
+    d_gated = root * (d_normed * gain_ref[0, 0:1, :]) - normed_gated * pull
+    dy_low = (d_gated * silu).astype(BF16)
+    dproj_ref[:, :width] = (d_gated * y * gate_sig * (1.0 + gate * (1.0 - gate_sig))).astype(BF16)
+
+    pre = pre_ref[...]
     sig = jax.nn.sigmoid(pre)
     conv_out = pre * sig
-    mask = mask_ref[0]
+    mask = gain_ref[0, 1:2, :]
     values = conv_out[:, 2 * state_dim :] * mask
     b_coef = halves(conv_out[:, :state_dim])
     c_coef = halves(conv_out[:, state_dim : 2 * state_dim])
-    biased, step_size, decay = step_rates(raw_ref[...].astype(F32), heads_ref)
+    biased, step_size, decay = step_rates(proj_ref[:, joint + width :].astype(F32), heads_ref)
     later = triangle(lambda row, col: col >= row)
     cumulative = mm_exact(triangle(lambda row, col: row >= col).astype(BF16), decay)
     across = cumulative.T
@@ -175,7 +189,6 @@
     step_chan = spread(step_size, width)
     scaled = values * step_chan
     scaled_parts = halves(scaled)
-    dy_low = dy_ref[...]
     dy = dy_low.astype(F32)
     scores = mm3(b_coef, c_coef, NT)
     low_half = lax.broadcasted_iota(jnp.int32, (BLOCK, LANES), 1) < LANES // 2
@@ -241,16 +254,16 @@
     d_values = (d_scaled * step_chan + skip_ref[0:1, :] * dy) * mask
     d_conv = jnp.concatenate([d_b, d_c, d_values], axis=1)
     d_pre = d_conv * (sig * (1.0 + pre * (1.0 - sig)))
-    for tap in range(4):
-        conv_grad_ref[tap : tap + 1, :] += jnp.sum(d_pre * ext[5 + tap : 5 + tap + BLOCK, :], axis=0, keepdims=True)
     conv_grad_ref[4:5, :] += jnp.sum(d_pre, axis=0, keepdims=True)
     dext[BLOCK : BLOCK + 8, :] = dext[0:8, :]
     dext[0:BLOCK, :] = d_pre
-    d_in = dext[3 : 3 + BLOCK, :] * taps_ref[0:1, :]
-    for tap in range(1, 4):
-        d_in = d_in + dext[3 - tap : 3 - tap + BLOCK, :] * taps_ref[tap : tap + 1, :]
-    dproj_ref[:, :joint] = d_in.astype(BF16)
-    dproj_ref[:, joint : joint + width] = dgate_ref[...]
+    conv_in = proj_ref[:, width : width + joint].astype(F32)
+    d_in = None
+    for tap in range(4):
+        ahead = d_pre if tap == 3 else dext[3 - tap : 3 - tap + BLOCK, :]
+        conv_grad_ref[tap : tap + 1, :] += jnp.sum(ahead * conv_in, axis=0, keepdims=True)
+        d_in = ahead * taps_ref[tap : tap + 1, :] if tap == 0 else d_in + ahead * taps_ref[tap : tap + 1, :]
+    dproj_ref[:, width : width + joint] = d_in.astype(BF16)
     dproj_ref[:, joint + width :] = d_raw.astype(BF16)
 
 
@@ -286,12 +299,14 @@
             pl.BlockSpec((BLOCK, width), row),
             pl.BlockSpec((1, state_dim, width), lambda s, c: (s * blocks + c, 0, 0)),
             pl.BlockSpec((1, 8, BLOCK), lambda s, c: (s * blocks + c, 0, 0)),
+            pl.BlockSpec((BLOCK, joint), row),
         ],
         out_shape=[
             jax.ShapeDtypeStruct((tokens, columns), BF16),
             jax.ShapeDtypeStruct((tokens, width), BF16),
             jax.ShapeDtypeStruct((seqs * blocks, state_dim, width), F32),
             jax.ShapeDtypeStruct((seqs * blocks, 8, BLOCK), F32),
+            jax.ShapeDtypeStruct((tokens, joint), F32),
         ],
         scratch_shapes=[
             pltpu.VMEM((BLOCK + 8, joint), F32),
@@ -300,29 +315,31 @@
         compiler_params=pltpu.CompilerParams(
             dimension_semantics=("arbitrary", "arbitrary"), vmem_limit_bytes=VMEM
         ),
+        cost_estimate=FREE,
         name="mixer_forward",
     )(mask, hidden, weight, taps, heads, skip)
 
 
-def mixer_backward(mask, projected, d_y, d_gate, states, taps, heads, skip, state_dim, width):
-    seqs = mask.shape[0]
+def mixer_backward(gains, projected, pre, y_all, d_normed, token_rows, states, taps, heads, skip, state_dim):
+    seqs, _, width = gains.shape
     tokens, columns = projected.shape
     blocks = tokens // seqs // BLOCK
     joint = 2 * state_dim + width
     place = lambda s, c: s * blocks + blocks - 1 - c
     row = lambda s, c: (place(s, c), 0)
+    block = lambda s, c: (place(s, c), 0, 0)
     whole = lambda s, c: (0, 0)
     return pl.pallas_call(
-        lambda *refs: backward_kernel(*refs, state_dim=state_dim, width=width, blocks=blocks),
+        lambda *refs: backward_kernel(*refs, state_dim=state_dim, width=width),
         grid=(seqs, blocks),
         in_specs=[
-            pl.BlockSpec((1, 1, width), lambda s, c: (s, 0, 0)),
+            pl.BlockSpec((1, 8, width), lambda s, c: (s, 0, 0)),
+            pl.BlockSpec((BLOCK, columns), row),
             pl.BlockSpec((BLOCK, joint), row),
-            pl.BlockSpec((16, joint), lambda s, c: (jnp.maximum(place(s, c) * (BLOCK // 16) - 1, 0), 0)),
-            pl.BlockSpec((BLOCK, LANES), lambda s, c: (place(s, c), (joint + width) // LANES)),
             pl.BlockSpec((BLOCK, width), row),
             pl.BlockSpec((BLOCK, width), row),
-            pl.BlockSpec((1, state_dim, width), lambda s, c: (place(s, c), 0, 0)),
+            pl.BlockSpec((1, 8, BLOCK), block),
+            pl.BlockSpec((1, state_dim, width), block),
             pl.BlockSpec((8, joint), whole),
             pl.BlockSpec((8, LANES), whole),
             pl.BlockSpec((8, width), whole),
@@ -331,14 +348,15 @@
             pl.BlockSpec((BLOCK, columns), row),
             pl.BlockSpec((8, joint), whole),
             pl.BlockSpec((8, LANES), whole),
+            pl.BlockSpec((8, width), whole),
         ],
         out_shape=[
             jax.ShapeDtypeStruct((tokens, columns), BF16),
             jax.ShapeDtypeStruct((8, joint), F32),
             jax.ShapeDtypeStruct((8, LANES), F32),
+            jax.ShapeDtypeStruct((8, width), F32),
         ],
         scratch_shapes=[
-            pltpu.VMEM((BLOCK + 8, joint), F32),
             pltpu.VMEM((BLOCK + 8, joint), F32),
             pltpu.VMEM((state_dim, width), F32),
             pltpu.VMEM((LANES, BLOCK), F32),
@@ -346,8 +364,54 @@
         compiler_params=pltpu.CompilerParams(
             dimension_semantics=("arbitrary", "arbitrary"), vmem_limit_bytes=VMEM
         ),
+        cost_estimate=FREE,
         name="mixer_backward",
-    )(mask, projected, projected, projected, d_y, d_gate, states, taps, heads, skip)
+    )(gains, projected, pre, y_all, d_normed, token_rows, states, taps, heads, skip)
+
+
+def row_sum(value):
+    ones = jnp.ones((8, value.shape[1]), BF16)
+    high, low = halves(value)
+    return mm(ones, high, NT) + mm(ones, low, NT)
+
+
+def pull_kernel(cot_ref, weight_ref, gate_ref, y_ref, gain_ref, d_normed_ref, dot_ref):
+    d_normed = mm(cot_ref[...], weight_ref[...], NT)
+    d_normed_ref[...] = d_normed
+    gate = gate_ref[...].astype(F32)
+    gated = y_ref[...].astype(F32) * (gate * jax.nn.sigmoid(gate))
+    dot_ref[0] = row_sum(d_normed * gain_ref[0, 0:1, :] * gated)
+
+
+def pull_back(cot_all, weight, projected, y_all, gains, gate_place):
+    seqs, _, width = gains.shape
+    tokens, depth = cot_all.shape
+    blocks = tokens // seqs // BLOCK
+    row = lambda s, c: (s * blocks + c, 0)
+    return pl.pallas_call(
+        pull_kernel,
+        grid=(seqs, blocks),
+        in_specs=[
+            pl.BlockSpec((BLOCK, depth), row),
+            pl.BlockSpec((width, depth), lambda s, c: (0, 0)),
+            pl.BlockSpec((BLOCK, width), lambda s, c: (s * blocks + c, gate_place)),
+            pl.BlockSpec((BLOCK, width), row),
+            pl.BlockSpec((1, 8, width), lambda s, c: (s, 0, 0)),
+        ],
+        out_specs=[
+            pl.BlockSpec((BLOCK, width), row),
+            pl.BlockSpec((1, 8, BLOCK), lambda s, c: (s * blocks + c, 0, 0)),
+        ],
+        out_shape=[
+            jax.ShapeDtypeStruct((tokens, width), F32),
+            jax.ShapeDtypeStruct((seqs * blocks, 8, BLOCK), F32),
+        ],
+        compiler_params=pltpu.CompilerParams(
+            dimension_semantics=("arbitrary", "arbitrary"), vmem_limit_bytes=VMEM
+        ),
+        cost_estimate=FREE,
+        name="pull_back",
+    )(cot_all, weight, projected, y_all, gains)
 
 
 def pad_last(array, size):
@@ -359,6 +423,157 @@
 
 def pad_rows(array, size):
     return jnp.pad(array, [(0, size - array.shape[0]), (0, 0)])
+
+
+def swap(value, axis, bit):
+    size = lax.axis_size(axis)
+    return lax.ppermute(value, axis, [(place, place ^ bit) for place in range(size)])
+
+
+def all_sum(value, axis):
+    bit = 1
+    while bit < lax.axis_size(axis):
+        value = value + swap(value, axis, bit)
+        bit *= 2
+    return value
+
+
+NEAR_FAR = ((1, 2), (2, 1))
+
+
+def reduce_cut(share, block, dtype):
+    return [
+        jnp.concatenate([block(share, near ^ far, half), block(share, near, half)], axis=0).astype(dtype)
+        for half, (near, far) in enumerate(NEAR_FAR)
+    ]
+
+
+def reduce_near(cuts):
+    return [swap(cut, "dp", near) for cut, (near, _) in zip(cuts, NEAR_FAR)]
+
+
+def reduce_far(share, block, got):
+    rows = got[0].shape[0] // 2
+    kept = [
+        (block(share, far, half) + got[half][:rows].astype(F32)).astype(got[half].dtype)
+        for half, (_, far) in enumerate(NEAR_FAR)
+    ]
+    mine = [block(share, 0, half) + got[half][rows:].astype(F32) for half in range(2)]
+    kept = lax.optimization_barrier(kept)
+    far_got = [swap(piece, "dp", far) for piece, (_, far) in zip(kept, NEAR_FAR)]
+    return jnp.concatenate([piece + other.astype(F32) for piece, other in zip(mine, far_got)], axis=0)
+
+
+def dp_gather(own):
+    rows = own.shape[0] // 2
+    upper, lower = own[:rows], own[rows:]
+    upper1, lower2 = swap(upper, "dp", 1), swap(lower, "dp", 2)
+    uppers = swap(jnp.concatenate([upper, upper1], axis=0), "dp", 2)
+    lowers = swap(jnp.concatenate([lower, lower2], axis=0), "dp", 1)
+    return [(upper, lower), (upper1, lowers[:rows]), (uppers[:rows], lower2), (uppers[rows:], lowers[rows:])]
+
+
+def line_permute(block, reach):
+    chips = lax.axis_size("mp") // 2
+    pairs = [(2 * z + c, 2 * ((z + reach) % chips) + c) for z in range(chips) for c in range(2)]
+    return lax.ppermute(block, "mp", pairs)
+
+
+def line_send(shares):
+    groups = [list(range(core, lax.axis_size("mp"), 2)) for core in range(2)]
+    return lax.all_to_all(shares, "mp", split_axis=0, concat_axis=0, axis_index_groups=groups, tiled=True)
+
+
+def pair_kernel(place_ref, own_ref, sibling_ref, own_weight_ref, sibling_weight_ref, *out_refs, dims):
+    share = mm(own_ref[...], own_weight_ref[...], dims) + mm(sibling_ref[...], sibling_weight_ref[...], dims)
+    share = share.astype(BF16)
+    if len(out_refs) == 1:
+        out_refs[0][0] = share
+        return
+    for reach, out_ref in enumerate(out_refs):
+
+        @pl.when(pl.program_id(0) == reach)
+        def _(out_ref=out_ref):
+            out_ref[...] = share
+
+
+def pair_product(left, theirs, own_weight, sibling_weight, dims, depth, tokens, stacked):
+    chips = lax.axis_size("mp") // 2
+    inner = left.shape[1]
+    whole = lambda i, place: (0, 0)
+    place = lax.axis_index("mp").astype(jnp.int32)
+    there = lambda i, place: lax.rem(place[0] + i, chips)
+    return pl.pallas_call(
+        lambda *refs: pair_kernel(*refs, dims=dims),
+        grid_spec=pltpu.PrefetchScalarGridSpec(
+            num_scalar_prefetch=1,
+            grid=(chips,),
+            in_specs=[
+                pl.BlockSpec((tokens, inner), lambda i, place: (2 * there(i, place) + place[1], 0)),
+                pl.BlockSpec((tokens, inner), lambda i, place: (there(i, place), 0)),
+                pl.BlockSpec(own_weight.shape, whole),
+                pl.BlockSpec(sibling_weight.shape, whole),
+            ],
+            out_specs=[pl.BlockSpec((1, tokens, depth), lambda i, place: (there(i, place), 0, 0))]
+            if stacked
+            else [pl.BlockSpec((tokens, depth), whole)] * chips,
+        ),
+        out_shape=[jax.ShapeDtypeStruct((chips, tokens, depth), BF16)]
+        if stacked
+        else [jax.ShapeDtypeStruct((tokens, depth), BF16)] * chips,
+        compiler_params=pltpu.CompilerParams(dimension_semantics=("arbitrary",), vmem_limit_bytes=VMEM),
+        cost_estimate=FREE,
+        name="pair_product",
+    )(jnp.stack([place // 2, place % 2]), left, theirs, own_weight, sibling_weight)
+
+
+def for_sibling(left, tokens):
+    mp = lax.axis_size("mp")
+    by_core = left.reshape(mp // 2, 2, tokens, left.shape[1])
+    other = 1 - lax.axis_index("mp") % 2
+    return lax.dynamic_index_in_dim(by_core, other, 1, keepdims=False).reshape(-1, left.shape[1])
+
+
+def in_place_order(pieces):
+    place = lax.axis_index("dp")
+    pieces = [jnp.concatenate(pair, axis=0) for pair in pieces]
+    odd, high = place % 2 == 1, place // 2 == 1
+    lows = [jnp.where(odd, pieces[k ^ 1], pieces[k]) for k in range(4)]
+    return jnp.concatenate([jnp.where(high, lows[k ^ 2], lows[k]).astype(F32) for k in range(4)], axis=0)
+
+
+def assemble_kernel(place_ref, *refs):
+    out_ref = refs[-1]
+    for own in range(4):
+
+        @pl.when(place_ref[0] == own)
+        def _(own=own):
+            order = [refs[2 * (own ^ p) + half][...].astype(F32) for p in range(4) for half in range(2)]
+            out_ref[...] = jnp.concatenate(order, axis=0).T
+
+
+def assemble(gathered):
+    pieces = [half for pair in gathered for half in pair]
+    half_rows, columns = pieces[0].shape
+    chunk = 512
+    return pl.pallas_call(
+        assemble_kernel,
+        grid=(pl.cdiv(columns, chunk),),
+        in_specs=[pl.BlockSpec(memory_space=pltpu.SMEM)]
+        + [pl.BlockSpec((half_rows, chunk), lambda i: (0, i)) for _ in pieces],
+        out_specs=pl.BlockSpec((chunk, 8 * half_rows), lambda i: (i, 0)),
+        out_shape=jax.ShapeDtypeStruct((columns, 8 * half_rows), F32),
+        compiler_params=pltpu.CompilerParams(dimension_semantics=("arbitrary",), vmem_limit_bytes=VMEM),
+        cost_estimate=FREE,
+        name="assemble",
+    )(lax.axis_index("dp").astype(jnp.int32)[None], *pieces).T
+
+
+def total(blocks):
+    result = blocks[0].astype(F32)
+    for index in range(1, len(blocks)):
+        result = result + blocks[index].astype(F32)
+    return result
 
 
 def on_device(
@@ -386,24 +601,39 @@
     )
     send = jnp.concatenate(
         [
+            by_place(slab[:, :inner], width),
             jnp.broadcast_to(slab[None, :, 2 * inner : 2 * inner + 2 * state_dim], (mp, part, 2 * state_dim)),
             by_place(slab[:, inner : 2 * inner], width),
-            by_place(slab[:, :inner], width),
             by_place(slab[:, inner + channels :], LANES),
         ],
         axis=2,
     )
     got = lax.all_to_all(send, "mp", split_axis=0, concat_axis=0, tiled=True)
-    weight = lax.all_gather(got.reshape(mp * part, columns), "dp", axis=0, tiled=True)
-
-    reorder = lambda array: array.reshape(-1, mp, dp, part).transpose(0, 2, 1, 3).reshape(-1, depth)
-    restore = lambda array: array.reshape(-1, dp, mp, part).transpose(0, 2, 1, 3).reshape(-1, depth)
+
+    def reorder(array):
+        apart = array.reshape(-1, mp, dp, part)
+        return jnp.concatenate(
+            [
+                lax.dynamic_index_in_dim(apart, dp_place ^ k, 2, keepdims=False).reshape(-1, mp * part)
+                for k in range(dp)
+            ],
+            axis=1,
+        )
+
+    def restore(array):
+        apart = array.reshape(-1, dp, mp, part)
+        return jnp.stack(
+            [lax.dynamic_index_in_dim(apart, dp_place ^ k, 1, keepdims=False) for k in range(dp)], axis=2
+        ).reshape(-1, depth)
+
+    line = mp <= 16
     inputs_f = inputs.astype(F32)
     rms_scale = lax.rsqrt(jnp.mean(inputs_f * inputs_f, axis=-1, keepdims=True) + EPS)
     normed = inputs_f * rms_scale
     hidden_own = reorder((normed * norm_gain[None, :]).astype(BF16))
+    hidden_own, got = lax.optimization_barrier((hidden_own, got))
+    weight = jnp.concatenate(sum(dp_gather(got.reshape(mp * part, columns)), ()), axis=0)
     hidden = lax.all_gather(hidden_own, "mp", axis=0, tiled=True)
-    cot_all = lax.all_gather(cotangent, "mp", axis=0, tiled=True)
 
     first_chan, first_head = mp_place * own, mp_place * own_heads
     cut = lambda array, first, size: lax.dynamic_slice_in_dim(array, first, size, array.ndim - 1)
@@ -425,11 +655,15 @@
     if seqs > 1:
         active_count = per_token(active_count)
 
-    projected, y_all, states, squares = mixer_forward(
+    if line:
+        sibling_out, sibling_weight = swap(out_weight, "mp", 1), swap(weight, "mp", 1)
+        weight, sibling_out, sibling_weight = lax.optimization_barrier((weight, sibling_out, sibling_weight))
+    projected, y_all, states, squares, pre = mixer_forward(
         mask, hidden, weight, taps, head_params, skip, state_dim, width
     )
-    total_square = lax.psum(squares[:, 0, :].reshape(all_tokens), "mp")[:, None]
-    gate = projected[:, joint : joint + own].astype(F32)
+    square_rows = all_sum(squares[:, 0, :], "mp")
+    total_square = square_rows.reshape(all_tokens)[:, None]
+    gate = projected[:, :own].astype(F32)
     y_f = y_all[:, :own].astype(F32)
     gate_sig = jax.nn.sigmoid(gate)
     silu_z = gate * gate_sig
@@ -437,45 +671,48 @@
     gain = cut(out_gain, first_chan, own)[None, :]
     out_root = lax.rsqrt(total_square / active_count + EPS)
     normed_out = (gated * out_root * gain * mask_tok).astype(BF16)
-    share = jnp.dot(normed_out, out_weight, preferred_element_type=F32).astype(BF16)
-    summed = lax.psum_scatter(share, "mp", scatter_dimension=0, tiled=True)
-    outputs = (inputs_f + summed.astype(F32)).astype(BF16)
-
-    d_normed = mm(cot_all, out_weight, NT)
-    upstream = d_normed * gain * mask_tok
-    inner_dot = lax.psum(jnp.sum(upstream * gated, axis=-1), "mp")[:, None]
-    out_weight_grad = lax.psum(mm(normed_out, cot_all, TN), "dp")
-    out_gain_grad = jnp.sum(d_normed * gated * out_root * mask_tok, axis=0)
-    d_gated = out_root * upstream - out_root * out_root * out_root * mask_tok * gated * inner_dot / active_count
-    d_y = pad_last((d_gated * silu_z).astype(BF16), width)
-    d_gate = pad_last((d_gated * y_f * gate_sig * (1.0 + gate * (1.0 - gate_sig))).astype(BF16), width)
-    d_proj, conv_grads, head_grads = mixer_backward(
-        mask, projected, d_y, d_gate, states, taps, head_params, skip, state_dim, width
-    )
-
-    d_share = mm(d_proj, weight, NT).astype(BF16)
-    d_hidden = lax.psum_scatter(d_share, "mp", scatter_dimension=0, tiled=True)
-    d_hidden = restore(d_hidden.astype(F32))
-    norm_gain_grad = jnp.sum(d_hidden * normed, axis=0)
-    d_normed_in = d_hidden * norm_gain[None, :]
-    input_back = rms_scale * (d_normed_in - normed * jnp.mean(d_normed_in * normed, axis=-1, keepdims=True))
-    input_grad = (cotangent.astype(F32) + input_back).astype(BF16)
-
-    weight_part = mm(hidden, d_proj, TN)
-    mine = lax.psum_scatter(weight_part, "dp", scatter_dimension=0, tiled=True)
-    blocks = lax.all_to_all(mine.reshape(mp, part, columns), "mp", split_axis=0, concat_axis=0, tiled=True)
-    flat = lambda piece: piece.transpose(1, 0, 2).reshape(part, -1)
-    grad_rows = jnp.concatenate(
+    if line:
+        theirs = swap(for_sibling(normed_out, tokens), "mp", 1)
+        shares = pair_product(normed_out, theirs, out_weight, sibling_out, NN, depth, tokens, True)[0]
+        cot_all = lax.all_gather(cotangent, "mp", axis=0, tiled=True)
+        cot_all, shares = lax.optimization_barrier((cot_all, shares))
+    else:
+        shares = mm(normed_out, out_weight).astype(BF16)
+        sent = [lax.psum_scatter(shares, "mp", scatter_dimension=0, tiled=True)]
+        late_cot, sent = lax.optimization_barrier((cotangent, sent))
+        cot_all = lax.all_gather(late_cot, "mp", axis=0, tiled=True)
+
+    gain_rows = pad_last(cut(out_gain, first_chan, own), width)
+    gains = jnp.concatenate(
         [
-            flat(blocks[:, :, joint : joint + own]),
-            flat(blocks[:, :, 2 * state_dim : 2 * state_dim + own]),
-            jnp.sum(blocks[:, :, : 2 * state_dim], axis=0),
-            flat(blocks[:, :, joint + width : joint + width + own_heads]),
+            gain_rows[None, None, :] * mask,
+            mask,
+            jnp.broadcast_to((active_heads * head_dim).astype(F32)[:, None, None], mask.shape),
+            jnp.zeros((seqs, 5, width), F32),
         ],
         axis=1,
     )
-    in_weight_grad = lax.all_gather(grad_rows, "dp", axis=0, tiled=True)
-
+    out_padded = pad_rows(out_weight, width)
+    d_normed, dots = pull_back(cot_all, out_padded, projected, y_all, gains, 0)
+    dot_rows = all_sum(dots[:, 0, :], "mp")
+    out_part = mm(normed_out, cot_all, TN)
+    if line:
+        dot_rows, shares = lax.optimization_barrier((dot_rows, shares))
+        sent = line_send(shares)
+    token_rows = jnp.stack([square_rows, dot_rows] + [jnp.zeros_like(dot_rows)] * 6, axis=1)
+    quarter = depth // dp
+
+    def in_block(share, k, half):
+        return share[k * quarter + half * (quarter // 2) : k * quarter + (half + 1) * (quarter // 2)]
+
+    def to_rows(mine):
+        return lax.all_to_all(mine.astype(BF16).reshape(mp, part, -1), "mp", split_axis=0, concat_axis=0, tiled=True)
+
+    token_rows, out_part = lax.optimization_barrier((token_rows, out_part))
+    out_mine = lax.psum_scatter(out_part, "dp", scatter_dimension=0, tiled=True)
+    d_proj, conv_grads, head_grads, gain_grads = mixer_backward(
+        gains, projected, pre, y_all, d_normed, token_rows, states, taps, head_params, skip, state_dim
+    )
     def place_in(array, first, size):
         return lax.dynamic_update_slice_in_dim(
             jnp.zeros(array.shape[:-1] + (size,), F32), array, first, array.ndim - 1
@@ -484,10 +721,64 @@
     conv_own = place_in(conv_grads[:5, 2 * state_dim : 2 * state_dim + own], first_chan, inner)
     conv_full = jnp.concatenate([conv_own, conv_grads[:5, : 2 * state_dim]], axis=1)
     head_full = place_in(head_grads[:3, :own_heads], first_head, heads)
-    gain_full = place_in(out_gain_grad, first_chan, inner)
-    conv_total, head_total, gain_total, norm_total = lax.psum(
-        (conv_full, head_full, gain_full, norm_gain_grad), ("dp", "mp")
-    )
+    gain_full = place_in(gain_grads[0, :own], first_chan, inner)
+    small = [conv_full.reshape(-1), head_full.reshape(-1), gain_full]
+    sizes = [piece.shape[0] for piece in small]
+    packed = jnp.concatenate(small)
+    count = -(-packed.shape[0] // 1024) * 1024
+    packed = jnp.pad(packed, (0, count - packed.shape[0])).reshape(-1, LANES)
+
+    if line:
+        d_proj, out_mine = lax.optimization_barrier((d_proj, out_mine))
+        theirs = swap(for_sibling(d_proj, tokens), "mp", 1)
+        share = mm(hidden, d_proj, TN)
+        near_cut = reduce_cut(share, in_block, BF16)
+        near_cut, theirs = lax.optimization_barrier((near_cut, theirs))
+        near_got = reduce_near(near_cut)
+        d_shares = pair_product(d_proj, theirs, weight, sibling_weight, NT, depth, tokens, False)
+        near_got, d_shares, sent = lax.optimization_barrier((near_got, d_shares, sent))
+        d_blocks = [d_shares[0], line_permute(d_shares[1], 1)]
+        mine = reduce_far(share, in_block, near_got)
+        mine, d_blocks, out_mine, packed = lax.optimization_barrier((mine, d_blocks, out_mine, packed))
+        out_weight_grad = lax.all_gather(out_mine, "dp", axis=0, tiled=True)
+        blocks = to_rows(mine)
+        d_blocks += [line_permute(d_shares[reach], reach) for reach in range(2, min(3, mp // 2))]
+        blocks, d_blocks, d_shares, packed, out_weight_grad = lax.optimization_barrier(
+            (blocks, d_blocks, d_shares, all_sum(packed, "dp"), out_weight_grad)
+        )
+        d_blocks += [line_permute(d_shares[reach], reach) for reach in range(3, mp // 2)]
+        d_hidden = total(d_blocks)
+    else:
+        packed = all_sum(packed, "dp")
+        out_weight_grad = lax.all_gather(out_mine, "dp", axis=0, tiled=True)
+        share = mm(hidden, d_proj, TN)
+        d_proj, share = lax.optimization_barrier((d_proj, share))
+        blocks = to_rows(reduce_far(share, in_block, reduce_near(reduce_cut(share, in_block, BF16))))
+        d_shares = mm(d_proj, weight, NT).astype(BF16)
+        d_hidden = lax.psum_scatter(d_shares, "mp", scatter_dimension=0, tiled=True).astype(F32)
+    outputs = (inputs_f + total(sent)).astype(BF16)
+    d_hidden = restore(d_hidden)
+    norm_gain_grad = jnp.sum(d_hidden * normed, axis=0)
+    norm_part = all_sum(norm_gain_grad.reshape(-1, LANES), "dp")
+    everything = all_sum(jnp.concatenate([packed, norm_part], axis=0), "mp")
+    norm_total = everything[packed.shape[0] :].reshape(depth)
+    packed = everything.reshape(-1)
+    conv_total = packed[: sizes[0]].reshape(conv_full.shape)
+    head_total = packed[sizes[0] : sizes[0] + sizes[1]].reshape(head_full.shape)
+    gain_total = packed[sizes[0] + sizes[1] : sum(sizes)]
+
+    d_normed_in = d_hidden * norm_gain[None, :]
+    input_back = rms_scale * (d_normed_in - normed * jnp.mean(d_normed_in * normed, axis=-1, keepdims=True))
+    input_grad = (cotangent.astype(F32) + input_back).astype(BF16)
+
+    flat = lambda first, size: blocks[:, :, first : first + size].transpose(1, 0, 2).reshape(part, -1)
+    shared = jnp.sum(blocks[:, :, width : width + 2 * state_dim].astype(F32), axis=0).astype(BF16)
+    grad_rows = jnp.concatenate(
+        [flat(0, own), flat(width + 2 * state_dim, own), shared, flat(width + joint, own_heads)], axis=1
+    )
+    gathered = dp_gather(grad_rows)
+    in_weight_grad = assemble(gathered) if line else in_place_order(gathered)
+
     return (
         outputs,
         input_grad,

time: 1050 us -> 598 us (0.57)
  waiting for transfers between devices: 601 us -> 267 us
  blocking collectives: 183 us -> 0 us
  Pallas kernels: 89.4 us -> 145 us
  starting transfers between devices: 0.83 us -> 45.7 us
  matrix products: 71.2 us -> 28.9 us
    ppermute x0 -> x32, waiting for transfers between devices: none -> 216 us  [the longest x29 127 us: swap(): lax.ppermute(value, axis, [(place, place ^ bit) for place in range(size)])]
    reduce_scatter x3 -> x1, waiting for transfers between devices: 210 us -> 0.02 us  [on_device(): out_mine = lax.psum_scatter(out_part, 'dp', scatter_dimension=0, tiled=True)]
    psum x2 -> x0, waiting for transfers between devices: 140 us -> none  [the longest x1 98.5 us: on_device(): out_weight_grad = lax.psum(mm(normed_out, cot_all, TN), 'dp')]
    all_gather x2 -> x1, waiting for transfers between devices: 137 us -> 0.01 us  [on_device(): out_weight_grad = lax.all_gather(out_mine, 'dp', axis=0, tiled=True)]
    all_to_all x2 -> x0, blocking collectives: 114 us -> none  [the longest x1 72.5 us: on_device(): lax.all_to_all(mine.reshape(mp, part, columns), 'mp', split_axis=0, conca...]
    all_gather x1, waiting for transfers between devices: 84.3 us -> 11.3 us  [on_device(): hidden = lax.all_gather(hidden_own, 'mp', axis=0, tiled=True)]
    psum x3 -> x0, blocking collectives: 69.5 us -> none  [the longest x1 40 us: on_device(): lax.psum((conv_full, head_full, gain_full, norm_gain_grad), ('dp', 'mp'))]
    pallas_call x0 -> x4, Pallas kernels: none -> 56.1 us  [the longest x2 31.2 us: pair_product(): pl.pallas_call(lambda *refs: pair_kernel(*refs, dims=dims), grid_spec=plt...]
  transfers between devices with their start and end apart: 9 -> 39, of which waited for: 9 -> 29; matrix products, arithmetic and copies ran while one was open for 9% -> 16% of each run, Pallas kernels for 4% -> 20%
where the time goes in v2:
time: 598 us; the launch traced here: 587 us
  waiting for transfers between devices  267 us (45%)
  Pallas kernels  145 us (24%)
  local copies, waits for them, and re-layouts  51.5 us (9%)
  starting transfers between devices  45.7 us (8%)
  other arithmetic  34.2 us (6%)
  matrix products  28.9 us (5%)
  between operations  15.1 us (3%)
    ppermute x29, waiting for transfers between devices, swap(): lax.ppermute(value, axis, [(place, place ^ bit) for place in range(size)])  127 us
    ppermute x3, waiting for transfers between devices, line_permute(): return lax.ppermute(block, 'mp', pairs)  89.3 us
    pallas_call x1, Pallas kernels, mixer_backward(): pl.pallas_call(lambda *refs: backward_kernel(*refs, state_dim=state_dim,...  49.6 us
    pallas_call x1, Pallas kernels, mixer_forward(): pl.pallas_call(lambda *refs: forward_kernel(*refs, state_dim=state_dim, w...  39.1 us
    pallas_call x2, Pallas kernels, pair_product(): pl.pallas_call(lambda *refs: pair_kernel(*refs, dims=dims), grid_spec=plt...  31.2 us
    dot_general x2, matrix products, mm(): return lax.dot_general(left, right, dims, preferred_element_type=F32)  28.9 us
    all_to_all x1, waiting for transfers between devices, on_device(): got = lax.all_to_all(send, 'mp', split_axis=0, concat_axis=0, tiled=True)  25.4 us
    ppermute x29, starting transfers between devices, swap(): lax.ppermute(value, axis, [(place, place ^ bit) for place in range(size)])  23.5 us
  transfers between devices with their start and end apart: 39, of which 29 were waited for; matrix products, arithmetic and copies ran while one was open for 16% of the time, Pallas kernels for 20%

profile of v2, /device:TPU:0, one launch (start us, length us, event | category | flops | bytes accessed | tf_op | source)
XLA Modules:
  0.0 587.2 jit_solution(16865071635803097394)
XLA Ops:
  13.4 6.5 %all-to-all-start = ((bf16[8,64,1408]{2,1,0:T(8,128)(2,1)}), bf16[8,64,1408]{2,1,0:T(8,128)(2,1)S(1)}, u32[]{:S(2)}, u32[]{:S(2)}) async-start(bf16[8,64,1408]{2,1,0:T(8,128)(2,1)} %fusion.20), calls=%async_computation | async-start | bytes 2883584 | tf_op jit(solution)/shard_map/all_to_all | solution.py:611
  29.5 25.4 %all-to-all-done = bf16[8,64,1408]{2,1,0:T(8,128)(2,1)S(1)} async-done(((bf16[8,64,1408]{2,1,0:T(8,128)(2,1)}), bf16[8,64,1408]{2,1,0:T(8,128)(2,1)S(1)}, u32[]{:S(2)}, u32[]{:S(2)}) %all-to-all-start) | async-done | bytes 1441824 | tf_op jit(solution)/shard_map/all_to_all | solution.py:611
  59.0 14.7 %collective-permute-done.1 = bf16[256,1408]{1,0:T(8,128)(2,1)S(1)} collective-permute-done((bf16[256,1408]{1,0:T(8,128)(2,1)S(1)}, bf16[256,1408]{1,0:T(8,128)(2,1)S(1)}, u32[]{:S(2)}, u32[]{:S(2)}) %collective-permute-start.1) | collective-permute-done | bytes 720928 | tf_op jit(solution)/shard_map/ppermute | solution.py:430
  79.9 26.4 %collective-permute-done.2 = bf16[512,1408]{1,0:T(8,128)(2,1)S(1)} collective-permute-done((bf16[512,1408]{1,0:T(8,128)(2,1)S(1)}, bf16[512,1408]{1,0:T(8,128)(2,1)S(1)}, u32[]{:S(2)}, u32[]{:S(2)}) %collective-permute-start.2) | collective-permute-done | bytes 1441824 | tf_op jit(solution)/shard_map/ppermute | solution.py:430
  115.6 7.8 %collective-permute-done.4.refs_4_ = bf16[512,2048]{1,0:T(8,128)(2,1)} collective-permute-done((bf16[512,2048]{1,0:T(8,128)(2,1)S(1)}, bf16[512,2048]{1,0:T(8,128)(2,1)}, u32[]{:S(2)}, u32[]{:S(2)}) %collective-permute-start.4) | collective-permute-done | bytes 2097184 | tf_op jit(solution)/shard_map/ppermute | solution.py:430
  124.7 11.3 %all-gather.4.cloned.1.call-done.refs_1_ = bf16[2048,2048]{1,0:T(8,128)(2,1)} async-done(((bf16[256,2048]{1,0:T(8,128)(2,1)}), bf16[2048,2048]{1,0:T(8,128)(2,1)}) %all-gather.4.cloned.1.call-update) | async-done | bytes 8388624 | tf_op jit(solution)/shard_map/all_gather | solution.py:636
  136.0 39.1 %mixer_forward.1 = (bf16[2048,1408]{1,0:T(8,128)(2,1)}, bf16[2048,512]{1,0:T(8,128)(2,1)}, f32[8,128,512]{2,1,0:T(8,128)}, f32[8,8,256]{2,1,0:T(8,128)}, f32[2048,768]{1,0:T(8,128)}) custom-call(f32[1,1,512]{2,1,0:T(1,128)} %broadcast_in_dim.54.refs_0_, bf16[2048,2048]{1,0:T(8,128)(2,1)} %all-gather.4.cloned.1.call-done.refs_1_, ...), custom_call_target="tpu_custom_call" | custom-call | flops 1 | bytes 1 | tf_op jit(solution)/shard_map/mixer_forward/pallas_call | solution.py:286
  177.3 6.2 %collective-permute-done.7 = f32[8,256]{1,0:T(8,128)S(1)} collective-permute-done((f32[8,256]{1,0:T(8,128)S(1)}, f32[8,256]{1,0:T(8,128)S(1)}, u32[]{:S(2)}, u32[]{:S(2)}) %collective-permute-start.7) | collective-permute-done | bytes 8224 | tf_op jit(solution)/shard_map/ppermute | solution.py:430
  195.7 9.3 %pair_product.2 = bf16[4,256,2048]{2,1,0:T(8,128)(2,1)} custom-call(s32[2]{0:T(128)} %pad_add_fusion.refs_0_, bf16[2048,512]{1,0:T(8,128)(2,1)} %copy-done.1, bf16[1024,512]{1,0:T(8,128)(2,1)} %collective-permute-done.9.refs_2_, bf16[512,2048]{1,0:T(8,128)(2,1)} %weight_ref.1, bf16[512,2048]{1,0:T(8,128)(2,1)} %collective-permute-done.4.refs_4_), custom_call_target="tpu_custom_call" | custom-call | flops 1 | bytes 1 | tf_op jit(solution)/shard_map/pair_product/pallas_call | solution.py:506
  205.0 13.6 %all-gather.6.cloned.1.call-done.cot_ref = bf16[2048,2048]{1,0:T(8,128)(2,1)} async-done(((bf16[256,2048]{1,0:T(8,128)(2,1)}), bf16[2048,2048]{1,0:T(8,128)(2,1)}) %all-gather.6.cloned.1.call-update) | async-done | bytes 8388624 | tf_op jit(solution)/shard_map/all_gather | solution.py:677
  218.6 12.4 %pull_back.1 = (f32[2048,512]{1,0:T(8,128)}, f32[8,8,256]{2,1,0:T(8,128)}) custom-call(bf16[2048,2048]{1,0:T(8,128)(2,1)} %all-gather.6.cloned.1.call-done.cot_ref, bf16[512,2048]{1,0:T(8,128)(2,1)} %weight_ref.1, bf16[2048,1408]{1,0:T(8,128)(2,1)} %get-tuple-element.66.gate_ref.refs_1_, bf16[2048,512]{1,0:T(8,128)(2,1)} %get-tuple-element.68.y_ref.refs_3_, ...), custom_call_target="tpu_custom_call" | custom-call | flops 1 | bytes 1 | tf_op jit(solution)/shard_map/pull_back/pallas_call | solution.py:391
  237.7 9.4 %fusion.38 = f32[512,2048]{1,0:T(8,128)} fusion(bf16[2048,512]{1,0:T(8,128)(2,1)S(1)} %copy-done.2, bf16[2048,2048]{1,0:T(8,128)(2,1)} %all-gather.6.cloned.1.call-done.cot_ref), kind=kOutput, calls=%fused_computation.109 | convolution fusion | flops 4294967296 | bytes 14680064 | tf_op jit(solution)/shard_map/dot_general | solution.py:23
  253.1 49.6 %mixer_backward.1 = (bf16[2048,1408]{1,0:T(8,128)(2,1)}, f32[8,768]{1,0:T(8,128)}, f32[8,128]{1,0:T(8,128)}, f32[8,512]{1,0:T(8,128)}) custom-call(f32[1,8,512]{2,1,0:T(8,128)} %maximum_maximum_fusion.1.gain_ref.refs_0_, bf16[2048,1408]{1,0:T(8,128)(2,1)} %get-tuple-element.66.gate_ref.refs_1_, f32[2048,768]{1,0:T(8,128)} %get-tuple-element.67.refs_2_, ...), custom_call_target="tpu_custom_call" | custom-call | flops 1 | bytes 1 | tf_op jit(solution)/shard_map/mixer_backward/pallas_call | solution.py:332
  306.2 19.4 %fusion.37 = (bf16[2048,1408]{1,0:T(8,128)(2,1)}, f32[2048,1408]{1,0:T(8,128)}) fusion(bf16[2048,2048]{1,0:T(8,128)(2,1)} %all-gather.4.cloned.1.call-done.refs_1_, bf16[2048,1408]{1,0:T(8,128)(2,1)S(1)} %copy-done.3), kind=kOutput, calls=%fused_computation.108 | convolution fusion | flops 11814043648 | bytes 31457280 | tf_op jit(solution)/shard_map/dot_general | solution.py:23
  332.3 21.8 %pair_product.3 = (bf16[256,2048]{1,0:T(8,128)(2,1)}, bf16[256,2048]{1,0:T(8,128)(2,1)}, bf16[256,2048]{1,0:T(8,128)(2,1)}, bf16[256,2048]{1,0:T(8,128)(2,1)}) custom-call(s32[2]{0:T(128)} %pad_add_fusion.refs_0_, bf16[2048,1408]{1,0:T(8,128)(2,1)} %get-tuple-element.80.refs_1_, bf16[1024,1408]{1,0:T(8,128)(2,1)} %copy-done.8, ...), custom_call_target="tpu_custom_call" | custom-call | flops 1 | bytes 1 | tf_op jit(solution)/shard_map/pair_product/pallas_call | solution.py:506
  354.1 8.3 %collective-permute-done.14 = bf16[512,1408]{1,0:T(8,128)(2,1)S(1)} collective-permute-done((bf16[512,1408]{1,0:T(8,128)(2,1)}, bf16[512,1408]{1,0:T(8,128)(2,1)S(1)}, u32[]{:S(2)}, u32[]{:S(2)}) %collective-permute-start.14) | collective-permute-done | bytes 1441824 | tf_op jit(solution)/shard_map/ppermute | solution.py:430
  372.4 10.8 %collective-permute-done.16 = bf16[256,1408]{1,0:T(8,128)(2,1)S(1)} collective-permute-done((bf16[256,1408]{1,0:T(8,128)(2,1)}, bf16[256,1408]{1,0:T(8,128)(2,1)S(1)}, u32[]{:S(2)}, u32[]{:S(2)}) %collective-permute-start.16) | collective-permute-done | bytes 720928 | tf_op jit(solution)/shard_map/ppermute | solution.py:430
  388.4 7.0 %collective-permute-done.18 = bf16[256,2048]{1,0:T(8,128)(2,1)} collective-permute-done((bf16[256,2048]{1,0:T(8,128)(2,1)}, bf16[256,2048]{1,0:T(8,128)(2,1)}, u32[]{:S(2)}, u32[]{:S(2)}) %collective-permute-start.18) | collective-permute-done | bytes 1048608 | tf_op jit(solution)/shard_map/ppermute | solution.py:479
  403.8 6.0 %collective-permute-done.20 = f32[208,128]{1,0:T(8,128)S(1)} collective-permute-done((f32[208,128]{1,0:T(8,128)S(1)}, f32[208,128]{1,0:T(8,128)S(1)}, u32[]{:S(2)}, u32[]{:S(2)}) %collective-permute-start.20) | collective-permute-done | bytes 106528 | tf_op jit(solution)/shard_map/ppermute | solution.py:430
  410.0 7.4 %collective-permute-done.21 = f32[208,128]{1,0:T(8,128)S(1)} collective-permute-done((f32[208,128]{1,0:T(8,128)S(1)}, f32[208,128]{1,0:T(8,128)S(1)}, u32[]{:S(2)}, u32[]{:S(2)}) %collective-permute-start.21) | collective-permute-done | bytes 106528 | tf_op jit(solution)/shard_map/ppermute | solution.py:430
  418.0 61.3 %collective-permute-done.19 = bf16[256,2048]{1,0:T(8,128)(2,1)} collective-permute-done((bf16[256,2048]{1,0:T(8,128)(2,1)}, bf16[256,2048]{1,0:T(8,128)(2,1)}, u32[]{:S(2)}, u32[]{:S(2)}) %collective-permute-start.19) | collective-permute-done | bytes 1048608 | tf_op jit(solution)/shard_map/ppermute | solution.py:479
  487.6 21.0 %collective-permute-done.22 = bf16[256,2048]{1,0:T(8,128)(2,1)S(1)} collective-permute-done((bf16[256,2048]{1,0:T(8,128)(2,1)}, bf16[256,2048]{1,0:T(8,128)(2,1)S(1)}, u32[]{:S(2)}, u32[]{:S(2)}) %collective-permute-start.22) | collective-permute-done | bytes 1048608 | tf_op jit(solution)/shard_map/ppermute | solution.py:479
  526.4 9.1 %collective-permute-done.24 = f32[16,128]{1,0:T(8,128)S(1)} collective-permute-done((f32[16,128]{1,0:T(8,128)S(1)}, f32[16,128]{1,0:T(8,128)S(1)}, u32[]{:S(2)}, u32[]{:S(2)}) %collective-permute-start.24) | collective-permute-done | bytes 8224 | tf_op jit(solution)/shard_map/ppermute | solution.py:430
  566.0 12.5 %assemble.1 = f32[8512,256]{1,0:T(8,128)} custom-call(s32[1]{0:T(128)} %bitcast.38.place_ref, bf16[32,8512]{1,0:T(8,128)(2,1)} %get-tuple-element.144.refs_0_, bf16[32,8512]{1,0:T(8,128)(2,1)} %get-tuple-element.143.refs_1_, bf16[32,8512]{1,0:T(8,128)(2,1)} %collective-permute-done.28.refs_2_, bf16[32,8512]{1,0:T(8,128)(2,1)} %get-tuple-element.140.refs_3_, ...), custom_call_target="tpu_custom_call" | custom-call | flops 1 | bytes 1 | tf_op jit(solution)/shard_map/assemble/pallas_call | solution.py:559
  (238 shorter events, 155.7 us)
Async XLA Ops:
  13.4 41.5 %all-to-all-start = ((bf16[8,64,1408]{2,1,0:T(8,128)(2,1)}), bf16[8,64,1408]{2,1,0:T(8,128)(2,1)S(1)}, u32[]{:S(2)}, u32[]{:S(2)}) async-start(bf16[8,64,1408]{2,1,0:T(8,128)(2,1)} %fusion.20), calls=%async_computation | async-start | bytes 2883584 | tf_op jit(solution)/shard_map/all_to_all | solution.py:611
  19.8 116.2 %all-gather.4.cloned.1.call-start = ((), (), s32[]{:S(2)}) async-start(), calls=%async_computation.4 | async-start | bytes 9437184 | tf_op jit(solution)/shard_map/all_gather | solution.py:636
  54.9 163.8 %all-gather.6.cloned.1.call-start = ((), (), s32[]{:S(2)}) async-start(), calls=%async_computation.5 | async-start | bytes 9437184 | tf_op jit(solution)/shard_map/all_gather | solution.py:677
  55.6 247.0 %reduce-scatter.2.cloned.1.call-start = ((), (), s32[]{:S(2)}) async-start(), calls=%async_computation.6 | async-start | bytes 5242880 | tf_op jit(solution)/shard_map/reduce_scatter | solution.py:712
  56.0 17.7 %collective-permute-start.1 = (bf16[256,1408]{1,0:T(8,128)(2,1)S(1)}, bf16[256,1408]{1,0:T(8,128)(2,1)S(1)}, u32[]{:S(2)}, u32[]{:S(2)}) collective-permute-start(bf16[256,1408]{1,0:T(8,128)(2,1)S(1)} %bitcast.89), channel_id=1, source_target_pairs={{0,16},{8,24},{16,0},{24,8},{1,17},{9,25},{17,1},{25,9},{2,18},{10... | collective-permute-start | bytes 2162696 | tf_op jit(solution)/shard_map/ppermute | solution.py:430
  57.5 17.8 %collective-permute-start = (bf16[256,1408]{1,0:T(8,128)(2,1)S(1)}, bf16[256,1408]{1,0:T(8,128)(2,1)S(1)}, u32[]{:S(2)}, u32[]{:S(2)}) collective-permute-start(bf16[256,1408]{1,0:T(8,128)(2,1)S(1)} %bitcast.92), channel_id=1, source_target_pairs={{0,8},{8,0},{16,24},{24,16},{1,9},{9,1},{17,25},{25,17},{2,10},{10... | collective-permute-start | bytes 2162696 | tf_op jit(solution)/shard_map/ppermute | solution.py:430
  73.8 32.4 %collective-permute-start.2 = (bf16[512,1408]{1,0:T(8,128)(2,1)S(1)}, bf16[512,1408]{1,0:T(8,128)(2,1)S(1)}, u32[]{:S(2)}, u32[]{:S(2)}) collective-permute-start(bf16[512,1408]{1,0:T(8,128)(2,1)S(1)} %pad_maximum_fusion.2), channel_id=1, source_target_pairs={{0,8},{8,0},{16,24},{24,16},{1,9},{9,1},{17,25},{25,17},{2,10},{10... | collective-permute-start | bytes 4325384 | tf_op jit(solution)/shard_map/ppermute | solution.py:430
  75.5 32.1 %collective-permute-start.3 = (bf16[512,1408]{1,0:T(8,128)(2,1)S(1)}, bf16[512,1408]{1,0:T(8,128)(2,1)S(1)}, u32[]{:S(2)}, u32[]{:S(2)}) collective-permute-start(bf16[512,1408]{1,0:T(8,128)(2,1)S(1)} %pad_maximum_fusion.3), channel_id=1, source_target_pairs={{0,16},{8,24},{16,0},{24,8},{1,17},{9,25},{17,1},{25,9},{2,18},{10... | collective-permute-start | bytes 4325384 | tf_op jit(solution)/shard_map/ppermute | solution.py:430
  247.9 106.2 %all-to-all-start.1 = ((bf16[4,256,2048]{2,1,0:T(8,128)(2,1)}), bf16[4,256,2048]{2,1,0:T(8,128)(2,1)}, u32[]{:S(2)}, u32[]{:S(2)}) async-start(bf16[4,256,2048]{2,1,0:T(8,128)(2,1)} %pair_product.2), calls=%async_computation.2 | async-start | bytes 8388608 | tf_op jit(solution)/shard_map/all_to_all | solution.py:484
  252.8 226.5 %all-gather.8.cloned.1.call-start = ((), (), s32[]{:S(2)}) async-start(), calls=%async_computation.7 | async-start | bytes 5242880 | tf_op jit(solution)/shard_map/all_gather | solution.py:743
  304.9 24.5 %collective-permute-start.13 = (bf16[1024,1408]{1,0:T(8,128)(2,1)S(1)}, bf16[1024,1408]{1,0:T(8,128)(2,1)S(1)}, u32[]{:S(2)}, u32[]{:S(2)}) collective-permute-start(bf16[1024,1408]{1,0:T(8,128)(2,1)S(1)} %bitcast.99), channel_id=1, source_target_pairs={{0,1},{1,0},{2,3},{3,2},{4,5},{5,4},{6,7},{7,6},{8,9},{9,8},{10,11... | collective-permute-start | bytes 8650760 | tf_op jit(solution)/shard_map/ppermute | solution.py:430
  329.4 33.0 %collective-permute-start.14 = (bf16[512,1408]{1,0:T(8,128)(2,1)}, bf16[512,1408]{1,0:T(8,128)(2,1)S(1)}, u32[]{:S(2)}, u32[]{:S(2)}) collective-permute-start(bf16[512,1408]{1,0:T(8,128)(2,1)} %get-tuple-element.81), channel_id=1, source_target_pairs={{0,8},{8,0},{16,24},{24,16},{1,9},{9,1},{17,25},{25,17},{2,10},{10... | collective-permute-start | bytes 4325384 | tf_op jit(solution)/shard_map/ppermute | solution.py:430
  330.8 32.8 %collective-permute-start.15 = (bf16[512,1408]{1,0:T(8,128)(2,1)}, bf16[512,1408]{1,0:T(8,128)(2,1)}, u32[]{:S(2)}, u32[]{:S(2)}) collective-permute-start(bf16[512,1408]{1,0:T(8,128)(2,1)} %get-tuple-element.82), channel_id=1, source_target_pairs={{0,16},{8,24},{16,0},{24,8},{1,17},{9,25},{17,1},{25,9},{2,18},{10... | collective-permute-start | bytes 4325384 | tf_op jit(solution)/shard_map/ppermute | solution.py:430
  366.9 16.3 %collective-permute-start.16 = (bf16[256,1408]{1,0:T(8,128)(2,1)}, bf16[256,1408]{1,0:T(8,128)(2,1)S(1)}, u32[]{:S(2)}, u32[]{:S(2)}) collective-permute-start(bf16[256,1408]{1,0:T(8,128)(2,1)} %get-tuple-element.93), channel_id=1, source_target_pairs={{0,16},{8,24},{16,0},{24,8},{1,17},{9,25},{17,1},{25,9},{2,18},{10... | collective-permute-start | bytes 2162696 | tf_op jit(solution)/shard_map/ppermute | solution.py:430
  368.4 16.1 %collective-permute-start.17 = (bf16[256,1408]{1,0:T(8,128)(2,1)}, bf16[256,1408]{1,0:T(8,128)(2,1)}, u32[]{:S(2)}, u32[]{:S(2)}) collective-permute-start(bf16[256,1408]{1,0:T(8,128)(2,1)} %get-tuple-element.94), channel_id=1, source_target_pairs={{0,8},{8,0},{16,24},{24,16},{1,9},{9,1},{17,25},{25,17},{2,10},{10... | collective-permute-start | bytes 2162696 | tf_op jit(solution)/shard_map/ppermute | solution.py:430
  370.3 25.0 %collective-permute-start.18 = (bf16[256,2048]{1,0:T(8,128)(2,1)}, bf16[256,2048]{1,0:T(8,128)(2,1)}, u32[]{:S(2)}, u32[]{:S(2)}) collective-permute-start(bf16[256,2048]{1,0:T(8,128)(2,1)} %get-tuple-element.96), channel_id=1, source_target_pairs={{0,2},{1,3},{2,4},{3,5},{4,6},{5,7},{6,0},{7,1},{8,10},{9,11},{10,... | collective-permute-start | bytes 3145736 | tf_op jit(solution)/shard_map/ppermute | solution.py:479
  395.4 84.0 %all-to-all-start.2 = ((bf16[8,64,1408]{2,1,0:T(8,128)(2,1)}), bf16[8,64,1408]{2,1,0:T(8,128)(2,1)S(1)}, u32[]{:S(2)}, u32[]{:S(2)}) async-start(bf16[8,64,1408]{2,1,0:T(8,128)(2,1)} %bitcast.95), calls=%async_computation.3 | async-start | bytes 2883584 | tf_op jit(solution)/shard_map/all_to_all | solution.py:709
  399.4 80.0 %collective-permute-start.19 = (bf16[256,2048]{1,0:T(8,128)(2,1)}, bf16[256,2048]{1,0:T(8,128)(2,1)}, u32[]{:S(2)}, u32[]{:S(2)}) collective-permute-start(bf16[256,2048]{1,0:T(8,128)(2,1)} %get-tuple-element.104), channel_id=1, source_target_pairs={{0,4},{1,5},{2,6},{3,7},{4,0},{5,1},{6,2},{7,3},{8,12},{9,13},{10,... | collective-permute-start | bytes 3145736 | tf_op jit(solution)/shard_map/ppermute | solution.py:479
  483.7 25.0 %collective-permute-start.22 = (bf16[256,2048]{1,0:T(8,128)(2,1)}, bf16[256,2048]{1,0:T(8,128)(2,1)S(1)}, u32[]{:S(2)}, u32[]{:S(2)}) collective-permute-start(bf16[256,2048]{1,0:T(8,128)(2,1)} %get-tuple-element.111), channel_id=1, source_target_pairs={{0,6},{1,7},{2,0},{3,1},{4,2},{5,3},{6,4},{7,5},{8,14},{9,15},{10,... | collective-permute-start | bytes 3145736 | tf_op jit(solution)/shard_map/ppermute | solution.py:479
  486.2 36.5 %collective-permute-start.28 = (bf16[32,8512]{1,0:T(8,128)(2,1)}, bf16[32,8512]{1,0:T(8,128)(2,1)}, u32[]{:S(2)}, u32[]{:S(2)}) collective-permute-start(bf16[32,8512]{1,0:T(8,128)(2,1)} %get-tuple-element.144.refs_0_), channel_id=1, source_target_pairs={{0,8},{8,0},{16,24},{24,16},{1,9},{9,1},{17,25},{25,17},{2,10},{10... | collective-permute-start | bytes 1634312 | tf_op jit(solution)/shard_map/ppermute | solution.py:430
  519.9 15.7 %collective-permute-start.29 = (bf16[32,8512]{1,0:T(8,128)(2,1)S(1)}, bf16[32,8512]{1,0:T(8,128)(2,1)S(1)}, u32[]{:S(2)}, u32[]{:S(2)}) collective-permute-start(bf16[32,8512]{1,0:T(8,128)(2,1)S(1)} %copy-done.5), channel_id=1, source_target_pairs={{0,16},{8,24},{16,0},{24,8},{1,17},{9,25},{17,1},{25,9},{2,18},{10... | collective-permute-start | bytes 1634312 | tf_op jit(solution)/shard_map/ppermute | solution.py:430
  522.1 13.4 %collective-permute-start.24 = (f32[16,128]{1,0:T(8,128)S(1)}, f32[16,128]{1,0:T(8,128)S(1)}, u32[]{:S(2)}, u32[]{:S(2)}) collective-permute-start(f32[16,128]{1,0:T(8,128)S(1)} %bitcast_add_fusion), channel_id=1, source_target_pairs={{0,16},{8,24},{16,0},{24,8},{1,17},{9,25},{17,1},{25,9},{2,18},{10... | collective-permute-start | bytes 24584 | tf_op jit(solution)/shard_map/ppermute | solution.py:430
  524.9 31.6 %collective-permute-start.31 = (bf16[64,8512]{1,0:T(8,128)(2,1)}, bf16[64,8512]{1,0:T(8,128)(2,1)}, u32[]{:S(2)}, u32[]{:S(2)}) collective-permute-start(bf16[64,8512]{1,0:T(8,128)(2,1)} %pad_maximum_fusion.8), channel_id=1, source_target_pairs={{0,16},{8,24},{16,0},{24,8},{1,17},{9,25},{17,1},{25,9},{2,18},{10... | collective-permute-start | bytes 3268616 | tf_op jit(solution)/shard_map/ppermute | solution.py:430
  536.7 26.9 %collective-permute-start.30 = (bf16[64,8512]{1,0:T(8,128)(2,1)}, bf16[64,8512]{1,0:T(8,128)(2,1)}, u32[]{:S(2)}, u32[]{:S(2)}) collective-permute-start(bf16[64,8512]{1,0:T(8,128)(2,1)} %pad_maximum_fusion.7), channel_id=1, source_target_pairs={{0,8},{8,0},{16,24},{24,16},{1,9},{9,1},{17,25},{25,17},{2,10},{10... | collective-permute-start | bytes 3268616 | tf_op jit(solution)/shard_map/ppermute | solution.py:430
  (37 other events, 263.8 us)
Sparse Core Ops, SparseCore 0:
  55.0 80.9 all-gather.3
  137.6 80.9 all-gather.5
  248.0 52.3 reduce-scatter.1
  395.5 53.3 all-gather.7

commit v3 on v2

--- a/solution.py
+++ b/solution.py
@@ -464,10 +464,15 @@
     return jnp.concatenate([piece + other.astype(F32) for piece, other in zip(mine, far_got)], axis=0)
 
 
-def dp_gather(own):
+def gather_near(own):
     rows = own.shape[0] // 2
     upper, lower = own[:rows], own[rows:]
-    upper1, lower2 = swap(upper, "dp", 1), swap(lower, "dp", 2)
+    return upper, lower, swap(upper, "dp", 1), swap(lower, "dp", 2)
+
+
+def gather_far(first):
+    upper, lower, upper1, lower2 = first
+    rows = upper.shape[0]
     uppers = swap(jnp.concatenate([upper, upper1], axis=0), "dp", 2)
     lowers = swap(jnp.concatenate([lower, lower2], axis=0), "dp", 1)
     return [(upper, lower), (upper1, lowers[:rows]), (uppers[:rows], lower2), (uppers[rows:], lowers[rows:])]
@@ -632,7 +637,7 @@
     normed = inputs_f * rms_scale
     hidden_own = reorder((normed * norm_gain[None, :]).astype(BF16))
     hidden_own, got = lax.optimization_barrier((hidden_own, got))
-    weight = jnp.concatenate(sum(dp_gather(got.reshape(mp * part, columns)), ()), axis=0)
+    weight = jnp.concatenate(sum(gather_far(gather_near(got.reshape(mp * part, columns))), ()), axis=0)
     hidden = lax.all_gather(hidden_own, "mp", axis=0, tiled=True)
 
     first_chan, first_head = mp_place * own, mp_place * own_heads
@@ -710,9 +715,19 @@
 
     token_rows, out_part = lax.optimization_barrier((token_rows, out_part))
     out_mine = lax.psum_scatter(out_part, "dp", scatter_dimension=0, tiled=True)
+    def rows_of(blocks):
+        flat = lambda first, size: blocks[:, :, first : first + size].transpose(1, 0, 2).reshape(part, -1)
+        shared = jnp.sum(blocks[:, :, width : width + 2 * state_dim].astype(F32), axis=0).astype(BF16)
+        return jnp.concatenate(
+            [flat(0, own), flat(width + 2 * state_dim, own), shared, flat(width + joint, own_heads)], axis=1
+        )
+
     d_proj, conv_grads, head_grads, gain_grads = mixer_backward(
         gains, projected, pre, y_all, d_normed, token_rows, states, taps, head_params, skip, state_dim
     )
+    d_proj, out_mine = lax.optimization_barrier((d_proj, out_mine))
+    out_weight_grad = lax.all_gather(out_mine, "dp", axis=0, tiled=True)
+
     def place_in(array, first, size):
         return lax.dynamic_update_slice_in_dim(
             jnp.zeros(array.shape[:-1] + (size,), F32), array, first, array.ndim - 1
@@ -729,33 +744,33 @@
     packed = jnp.pad(packed, (0, count - packed.shape[0])).reshape(-1, LANES)
 
     if line:
-        d_proj, out_mine = lax.optimization_barrier((d_proj, out_mine))
         theirs = swap(for_sibling(d_proj, tokens), "mp", 1)
+        d_shares = pair_product(d_proj, theirs, weight, sibling_weight, NT, depth, tokens, False)
+        d_shares, d_proj, sent = lax.optimization_barrier((d_shares, d_proj, sent))
+        reaches = [1] + list(range(mp // 2 - 1, 1, -1))
+        d_blocks = [d_shares[0], line_permute(d_shares[1], 1)]
         share = mm(hidden, d_proj, TN)
         near_cut = reduce_cut(share, in_block, BF16)
-        near_cut, theirs = lax.optimization_barrier((near_cut, theirs))
+        near_cut, d_blocks, out_weight_grad = lax.optimization_barrier((near_cut, d_blocks, out_weight_grad))
         near_got = reduce_near(near_cut)
-        d_shares = pair_product(d_proj, theirs, weight, sibling_weight, NT, depth, tokens, False)
-        near_got, d_shares, sent = lax.optimization_barrier((near_got, d_shares, sent))
-        d_blocks = [d_shares[0], line_permute(d_shares[1], 1)]
+        d_blocks += [line_permute(d_shares[reach], reach) for reach in reaches[1:2]]
+        near_got, d_blocks = lax.optimization_barrier((near_got, d_blocks))
         mine = reduce_far(share, in_block, near_got)
-        mine, d_blocks, out_mine, packed = lax.optimization_barrier((mine, d_blocks, out_mine, packed))
-        out_weight_grad = lax.all_gather(out_mine, "dp", axis=0, tiled=True)
+        mine, packed = lax.optimization_barrier((mine, packed))
         blocks = to_rows(mine)
-        d_blocks += [line_permute(d_shares[reach], reach) for reach in range(2, min(3, mp // 2))]
-        blocks, d_blocks, d_shares, packed, out_weight_grad = lax.optimization_barrier(
-            (blocks, d_blocks, d_shares, all_sum(packed, "dp"), out_weight_grad)
-        )
-        d_blocks += [line_permute(d_shares[reach], reach) for reach in range(3, mp // 2)]
+        blocks, d_shares, packed = lax.optimization_barrier((blocks, d_shares, all_sum(packed, "dp")))
+        d_blocks += [line_permute(d_shares[reach], reach) for reach in reaches[2:]]
+        gathered = gather_far(gather_near(rows_of(blocks)))
+        in_weight_grad, d_blocks = lax.optimization_barrier((assemble(gathered), d_blocks))
         d_hidden = total(d_blocks)
     else:
         packed = all_sum(packed, "dp")
-        out_weight_grad = lax.all_gather(out_mine, "dp", axis=0, tiled=True)
         share = mm(hidden, d_proj, TN)
         d_proj, share = lax.optimization_barrier((d_proj, share))
         blocks = to_rows(reduce_far(share, in_block, reduce_near(reduce_cut(share, in_block, BF16))))
         d_shares = mm(d_proj, weight, NT).astype(BF16)
         d_hidden = lax.psum_scatter(d_shares, "mp", scatter_dimension=0, tiled=True).astype(F32)
+        in_weight_grad = in_place_order(gather_far(gather_near(rows_of(blocks))))
     outputs = (inputs_f + total(sent)).astype(BF16)
     d_hidden = restore(d_hidden)
     norm_gain_grad = jnp.sum(d_hidden * normed, axis=0)
@@ -770,14 +785,6 @@
     d_normed_in = d_hidden * norm_gain[None, :]
     input_back = rms_scale * (d_normed_in - normed * jnp.mean(d_normed_in * normed, axis=-1, keepdims=True))
     input_grad = (cotangent.astype(F32) + input_back).astype(BF16)
-
-    flat = lambda first, size: blocks[:, :, first : first + size].transpose(1, 0, 2).reshape(part, -1)
-    shared = jnp.sum(blocks[:, :, width : width + 2 * state_dim].astype(F32), axis=0).astype(BF16)
-    grad_rows = jnp.concatenate(
-        [flat(0, own), flat(width + 2 * state_dim, own), shared, flat(width + joint, own_heads)], axis=1
-    )
-    gathered = dp_gather(grad_rows)
-    in_weight_grad = assemble(gathered) if line else in_place_order(gathered)
 
     return (
         outputs,

time: 598 us -> 585 us (0.978)
  starting transfers between devices: 45.7 us -> 38.9 us
    ppermute x3, waiting for transfers between devices: 89.3 us -> 35.6 us  [line_permute(): return lax.ppermute(block, 'mp', pairs)]
    all_to_all x1, waiting for transfers between devices: 0.01 us -> 24.1 us  [to_rows(): lax.all_to_all(mine.astype(BF16).reshape(mp, part, -1), 'mp', split_axis=...]
    ppermute x29, waiting for transfers between devices: 127 us -> 150 us  [swap(): lax.ppermute(value, axis, [(place, place ^ bit) for place in range(size)])]
    all_to_all x1, waiting for transfers between devices: 0.01 us -> 10.5 us  [line_send(): lax.all_to_all(shares, 'mp', split_axis=0, concat_axis=0, axis_index_grou...]
    ppermute x3, starting transfers between devices: 6.31 us -> 0.2 us  [line_permute(): return lax.ppermute(block, 'mp', pairs)]
  transfers between devices with their start and end apart: 39 -> 39, of which waited for: 29 -> 33; matrix products, arithmetic and copies ran while one was open for 16% -> 12% of each run, Pallas kernels for 20% -> 23%
where the time goes in v3:
time: 585 us; the launch traced here: 579 us
  waiting for transfers between devices  271 us (46%)
  Pallas kernels  145 us (25%)
  local copies, waits for them, and re-layouts  49.2 us (8%)
  starting transfers between devices  38.9 us (7%)
  other arithmetic  31.1 us (5%)
  matrix products  28.3 us (5%)
  between operations  15.3 us (3%)
    ppermute x29, waiting for transfers between devices, swap(): lax.ppermute(value, axis, [(place, place ^ bit) for place in range(size)])  150 us
    pallas_call x1, Pallas kernels, mixer_backward(): pl.pallas_call(lambda *refs: backward_kernel(*refs, state_dim=state_dim,...  49.6 us
    pallas_call x1, Pallas kernels, mixer_forward(): pl.pallas_call(lambda *refs: forward_kernel(*refs, state_dim=state_dim, w...  39.1 us
    ppermute x3, waiting for transfers between devices, line_permute(): return lax.ppermute(block, 'mp', pairs)  35.6 us
    pallas_call x2, Pallas kernels, pair_product(): pl.pallas_call(lambda *refs: pair_kernel(*refs, dims=dims), grid_spec=plt...  32.2 us
    dot_general x2, matrix products, mm(): return lax.dot_general(left, right, dims, preferred_element_type=F32)  28.3 us
    all_to_all x1, waiting for transfers between devices, on_device(): got = lax.all_to_all(send, 'mp', split_axis=0, concat_axis=0, tiled=True)  25.4 us
    all_to_all x1, waiting for transfers between devices, to_rows(): lax.all_to_all(mine.astype(BF16).reshape(mp, part, -1), 'mp', split_axis=...  24.1 us
  transfers between devices with their start and end apart: 39, of which 33 were waited for; matrix products, arithmetic and copies ran while one was open for 12% of the time, Pallas kernels for 23%

profile of v3, /device:TPU:0, one launch (start us, length us, event | category | flops | bytes accessed | tf_op | source)
XLA Modules:
  0.0 579.1 jit_solution(16503507613371508909)
XLA Ops:
  13.4 6.5 %all-to-all-start = ((bf16[8,64,1408]{2,1,0:T(8,128)(2,1)}), bf16[8,64,1408]{2,1,0:T(8,128)(2,1)S(1)}, u32[]{:S(2)}, u32[]{:S(2)}) async-start(bf16[8,64,1408]{2,1,0:T(8,128)(2,1)} %fusion.20), calls=%async_computation | async-start | bytes 2883584 | tf_op jit(solution)/shard_map/all_to_all | solution.py:616
  29.5 25.4 %all-to-all-done = bf16[8,64,1408]{2,1,0:T(8,128)(2,1)S(1)} async-done(((bf16[8,64,1408]{2,1,0:T(8,128)(2,1)}), bf16[8,64,1408]{2,1,0:T(8,128)(2,1)S(1)}, u32[]{:S(2)}, u32[]{:S(2)}) %all-to-all-start) | async-done | bytes 1441824 | tf_op jit(solution)/shard_map/all_to_all | solution.py:616
  59.4 14.7 %collective-permute-done.1 = bf16[256,1408]{1,0:T(8,128)(2,1)S(1)} collective-permute-done((bf16[256,1408]{1,0:T(8,128)(2,1)S(1)}, bf16[256,1408]{1,0:T(8,128)(2,1)S(1)}, u32[]{:S(2)}, u32[]{:S(2)}) %collective-permute-start.1) | collective-permute-done | bytes 720928 | tf_op jit(solution)/shard_map/ppermute | solution.py:430
  80.2 26.4 %collective-permute-done.2 = bf16[512,1408]{1,0:T(8,128)(2,1)S(1)} collective-permute-done((bf16[512,1408]{1,0:T(8,128)(2,1)S(1)}, bf16[512,1408]{1,0:T(8,128)(2,1)S(1)}, u32[]{:S(2)}, u32[]{:S(2)}) %collective-permute-start.2) | collective-permute-done | bytes 1441824 | tf_op jit(solution)/shard_map/ppermute | solution.py:430
  115.9 8.5 %collective-permute-done.4.refs_4_ = bf16[512,2048]{1,0:T(8,128)(2,1)} collective-permute-done((bf16[512,2048]{1,0:T(8,128)(2,1)S(1)}, bf16[512,2048]{1,0:T(8,128)(2,1)}, u32[]{:S(2)}, u32[]{:S(2)}) %collective-permute-start.4) | collective-permute-done | bytes 2097184 | tf_op jit(solution)/shard_map/ppermute | solution.py:430
  125.0 11.0 %all-gather.4.cloned.1.call-done.refs_1_ = bf16[2048,2048]{1,0:T(8,128)(2,1)} async-done(((bf16[256,2048]{1,0:T(8,128)(2,1)}), bf16[2048,2048]{1,0:T(8,128)(2,1)}) %all-gather.4.cloned.1.call-update) | async-done | bytes 8388624 | tf_op jit(solution)/shard_map/all_gather | solution.py:641
  136.0 39.1 %mixer_forward.1 = (bf16[2048,1408]{1,0:T(8,128)(2,1)}, bf16[2048,512]{1,0:T(8,128)(2,1)}, f32[8,128,512]{2,1,0:T(8,128)}, f32[8,8,256]{2,1,0:T(8,128)}, f32[2048,768]{1,0:T(8,128)}) custom-call(f32[1,1,512]{2,1,0:T(1,128)} %broadcast_in_dim.53.refs_0_, bf16[2048,2048]{1,0:T(8,128)(2,1)} %all-gather.4.cloned.1.call-done.refs_1_, ...), custom_call_target="tpu_custom_call" | custom-call | flops 1 | bytes 1 | tf_op jit(solution)/shard_map/mixer_forward/pallas_call | solution.py:286
  177.3 6.2 %collective-permute-done.7 = f32[8,256]{1,0:T(8,128)S(1)} collective-permute-done((f32[8,256]{1,0:T(8,128)S(1)}, f32[8,256]{1,0:T(8,128)S(1)}, u32[]{:S(2)}, u32[]{:S(2)}) %collective-permute-start.7) | collective-permute-done | bytes 8224 | tf_op jit(solution)/shard_map/ppermute | solution.py:430
  195.7 9.4 %pair_product.2 = bf16[4,256,2048]{2,1,0:T(8,128)(2,1)} custom-call(s32[2]{0:T(128)} %pad_add_fusion.refs_0_, bf16[2048,512]{1,0:T(8,128)(2,1)} %copy-done.1, bf16[1024,512]{1,0:T(8,128)(2,1)} %collective-permute-done.9.refs_2_, bf16[512,2048]{1,0:T(8,128)(2,1)} %weight_ref.1, bf16[512,2048]{1,0:T(8,128)(2,1)} %collective-permute-done.4.refs_4_), custom_call_target="tpu_custom_call" | custom-call | flops 1 | bytes 1 | tf_op jit(solution)/shard_map/pair_product/pallas_call | solution.py:511
  205.1 13.6 %all-gather.6.cloned.1.call-done.cot_ref = bf16[2048,2048]{1,0:T(8,128)(2,1)} async-done(((bf16[256,2048]{1,0:T(8,128)(2,1)}), bf16[2048,2048]{1,0:T(8,128)(2,1)}) %all-gather.6.cloned.1.call-update) | async-done | bytes 8388624 | tf_op jit(solution)/shard_map/all_gather | solution.py:682
  218.6 12.4 %pull_back.1 = (f32[2048,512]{1,0:T(8,128)}, f32[8,8,256]{2,1,0:T(8,128)}) custom-call(bf16[2048,2048]{1,0:T(8,128)(2,1)} %all-gather.6.cloned.1.call-done.cot_ref, bf16[512,2048]{1,0:T(8,128)(2,1)} %weight_ref.1, bf16[2048,1408]{1,0:T(8,128)(2,1)} %get-tuple-element.70.gate_ref.refs_1_, bf16[2048,512]{1,0:T(8,128)(2,1)} %get-tuple-element.72.y_ref.refs_3_, ...), custom_call_target="tpu_custom_call" | custom-call | flops 1 | bytes 1 | tf_op jit(solution)/shard_map/pull_back/pallas_call | solution.py:391
  237.7 9.5 %fusion.38 = f32[512,2048]{1,0:T(8,128)} fusion(bf16[2048,512]{1,0:T(8,128)(2,1)S(1)} %copy-done.2, bf16[2048,2048]{1,0:T(8,128)(2,1)} %all-gather.6.cloned.1.call-done.cot_ref), kind=kOutput, calls=%fused_computation.109 | convolution fusion | flops 4294967296 | bytes 14680064 | tf_op jit(solution)/shard_map/dot_general | solution.py:23
  253.0 49.6 %mixer_backward.1 = (bf16[2048,1408]{1,0:T(8,128)(2,1)}, f32[8,768]{1,0:T(8,128)}, f32[8,128]{1,0:T(8,128)}, f32[8,512]{1,0:T(8,128)}) custom-call(f32[1,8,512]{2,1,0:T(8,128)} %maximum_maximum_fusion.1.gain_ref.refs_0_, bf16[2048,1408]{1,0:T(8,128)(2,1)} %get-tuple-element.70.gate_ref.refs_1_, f32[2048,768]{1,0:T(8,128)} %get-tuple-element.71.refs_2_, ...), custom_call_target="tpu_custom_call" | custom-call | flops 1 | bytes 1 | tf_op jit(solution)/shard_map/mixer_backward/pallas_call | solution.py:332
  311.9 22.8 %pair_product.3 = (bf16[256,2048]{1,0:T(8,128)(2,1)}, bf16[256,2048]{1,0:T(8,128)(2,1)}, bf16[256,2048]{1,0:T(8,128)(2,1)}, bf16[256,2048]{1,0:T(8,128)(2,1)}) custom-call(s32[2]{0:T(128)} %pad_add_fusion.refs_0_, bf16[2048,1408]{1,0:T(8,128)(2,1)} %get-tuple-element.92.refs_1_, bf16[1024,1408]{1,0:T(8,128)(2,1)} %collective-permute-done.13.refs_2_, ...), custom_call_target="tpu_custom_call" | custom-call | flops 1 | bytes 1 | tf_op jit(solution)/shard_map/pair_product/pallas_call | solution.py:511
  334.7 10.5 %all-to-all-done.1 = bf16[4,256,2048]{2,1,0:T(8,128)(2,1)} async-done(((bf16[4,256,2048]{2,1,0:T(8,128)(2,1)}), bf16[4,256,2048]{2,1,0:T(8,128)(2,1)}, u32[]{:S(2)}, u32[]{:S(2)}) %all-to-all-start.1) | async-done | bytes 4194336 | tf_op jit(solution)/shard_map/all_to_all | solution.py:489
  345.5 18.8 %fusion.37 = (bf16[2048,1408]{1,0:T(8,128)(2,1)S(1)}, f32[2048,1408]{1,0:T(8,128)}) fusion(bf16[2048,2048]{1,0:T(8,128)(2,1)} %all-gather.4.cloned.1.call-done.refs_1_, bf16[2048,1408]{1,0:T(8,128)(2,1)} %get-tuple-element.92.refs_1_), kind=kOutput, calls=%fused_computation.108 | convolution fusion | flops 11814043648 | bytes 31457280 | tf_op jit(solution)/shard_map/dot_general | solution.py:23
  375.4 21.9 %collective-permute-done.17 = bf16[256,2048]{1,0:T(8,128)(2,1)S(1)} collective-permute-done((bf16[256,2048]{1,0:T(8,128)(2,1)S(1)}, bf16[256,2048]{1,0:T(8,128)(2,1)S(1)}, u32[]{:S(2)}, u32[]{:S(2)}) %collective-permute-start.17) | collective-permute-done | bytes 1048608 | tf_op jit(solution)/shard_map/ppermute | solution.py:484
  397.3 6.3 %collective-permute-done.15 = bf16[512,1408]{1,0:T(8,128)(2,1)S(1)} collective-permute-done((bf16[512,1408]{1,0:T(8,128)(2,1)}, bf16[512,1408]{1,0:T(8,128)(2,1)S(1)}, u32[]{:S(2)}, u32[]{:S(2)}) %collective-permute-start.15) | collective-permute-done | bytes 1441824 | tf_op jit(solution)/shard_map/ppermute | solution.py:430
  411.9 11.6 %collective-permute-done.18 = bf16[256,1408]{1,0:T(8,128)(2,1)S(1)} collective-permute-done((bf16[256,1408]{1,0:T(8,128)(2,1)}, bf16[256,1408]{1,0:T(8,128)(2,1)S(1)}, u32[]{:S(2)}, u32[]{:S(2)}) %collective-permute-start.18) | collective-permute-done | bytes 720928 | tf_op jit(solution)/shard_map/ppermute | solution.py:430
  442.7 24.1 %all-to-all-done.2 = bf16[8,64,1408]{2,1,0:T(8,128)(2,1)S(1)} async-done(((bf16[8,64,1408]{2,1,0:T(8,128)(2,1)}), bf16[8,64,1408]{2,1,0:T(8,128)(2,1)S(1)}, u32[]{:S(2)}, u32[]{:S(2)}) %all-to-all-start.2) | async-done | bytes 1441824 | tf_op jit(solution)/shard_map/all_to_all | solution.py:714
  473.3 12.1 %collective-permute-done.22.refs_2_ = bf16[32,8512]{1,0:T(8,128)(2,1)S(1)} collective-permute-done((bf16[32,8512]{1,0:T(8,128)(2,1)S(1)}, bf16[32,8512]{1,0:T(8,128)(2,1)S(1)}, u32[]{:S(2)}, u32[]{:S(2)}) %collective-permute-start.22) | collective-permute-done | bytes 544800 | tf_op jit(solution)/shard_map/ppermute | solution.py:430
  487.7 22.8 %collective-permute-done.25 = bf16[64,8512]{1,0:T(8,128)(2,1)S(1)} collective-permute-done((bf16[64,8512]{1,0:T(8,128)(2,1)S(1)}, bf16[64,8512]{1,0:T(8,128)(2,1)S(1)}, u32[]{:S(2)}, u32[]{:S(2)}) %collective-permute-start.25) | collective-permute-done | bytes 1089568 | tf_op jit(solution)/shard_map/ppermute | solution.py:430
  512.7 12.1 %assemble.1 = f32[8512,256]{1,0:T(8,128)} custom-call(s32[1]{0:T(128)} %bitcast.27.place_ref, bf16[32,8512]{1,0:T(8,128)(2,1)} %copy-done.5, bf16[32,8512]{1,0:T(8,128)(2,1)} %copy-done.4, bf16[32,8512]{1,0:T(8,128)(2,1)} %copy-done.7, bf16[32,8512]{1,0:T(8,128)(2,1)} %get-tuple-element.148.refs_3_, bf16[32,8512]{1,0:T(8,128)(2,1)} %get-tuple-element.150.refs_4_, ...), custom_call_target="tpu_custom_call" | custom-call | flops 1 | bytes 1 | tf_op jit(solution)/shard_map/assemble/pallas_call | solution.py:564
  524.8 8.3 %collective-permute-done.26 = bf16[256,2048]{1,0:T(8,128)(2,1)S(1)} collective-permute-done((bf16[256,2048]{1,0:T(8,128)(2,1)S(1)}, bf16[256,2048]{1,0:T(8,128)(2,1)S(1)}, u32[]{:S(2)}, u32[]{:S(2)}) %collective-permute-start.26) | collective-permute-done | bytes 1048608 | tf_op jit(solution)/shard_map/ppermute | solution.py:484
  (246 shorter events, 160.4 us)
Async XLA Ops:
  13.4 41.5 %all-to-all-start = ((bf16[8,64,1408]{2,1,0:T(8,128)(2,1)}), bf16[8,64,1408]{2,1,0:T(8,128)(2,1)S(1)}, u32[]{:S(2)}, u32[]{:S(2)}) async-start(bf16[8,64,1408]{2,1,0:T(8,128)(2,1)} %fusion.20), calls=%async_computation | async-start | bytes 2883584 | tf_op jit(solution)/shard_map/all_to_all | solution.py:616
  19.8 116.2 %all-gather.4.cloned.1.call-start = ((), (), s32[]{:S(2)}) async-start(), calls=%async_computation.4 | async-start | bytes 9437184 | tf_op jit(solution)/shard_map/all_gather | solution.py:641
  54.9 163.8 %all-gather.6.cloned.1.call-start = ((), (), s32[]{:S(2)}) async-start(), calls=%async_computation.5 | async-start | bytes 9437184 | tf_op jit(solution)/shard_map/all_gather | solution.py:682
  55.6 247.1 %reduce-scatter.2.cloned.1.call-start = ((), (), s32[]{:S(2)}) async-start(), calls=%async_computation.6 | async-start | bytes 5242880 | tf_op jit(solution)/shard_map/reduce_scatter | solution.py:717
  56.3 17.7 %collective-permute-start.1 = (bf16[256,1408]{1,0:T(8,128)(2,1)S(1)}, bf16[256,1408]{1,0:T(8,128)(2,1)S(1)}, u32[]{:S(2)}, u32[]{:S(2)}) collective-permute-start(bf16[256,1408]{1,0:T(8,128)(2,1)S(1)} %bitcast.89), channel_id=1, source_target_pairs={{0,16},{8,24},{16,0},{24,8},{1,17},{9,25},{17,1},{25,9},{2,18},{10... | collective-permute-start | bytes 2162696 | tf_op jit(solution)/shard_map/ppermute | solution.py:430
  57.9 17.8 %collective-permute-start = (bf16[256,1408]{1,0:T(8,128)(2,1)S(1)}, bf16[256,1408]{1,0:T(8,128)(2,1)S(1)}, u32[]{:S(2)}, u32[]{:S(2)}) collective-permute-start(bf16[256,1408]{1,0:T(8,128)(2,1)S(1)} %bitcast.92), channel_id=1, source_target_pairs={{0,8},{8,0},{16,24},{24,16},{1,9},{9,1},{17,25},{25,17},{2,10},{10... | collective-permute-start | bytes 2162696 | tf_op jit(solution)/shard_map/ppermute | solution.py:430
  74.2 32.4 %collective-permute-start.2 = (bf16[512,1408]{1,0:T(8,128)(2,1)S(1)}, bf16[512,1408]{1,0:T(8,128)(2,1)S(1)}, u32[]{:S(2)}, u32[]{:S(2)}) collective-permute-start(bf16[512,1408]{1,0:T(8,128)(2,1)S(1)} %pad_maximum_fusion.2), channel_id=1, source_target_pairs={{0,8},{8,0},{16,24},{24,16},{1,9},{9,1},{17,25},{25,17},{2,10},{10... | collective-permute-start | bytes 4325384 | tf_op jit(solution)/shard_map/ppermute | solution.py:430
  75.8 32.1 %collective-permute-start.3 = (bf16[512,1408]{1,0:T(8,128)(2,1)S(1)}, bf16[512,1408]{1,0:T(8,128)(2,1)S(1)}, u32[]{:S(2)}, u32[]{:S(2)}) collective-permute-start(bf16[512,1408]{1,0:T(8,128)(2,1)S(1)} %pad_maximum_fusion.3), channel_id=1, source_target_pairs={{0,16},{8,24},{16,0},{24,8},{1,17},{9,25},{17,1},{25,9},{2,18},{10... | collective-permute-start | bytes 4325384 | tf_op jit(solution)/shard_map/ppermute | solution.py:430
  111.7 13.3 %collective-permute-start.5 = (bf16[2048,1408]{1,0:T(8,128)(2,1)}, bf16[2048,1408]{1,0:T(8,128)(2,1)}, u32[]{:S(2)}, u32[]{:S(2)}) collective-permute-start(bf16[2048,1408]{1,0:T(8,128)(2,1)} %slice_dynamic-update-slice_fusion.refs_2_.refs_3_), channel_id=1, source_target_pairs={{0,1},{1,0},{2,3},{3,2},{4,5},{5,4},{6,7},{7,6},{8,9},{9,8},{10,11... | collective-permute-start | bytes 17301512 | tf_op jit(solution)/shard_map/ppermute | solution.py:430
  111.7 12.7 %collective-permute-start.4 = (bf16[512,2048]{1,0:T(8,128)(2,1)S(1)}, bf16[512,2048]{1,0:T(8,128)(2,1)}, u32[]{:S(2)}, u32[]{:S(2)}) collective-permute-start(bf16[512,2048]{1,0:T(8,128)(2,1)S(1)} %copy-done.3), channel_id=1, source_target_pairs={{0,1},{1,0},{2,3},{3,2},{4,5},{5,4},{6,7},{7,6},{8,9},{9,8},{10,11... | collective-permute-start | bytes 6291464 | tf_op jit(solution)/shard_map/ppermute | solution.py:430
  247.9 97.3 %all-to-all-start.1 = ((bf16[4,256,2048]{2,1,0:T(8,128)(2,1)}), bf16[4,256,2048]{2,1,0:T(8,128)(2,1)}, u32[]{:S(2)}, u32[]{:S(2)}) async-start(bf16[4,256,2048]{2,1,0:T(8,128)(2,1)} %pair_product.2), calls=%async_computation.2 | async-start | bytes 8388608 | tf_op jit(solution)/shard_map/all_to_all | solution.py:489
  252.8 118.9 %all-gather.8.cloned.1.call-start = ((), (), s32[]{:S(2)}) async-start(), calls=%async_computation.7 | async-start | bytes 5242880 | tf_op jit(solution)/shard_map/all_gather | solution.py:729
  345.3 26.4 %collective-permute-start.14 = (bf16[256,2048]{1,0:T(8,128)(2,1)}, bf16[256,2048]{1,0:T(8,128)(2,1)}, u32[]{:S(2)}, u32[]{:S(2)}) collective-permute-start(bf16[256,2048]{1,0:T(8,128)(2,1)} %get-tuple-element.94), channel_id=1, source_target_pairs={{0,2},{1,3},{2,4},{3,5},{4,6},{5,7},{6,0},{7,1},{8,10},{9,11},{10,... | collective-permute-start | bytes 3145736 | tf_op jit(solution)/shard_map/ppermute | solution.py:484
  371.7 31.8 %collective-permute-start.15 = (bf16[512,1408]{1,0:T(8,128)(2,1)}, bf16[512,1408]{1,0:T(8,128)(2,1)S(1)}, u32[]{:S(2)}, u32[]{:S(2)}) collective-permute-start(bf16[512,1408]{1,0:T(8,128)(2,1)} %get-tuple-element.96), channel_id=1, source_target_pairs={{0,8},{8,0},{16,24},{24,16},{1,9},{9,1},{17,25},{25,17},{2,10},{10... | collective-permute-start | bytes 4325384 | tf_op jit(solution)/shard_map/ppermute | solution.py:430
  373.2 31.5 %collective-permute-start.16 = (bf16[512,1408]{1,0:T(8,128)(2,1)}, bf16[512,1408]{1,0:T(8,128)(2,1)S(1)}, u32[]{:S(2)}, u32[]{:S(2)}) collective-permute-start(bf16[512,1408]{1,0:T(8,128)(2,1)} %get-tuple-element.97), channel_id=1, source_target_pairs={{0,16},{8,24},{16,0},{24,8},{1,17},{9,25},{17,1},{25,9},{2,18},{10... | collective-permute-start | bytes 4325384 | tf_op jit(solution)/shard_map/ppermute | solution.py:430
  375.4 21.9 %collective-permute-start.17 = (bf16[256,2048]{1,0:T(8,128)(2,1)S(1)}, bf16[256,2048]{1,0:T(8,128)(2,1)S(1)}, u32[]{:S(2)}, u32[]{:S(2)}) collective-permute-start(bf16[256,2048]{1,0:T(8,128)(2,1)S(1)} %copy-done.23), channel_id=1, source_target_pairs={{0,6},{1,7},{2,0},{3,1},{4,2},{5,3},{6,4},{7,5},{8,14},{9,15},{10,... | collective-permute-start | bytes 3145736 | tf_op jit(solution)/shard_map/ppermute | solution.py:484
  408.5 15.0 %collective-permute-start.18 = (bf16[256,1408]{1,0:T(8,128)(2,1)}, bf16[256,1408]{1,0:T(8,128)(2,1)S(1)}, u32[]{:S(2)}, u32[]{:S(2)}) collective-permute-start(bf16[256,1408]{1,0:T(8,128)(2,1)} %get-tuple-element.103), channel_id=1, source_target_pairs={{0,16},{8,24},{16,0},{24,8},{1,17},{9,25},{17,1},{25,9},{2,18},{10... | collective-permute-start | bytes 2162696 | tf_op jit(solution)/shard_map/ppermute | solution.py:430
  410.0 14.3 %collective-permute-start.19 = (bf16[256,1408]{1,0:T(8,128)(2,1)}, bf16[256,1408]{1,0:T(8,128)(2,1)}, u32[]{:S(2)}, u32[]{:S(2)}) collective-permute-start(bf16[256,1408]{1,0:T(8,128)(2,1)} %get-tuple-element.104), channel_id=1, source_target_pairs={{0,8},{8,0},{16,24},{24,16},{1,9},{9,1},{17,25},{25,17},{2,10},{10... | collective-permute-start | bytes 2162696 | tf_op jit(solution)/shard_map/ppermute | solution.py:430
  428.1 38.8 %all-to-all-start.2 = ((bf16[8,64,1408]{2,1,0:T(8,128)(2,1)}), bf16[8,64,1408]{2,1,0:T(8,128)(2,1)S(1)}, u32[]{:S(2)}, u32[]{:S(2)}) async-start(bf16[8,64,1408]{2,1,0:T(8,128)(2,1)} %bitcast.95), calls=%async_computation.3 | async-start | bytes 2883584 | tf_op jit(solution)/shard_map/all_to_all | solution.py:714
  471.4 14.1 %collective-permute-start.22 = (bf16[32,8512]{1,0:T(8,128)(2,1)S(1)}, bf16[32,8512]{1,0:T(8,128)(2,1)S(1)}, u32[]{:S(2)}, u32[]{:S(2)}) collective-permute-start(bf16[32,8512]{1,0:T(8,128)(2,1)S(1)} %get-tuple-element.152.refs_0_), channel_id=1, source_target_pairs={{0,8},{8,0},{16,24},{24,16},{1,9},{9,1},{17,25},{25,17},{2,10},{10... | collective-permute-start | bytes 1634312 | tf_op jit(solution)/shard_map/ppermute | solution.py:430
  472.6 14.1 %collective-permute-start.23 = (bf16[32,8512]{1,0:T(8,128)(2,1)S(1)}, bf16[32,8512]{1,0:T(8,128)(2,1)S(1)}, u32[]{:S(2)}, u32[]{:S(2)}) collective-permute-start(bf16[32,8512]{1,0:T(8,128)(2,1)S(1)} %get-tuple-element.151.refs_1_), channel_id=1, source_target_pairs={{0,16},{8,24},{16,0},{24,8},{1,17},{9,25},{17,1},{25,9},{2,18},{10... | collective-permute-start | bytes 1634312 | tf_op jit(solution)/shard_map/ppermute | solution.py:430
  485.6 24.9 %collective-permute-start.25 = (bf16[64,8512]{1,0:T(8,128)(2,1)S(1)}, bf16[64,8512]{1,0:T(8,128)(2,1)S(1)}, u32[]{:S(2)}, u32[]{:S(2)}) collective-permute-start(bf16[64,8512]{1,0:T(8,128)(2,1)S(1)} %pad_maximum_fusion.8), channel_id=1, source_target_pairs={{0,16},{8,24},{16,0},{24,8},{1,17},{9,25},{17,1},{25,9},{2,18},{10... | collective-permute-start | bytes 3268616 | tf_op jit(solution)/shard_map/ppermute | solution.py:430
  486.7 46.4 %collective-permute-start.26 = (bf16[256,2048]{1,0:T(8,128)(2,1)S(1)}, bf16[256,2048]{1,0:T(8,128)(2,1)S(1)}, u32[]{:S(2)}, u32[]{:S(2)}) collective-permute-start(bf16[256,2048]{1,0:T(8,128)(2,1)S(1)} %copy-done.22), channel_id=1, source_target_pairs={{0,4},{1,5},{2,6},{3,7},{4,0},{5,1},{6,2},{7,3},{8,12},{9,13},{10,... | collective-permute-start | bytes 3145736 | tf_op jit(solution)/shard_map/ppermute | solution.py:484
  486.9 24.7 %collective-permute-start.24 = (bf16[64,8512]{1,0:T(8,128)(2,1)S(1)}, bf16[64,8512]{1,0:T(8,128)(2,1)S(1)}, u32[]{:S(2)}, u32[]{:S(2)}) collective-permute-start(bf16[64,8512]{1,0:T(8,128)(2,1)S(1)} %pad_maximum_fusion.7), channel_id=1, source_target_pairs={{0,8},{8,0},{16,24},{24,16},{1,9},{9,1},{17,25},{25,17},{2,10},{10... | collective-permute-start | bytes 3268616 | tf_op jit(solution)/shard_map/ppermute | solution.py:430
  (41 other events, 316.8 us)
Sparse Core Ops, SparseCore 0:
  55.0 80.9 all-gather.3
  137.6 80.9 all-gather.5
  248.1 52.3 reduce-scatter.1
  306.4 54.1 all-gather.7

commit v4 on v3

--- a/solution.py
+++ b/solution.py
@@ -467,15 +467,13 @@
 def gather_near(own):
     rows = own.shape[0] // 2
     upper, lower = own[:rows], own[rows:]
-    return upper, lower, swap(upper, "dp", 1), swap(lower, "dp", 2)
+    upper1, lower2 = swap(upper, "dp", 1), swap(lower, "dp", 2)
+    upper2, lower1 = swap(upper, "dp", 2), swap(lower, "dp", 1)
+    return [(upper, lower), (upper1, lower1), (upper2, lower2)]
 
 
 def gather_far(first):
-    upper, lower, upper1, lower2 = first
-    rows = upper.shape[0]
-    uppers = swap(jnp.concatenate([upper, upper1], axis=0), "dp", 2)
-    lowers = swap(jnp.concatenate([lower, lower2], axis=0), "dp", 1)
-    return [(upper, lower), (upper1, lowers[:rows]), (uppers[:rows], lower2), (uppers[rows:], lowers[rows:])]
+    return first + [(swap(first[1][0], "dp", 2), swap(first[2][1], "dp", 1))]
 
 
 def line_permute(block, reach):
@@ -547,6 +545,24 @@
     return jnp.concatenate([jnp.where(high, lows[k ^ 2], lows[k]).astype(F32) for k in range(4)], axis=0)
 
 
+def keep_kernel(in_ref, out_ref):
+    out_ref[...] = in_ref[...]
+
+
+def keep(array):
+    rows = 64
+    spec = pl.BlockSpec((rows, array.shape[1]), lambda i: (i, 0))
+    return pl.pallas_call(
+        keep_kernel,
+        grid=(array.shape[0] // rows,),
+        in_specs=[spec],
+        out_specs=spec,
+        out_shape=jax.ShapeDtypeStruct(array.shape, array.dtype),
+        cost_estimate=FREE,
+        name="keep",
+    )(array)
+
+
 def assemble_kernel(place_ref, *refs):
     out_ref = refs[-1]
     for own in range(4):
@@ -560,7 +576,7 @@
 def assemble(gathered):
     pieces = [half for pair in gathered for half in pair]
     half_rows, columns = pieces[0].shape
-    chunk = 512
+    chunk = 1280
     return pl.pallas_call(
         assemble_kernel,
         grid=(pl.cdiv(columns, chunk),),
@@ -569,7 +585,7 @@
         out_specs=pl.BlockSpec((chunk, 8 * half_rows), lambda i: (i, 0)),
         out_shape=jax.ShapeDtypeStruct((columns, 8 * half_rows), F32),
         compiler_params=pltpu.CompilerParams(dimension_semantics=("arbitrary",), vmem_limit_bytes=VMEM),
-        cost_estimate=FREE,
+        cost_estimate=pl.CostEstimate(flops=1, bytes_accessed=30 * 2**20, transcendentals=0),
         name="assemble",
     )(lax.axis_index("dp").astype(jnp.int32)[None], *pieces).T
 
@@ -634,8 +650,9 @@
     line = mp <= 16
     inputs_f = inputs.astype(F32)
     rms_scale = lax.rsqrt(jnp.mean(inputs_f * inputs_f, axis=-1, keepdims=True) + EPS)
-    normed = inputs_f * rms_scale
-    hidden_own = reorder((normed * norm_gain[None, :]).astype(BF16))
+    gain_in = reorder(norm_gain[None, :])
+    normed = reorder(inputs).astype(F32) * rms_scale
+    hidden_own = (normed * gain_in).astype(BF16)
     hidden_own, got = lax.optimization_barrier((hidden_own, got))
     weight = jnp.concatenate(sum(gather_far(gather_near(got.reshape(mp * part, columns))), ()), axis=0)
     hidden = lax.all_gather(hidden_own, "mp", axis=0, tiled=True)
@@ -715,6 +732,10 @@
 
     token_rows, out_part = lax.optimization_barrier((token_rows, out_part))
     out_mine = lax.psum_scatter(out_part, "dp", scatter_dimension=0, tiled=True)
+    def norm_share(d_hidden):
+        share = restore(jnp.sum(d_hidden * normed, axis=0)[None, :])
+        return all_sum(share.reshape(-1, LANES), "dp")
+
     def rows_of(blocks):
         flat = lambda first, size: blocks[:, :, first : first + size].transpose(1, 0, 2).reshape(part, -1)
         shared = jnp.sum(blocks[:, :, width : width + 2 * state_dim].astype(F32), axis=0).astype(BF16)
@@ -756,13 +777,15 @@
         d_blocks += [line_permute(d_shares[reach], reach) for reach in reaches[1:2]]
         near_got, d_blocks = lax.optimization_barrier((near_got, d_blocks))
         mine = reduce_far(share, in_block, near_got)
-        mine, packed = lax.optimization_barrier((mine, packed))
+        d_blocks += [line_permute(d_shares[reach], reach) for reach in reaches[2:]]
+        mine, packed, d_blocks = lax.optimization_barrier((mine, packed, d_blocks))
         blocks = to_rows(mine)
-        blocks, d_shares, packed = lax.optimization_barrier((blocks, d_shares, all_sum(packed, "dp")))
-        d_blocks += [line_permute(d_shares[reach], reach) for reach in reaches[2:]]
-        gathered = gather_far(gather_near(rows_of(blocks)))
-        in_weight_grad, d_blocks = lax.optimization_barrier((assemble(gathered), d_blocks))
         d_hidden = total(d_blocks)
+        norm_part = norm_share(d_hidden)
+        blocks, packed, out_weight_grad, norm_part = lax.optimization_barrier(
+            (blocks, all_sum(packed, "dp"), keep(out_weight_grad), norm_part)
+        )
+        in_weight_grad = assemble(gather_far(gather_near(rows_of(blocks))))
     else:
         packed = all_sum(packed, "dp")
         share = mm(hidden, d_proj, TN)
@@ -772,9 +795,8 @@
         d_hidden = lax.psum_scatter(d_shares, "mp", scatter_dimension=0, tiled=True).astype(F32)
         in_weight_grad = in_place_order(gather_far(gather_near(rows_of(blocks))))
     outputs = (inputs_f + total(sent)).astype(BF16)
-    d_hidden = restore(d_hidden)
-    norm_gain_grad = jnp.sum(d_hidden * normed, axis=0)
-    norm_part = all_sum(norm_gain_grad.reshape(-1, LANES), "dp")
+    if not line:
+        norm_part = norm_share(d_hidden)
     everything = all_sum(jnp.concatenate([packed, norm_part], axis=0), "mp")
     norm_total = everything[packed.shape[0] :].reshape(depth)
     packed = everything.reshape(-1)
@@ -782,9 +804,9 @@
     head_total = packed[sizes[0] : sizes[0] + sizes[1]].reshape(head_full.shape)
     gain_total = packed[sizes[0] + sizes[1] : sum(sizes)]
 
-    d_normed_in = d_hidden * norm_gain[None, :]
+    d_normed_in = d_hidden * gain_in
     input_back = rms_scale * (d_normed_in - normed * jnp.mean(d_normed_in * normed, axis=-1, keepdims=True))
-    input_grad = (cotangent.astype(F32) + input_back).astype(BF16)
+    input_grad = restore((reorder(cotangent).astype(F32) + input_back).astype(BF16))
 
     return (
         outputs,

time: 585 us -> 565 us (0.966)
  waiting for transfers between devices: 271 us -> 226 us
  local copies, waits for them, and re-layouts: 49.2 us -> 60.6 us
  starting transfers between devices: 38.9 us -> 45 us
    ppermute x29 -> x33, waiting for transfers between devices: 150 us -> 115 us  [swap(): lax.ppermute(value, axis, [(place, place ^ bit) for place in range(size)])]
    all_to_all x1, waiting for transfers between devices: 24.1 us -> 0.78 us  [to_rows(): lax.all_to_all(mine.astype(BF16).reshape(mp, part, -1), 'mp', split_axis=...]
    ppermute x3, waiting for transfers between devices: 35.6 us -> 54.2 us  [line_permute(): return lax.ppermute(block, 'mp', pairs)]
    reshape x4 -> x12, local copies, waits for them, and re-layouts: 4.36 us -> 16 us  [reorder(): lax.dynamic_index_in_dim(apart, dp_place ^ k, 2, keepdims=False)]
    all_to_all x1, waiting for transfers between devices: 25.4 us -> 17.2 us  [on_device(): got = lax.all_to_all(send, 'mp', split_axis=0, concat_axis=0, tiled=True)]
    pallas_call x0 -> x1, Pallas kernels: none -> 6.61 us  [keep(): pl.pallas_call(keep_kernel, grid=(array.shape[0] // rows,), in_specs=[spe...]
    ppermute x29 -> x33, starting transfers between devices: 22.7 us -> 28.6 us  [swap(): lax.ppermute(value, axis, [(place, place ^ bit) for place in range(size)])]
    unnamed x62 -> x97, local copies, waits for them, and re-layouts: 11.4 us -> 12.8 us
  transfers between devices with their start and end apart: 39 -> 43, of which waited for: 33 -> 32; matrix products, arithmetic and copies ran while one was open for 12% -> 19% of each run, Pallas kernels for 23% -> 23%
where the time goes in v4:
time: 565 us; the launch traced here: 560 us
  waiting for transfers between devices  226 us (40%)
  Pallas kernels  148 us (26%)
  local copies, waits for them, and re-layouts  60.6 us (11%)
  starting transfers between devices  45 us (8%)
  other arithmetic  35.9 us (6%)
  matrix products  28.2 us (5%)
  between operations  15.5 us (3%)
    ppermute x33, waiting for transfers between devices, swap(): lax.ppermute(value, axis, [(place, place ^ bit) for place in range(size)])  115 us
    ppermute x3, waiting for transfers between devices, line_permute(): return lax.ppermute(block, 'mp', pairs)  54.2 us
    pallas_call x1, Pallas kernels, mixer_backward(): pl.pallas_call(lambda *refs: backward_kernel(*refs, state_dim=state_dim,...  49.6 us
    pallas_call x1, Pallas kernels, mixer_forward(): pl.pallas_call(lambda *refs: forward_kernel(*refs, state_dim=state_dim, w...  39.1 us
    pallas_call x2, Pallas kernels, pair_product(): pl.pallas_call(lambda *refs: pair_kernel(*refs, dims=dims), grid_spec=plt...  32.2 us
    ppermute x33, starting transfers between devices, swap(): lax.ppermute(value, axis, [(place, place ^ bit) for place in range(size)])  28.6 us
    dot_general x2, matrix products, mm(): return lax.dot_general(left, right, dims, preferred_element_type=F32)  28.2 us
    all_to_all x1, waiting for transfers between devices, on_device(): got = lax.all_to_all(send, 'mp', split_axis=0, concat_axis=0, tiled=True)  17.2 us
  transfers between devices with their start and end apart: 43, of which 32 were waited for; matrix products, arithmetic and copies ran while one was open for 19% of the time, Pallas kernels for 23%

profile of v4, /device:TPU:0, one launch (start us, length us, event | category | flops | bytes accessed | tf_op | source)
XLA Modules:
  0.0 559.5 jit_solution(12958563230281188145)
XLA Ops:
  13.4 6.5 %all-to-all-start = ((bf16[8,64,1408]{2,1,0:T(8,128)(2,1)}), bf16[8,64,1408]{2,1,0:T(8,128)(2,1)S(1)}, u32[]{:S(2)}, u32[]{:S(2)}) async-start(bf16[8,64,1408]{2,1,0:T(8,128)(2,1)} %fusion.9), calls=%async_computation | async-start | bytes 2883584 | tf_op jit(solution)/shard_map/all_to_all | solution.py:632
  37.7 17.2 %all-to-all-done = bf16[8,64,1408]{2,1,0:T(8,128)(2,1)S(1)} async-done(((bf16[8,64,1408]{2,1,0:T(8,128)(2,1)}), bf16[8,64,1408]{2,1,0:T(8,128)(2,1)S(1)}, u32[]{:S(2)}, u32[]{:S(2)}) %all-to-all-start) | async-done | bytes 1441824 | tf_op jit(solution)/shard_map/all_to_all | solution.py:632
  62.4 13.1 %collective-permute-done = bf16[256,1408]{1,0:T(8,128)(2,1)S(1)} collective-permute-done((bf16[256,1408]{1,0:T(8,128)(2,1)S(1)}, bf16[256,1408]{1,0:T(8,128)(2,1)S(1)}, u32[]{:S(2)}, u32[]{:S(2)}) %collective-permute-start) | collective-permute-done | bytes 720928 | tf_op jit(solution)/shard_map/ppermute | solution.py:430
  79.4 11.5 %collective-permute-done.1 = bf16[256,1408]{1,0:T(8,128)(2,1)S(1)} collective-permute-done((bf16[256,1408]{1,0:T(8,128)(2,1)S(1)}, bf16[256,1408]{1,0:T(8,128)(2,1)S(1)}, u32[]{:S(2)}, u32[]{:S(2)}) %collective-permute-start.1) | collective-permute-done | bytes 720928 | tf_op jit(solution)/shard_map/ppermute | solution.py:430
  94.3 11.9 %collective-permute-done.4 = bf16[256,1408]{1,0:T(8,128)(2,1)S(1)} collective-permute-done((bf16[256,1408]{1,0:T(8,128)(2,1)S(1)}, bf16[256,1408]{1,0:T(8,128)(2,1)S(1)}, u32[]{:S(2)}, u32[]{:S(2)}) %collective-permute-start.4) | collective-permute-done | bytes 720928 | tf_op jit(solution)/shard_map/ppermute | solution.py:430
  112.2 7.8 %collective-permute-done.6.refs_4_ = bf16[512,2048]{1,0:T(8,128)(2,1)} collective-permute-done((bf16[512,2048]{1,0:T(8,128)(2,1)S(1)}, bf16[512,2048]{1,0:T(8,128)(2,1)}, u32[]{:S(2)}, u32[]{:S(2)}) %collective-permute-start.6) | collective-permute-done | bytes 2097184 | tf_op jit(solution)/shard_map/ppermute | solution.py:430
  121.2 14.8 %all-gather.4.cloned.1.call-done.refs_1_ = bf16[2048,2048]{1,0:T(8,128)(2,1)} async-done(((bf16[256,2048]{1,0:T(8,128)(2,1)}), bf16[2048,2048]{1,0:T(8,128)(2,1)}) %all-gather.4.cloned.1.call-update) | async-done | bytes 8388624 | tf_op jit(solution)/shard_map/all_gather | solution.py:658
  136.0 39.1 %mixer_forward.1 = (bf16[2048,1408]{1,0:T(8,128)(2,1)}, bf16[2048,512]{1,0:T(8,128)(2,1)}, f32[8,128,512]{2,1,0:T(8,128)}, f32[8,8,256]{2,1,0:T(8,128)}, f32[2048,768]{1,0:T(8,128)}) custom-call(f32[1,1,512]{2,1,0:T(1,128)} %broadcast_in_dim.51.refs_0_, bf16[2048,2048]{1,0:T(8,128)(2,1)} %all-gather.4.cloned.1.call-done.refs_1_, ...), custom_call_target="tpu_custom_call" | custom-call | flops 1 | bytes 1 | tf_op jit(solution)/shard_map/mixer_forward/pallas_call | solution.py:286
  177.3 6.2 %collective-permute-done.9 = f32[8,256]{1,0:T(8,128)S(1)} collective-permute-done((f32[8,256]{1,0:T(8,128)S(1)}, f32[8,256]{1,0:T(8,128)S(1)}, u32[]{:S(2)}, u32[]{:S(2)}) %collective-permute-start.9) | collective-permute-done | bytes 8224 | tf_op jit(solution)/shard_map/ppermute | solution.py:430
  195.7 9.3 %pair_product.2 = bf16[4,256,2048]{2,1,0:T(8,128)(2,1)} custom-call(s32[2]{0:T(128)} %pad_add_fusion.refs_0_, bf16[2048,512]{1,0:T(8,128)(2,1)} %copy-done, bf16[1024,512]{1,0:T(8,128)(2,1)} %collective-permute-done.11.refs_2_, bf16[512,2048]{1,0:T(8,128)(2,1)} %weight_ref.1, bf16[512,2048]{1,0:T(8,128)(2,1)} %collective-permute-done.6.refs_4_), custom_call_target="tpu_custom_call" | custom-call | flops 1 | bytes 1 | tf_op jit(solution)/shard_map/pair_product/pallas_call | solution.py:509
  205.0 13.6 %all-gather.6.cloned.1.call-done.cot_ref = bf16[2048,2048]{1,0:T(8,128)(2,1)} async-done(((bf16[256,2048]{1,0:T(8,128)(2,1)}), bf16[2048,2048]{1,0:T(8,128)(2,1)}) %all-gather.6.cloned.1.call-update) | async-done | bytes 8388624 | tf_op jit(solution)/shard_map/all_gather | solution.py:699
  218.6 12.4 %pull_back.1 = (f32[2048,512]{1,0:T(8,128)}, f32[8,8,256]{2,1,0:T(8,128)}) custom-call(bf16[2048,2048]{1,0:T(8,128)(2,1)} %all-gather.6.cloned.1.call-done.cot_ref, bf16[512,2048]{1,0:T(8,128)(2,1)} %weight_ref.1, bf16[2048,1408]{1,0:T(8,128)(2,1)} %get-tuple-element.70.gate_ref.refs_1_, bf16[2048,512]{1,0:T(8,128)(2,1)} %get-tuple-element.72.y_ref.refs_3_, ...), custom_call_target="tpu_custom_call" | custom-call | flops 1 | bytes 1 | tf_op jit(solution)/shard_map/pull_back/pallas_call | solution.py:391
  237.7 9.4 %fusion.28 = f32[512,2048]{1,0:T(8,128)} fusion(bf16[2048,512]{1,0:T(8,128)(2,1)S(1)} %copy-done.1, bf16[2048,2048]{1,0:T(8,128)(2,1)} %all-gather.6.cloned.1.call-done.cot_ref), kind=kOutput, calls=%fused_computation.113 | convolution fusion | flops 4294967296 | bytes 14680064 | tf_op jit(solution)/shard_map/dot_general | solution.py:23
  253.0 49.6 %mixer_backward.1 = (bf16[2048,1408]{1,0:T(8,128)(2,1)}, f32[8,768]{1,0:T(8,128)}, f32[8,128]{1,0:T(8,128)}, f32[8,512]{1,0:T(8,128)}) custom-call(f32[1,8,512]{2,1,0:T(8,128)} %maximum_maximum_fusion.1.gain_ref.refs_0_, bf16[2048,1408]{1,0:T(8,128)(2,1)} %get-tuple-element.70.gate_ref.refs_1_, f32[2048,768]{1,0:T(8,128)} %get-tuple-element.71.refs_2_, ...), custom_call_target="tpu_custom_call" | custom-call | flops 1 | bytes 1 | tf_op jit(solution)/shard_map/mixer_backward/pallas_call | solution.py:332
  311.9 22.9 %pair_product.3 = (bf16[256,2048]{1,0:T(8,128)(2,1)}, bf16[256,2048]{1,0:T(8,128)(2,1)}, bf16[256,2048]{1,0:T(8,128)(2,1)}, bf16[256,2048]{1,0:T(8,128)(2,1)}) custom-call(s32[2]{0:T(128)} %pad_add_fusion.refs_0_, bf16[2048,1408]{1,0:T(8,128)(2,1)} %get-tuple-element.92.refs_1_, bf16[1024,1408]{1,0:T(8,128)(2,1)} %collective-permute-done.15.refs_2_, ...), custom_call_target="tpu_custom_call" | custom-call | flops 1 | bytes 1 | tf_op jit(solution)/shard_map/pair_product/pallas_call | solution.py:509
  334.8 10.5 %all-to-all-done.1 = bf16[4,256,2048]{2,1,0:T(8,128)(2,1)} async-done(((bf16[4,256,2048]{2,1,0:T(8,128)(2,1)}), bf16[4,256,2048]{2,1,0:T(8,128)(2,1)}, u32[]{:S(2)}, u32[]{:S(2)}) %all-to-all-start.1) | async-done | bytes 4194336 | tf_op jit(solution)/shard_map/all_to_all | solution.py:487
  345.4 18.8 %fusion.27 = (bf16[2048,1408]{1,0:T(8,128)(2,1)S(1)}, f32[2048,1408]{1,0:T(8,128)}) fusion(bf16[2048,2048]{1,0:T(8,128)(2,1)} %all-gather.4.cloned.1.call-done.refs_1_, bf16[2048,1408]{1,0:T(8,128)(2,1)} %get-tuple-element.92.refs_1_), kind=kOutput, calls=%fused_computation.112 | convolution fusion | flops 11814043648 | bytes 31457280 | tf_op jit(solution)/shard_map/dot_general | solution.py:23
  375.2 22.1 %collective-permute-done.19 = bf16[256,2048]{1,0:T(8,128)(2,1)} collective-permute-done((bf16[256,2048]{1,0:T(8,128)(2,1)S(1)}, bf16[256,2048]{1,0:T(8,128)(2,1)}, u32[]{:S(2)}, u32[]{:S(2)}) %collective-permute-start.19) | collective-permute-done | bytes 1048608 | tf_op jit(solution)/shard_map/ppermute | solution.py:482
  412.5 11.0 %collective-permute-done.20 = bf16[256,1408]{1,0:T(8,128)(2,1)S(1)} collective-permute-done((bf16[256,1408]{1,0:T(8,128)(2,1)}, bf16[256,1408]{1,0:T(8,128)(2,1)S(1)}, u32[]{:S(2)}, u32[]{:S(2)}) %collective-permute-start.20) | collective-permute-done | bytes 720928 | tf_op jit(solution)/shard_map/ppermute | solution.py:430
  428.1 27.4 %collective-permute-done.22 = bf16[256,2048]{1,0:T(8,128)(2,1)S(1)} collective-permute-done((bf16[256,2048]{1,0:T(8,128)(2,1)}, bf16[256,2048]{1,0:T(8,128)(2,1)S(1)}, u32[]{:S(2)}, u32[]{:S(2)}) %collective-permute-start.22) | collective-permute-done | bytes 1048608 | tf_op jit(solution)/shard_map/ppermute | solution.py:482
  480.3 6.6 %keep.1 = f32[512,2048]{1,0:T(8,128)} custom-call(f32[512,2048]{1,0:T(8,128)} %all-gather.8.cloned.1.call-done.in_ref), custom_call_target="tpu_custom_call" | custom-call | flops 1 | bytes 1 | tf_op jit(solution)/shard_map/keep/pallas_call | solution.py:555
  526.4 6.7 %collective-permute-done.31.refs_3_ = bf16[32,8512]{1,0:T(8,128)(2,1)S(1)} collective-permute-done((bf16[32,8512]{1,0:T(8,128)(2,1)}, bf16[32,8512]{1,0:T(8,128)(2,1)S(1)}, u32[]{:S(2)}, u32[]{:S(2)}) %collective-permute-start.31) | collective-permute-done | bytes 544800 | tf_op jit(solution)/shard_map/ppermute | solution.py:430
  533.6 10.0 %collective-permute-done.34.refs_6_ = bf16[32,8512]{1,0:T(8,128)(2,1)S(1)} collective-permute-done((bf16[32,8512]{1,0:T(8,128)(2,1)}, bf16[32,8512]{1,0:T(8,128)(2,1)S(1)}, u32[]{:S(2)}, u32[]{:S(2)}) %collective-permute-start.34) | collective-permute-done | bytes 544800 | tf_op jit(solution)/shard_map/ppermute | solution.py:430
  544.6 8.1 %assemble.1 = f32[8512,256]{1,0:T(8,128)} custom-call(s32[1]{0:T(128)} %bitcast.47.place_ref, bf16[32,8512]{1,0:T(8,128)(2,1)} %get-tuple-element.170.refs_0_, bf16[32,8512]{1,0:T(8,128)(2,1)} %get-tuple-element.169.refs_1_, bf16[32,8512]{1,0:T(8,128)(2,1)} %collective-permute-done.30.refs_2_, bf16[32,8512]{1,0:T(8,128)(2,1)} %copy-done.22, ...), custom_call_target="tpu_custom_call" | custom-call | flops 1 | bytes 31457280 | tf_op jit(solution)/shard_map/assemble/pallas_call | solution.py:580
  (297 shorter events, 177.6 us)
Async XLA Ops:
  13.4 41.5 %all-to-all-start = ((bf16[8,64,1408]{2,1,0:T(8,128)(2,1)}), bf16[8,64,1408]{2,1,0:T(8,128)(2,1)S(1)}, u32[]{:S(2)}, u32[]{:S(2)}) async-start(bf16[8,64,1408]{2,1,0:T(8,128)(2,1)} %fusion.9), calls=%async_computation | async-start | bytes 2883584 | tf_op jit(solution)/shard_map/all_to_all | solution.py:632
  19.8 116.2 %all-gather.4.cloned.1.call-start = ((), (), s32[]{:S(2)}) async-start(), calls=%async_computation.4 | async-start | bytes 9437184 | tf_op jit(solution)/shard_map/all_gather | solution.py:658
  54.9 163.7 %all-gather.6.cloned.1.call-start = ((), (), s32[]{:S(2)}) async-start(), calls=%async_computation.5 | async-start | bytes 9437184 | tf_op jit(solution)/shard_map/all_gather | solution.py:699
  55.6 247.0 %reduce-scatter.2.cloned.1.call-start = ((), (), s32[]{:S(2)}) async-start(), calls=%async_computation.6 | async-start | bytes 5242880 | tf_op jit(solution)/shard_map/reduce_scatter | solution.py:734
  56.3 19.1 %collective-permute-start = (bf16[256,1408]{1,0:T(8,128)(2,1)S(1)}, bf16[256,1408]{1,0:T(8,128)(2,1)S(1)}, u32[]{:S(2)}, u32[]{:S(2)}) collective-permute-start(bf16[256,1408]{1,0:T(8,128)(2,1)S(1)} %bitcast.100), channel_id=1, source_target_pairs={{0,8},{8,0},{16,24},{24,16},{1,9},{9,1},{17,25},{25,17},{2,10},{10... | collective-permute-start | bytes 2162696 | tf_op jit(solution)/shard_map/ppermute | solution.py:430
  57.9 19.1 %collective-permute-start.3 = (bf16[256,1408]{1,0:T(8,128)(2,1)S(1)}, bf16[256,1408]{1,0:T(8,128)(2,1)S(1)}, u32[]{:S(2)}, u32[]{:S(2)}) collective-permute-start(bf16[256,1408]{1,0:T(8,128)(2,1)S(1)} %bitcast.103), channel_id=1, source_target_pairs={{0,16},{8,24},{16,0},{24,8},{1,17},{9,25},{17,1},{25,9},{2,18},{10... | collective-permute-start | bytes 2162696 | tf_op jit(solution)/shard_map/ppermute | solution.py:430
  59.4 31.5 %collective-permute-start.1 = (bf16[256,1408]{1,0:T(8,128)(2,1)S(1)}, bf16[256,1408]{1,0:T(8,128)(2,1)S(1)}, u32[]{:S(2)}, u32[]{:S(2)}) collective-permute-start(bf16[256,1408]{1,0:T(8,128)(2,1)S(1)} %bitcast.104), channel_id=1, source_target_pairs={{0,8},{8,0},{16,24},{24,16},{1,9},{9,1},{17,25},{25,17},{2,10},{10... | collective-permute-start | bytes 2162696 | tf_op jit(solution)/shard_map/ppermute | solution.py:430
  59.9 32.5 %collective-permute-start.2 = (bf16[256,1408]{1,0:T(8,128)(2,1)S(1)}, bf16[256,1408]{1,0:T(8,128)(2,1)S(1)}, u32[]{:S(2)}, u32[]{:S(2)}) collective-permute-start(bf16[256,1408]{1,0:T(8,128)(2,1)S(1)} %bitcast.101), channel_id=1, source_target_pairs={{0,16},{8,24},{16,0},{24,8},{1,17},{9,25},{17,1},{25,9},{2,18},{10... | collective-permute-start | bytes 2162696 | tf_op jit(solution)/shard_map/ppermute | solution.py:430
  75.5 30.7 %collective-permute-start.4 = (bf16[256,1408]{1,0:T(8,128)(2,1)S(1)}, bf16[256,1408]{1,0:T(8,128)(2,1)S(1)}, u32[]{:S(2)}, u32[]{:S(2)}) collective-permute-start(bf16[256,1408]{1,0:T(8,128)(2,1)S(1)} %collective-permute-done), channel_id=1, source_target_pairs={{0,16},{8,24},{16,0},{24,8},{1,17},{9,25},{17,1},{25,9},{2,18},{10... | collective-permute-start | bytes 2162696 | tf_op jit(solution)/shard_map/ppermute | solution.py:430
  77.0 30.1 %collective-permute-start.5 = (bf16[256,1408]{1,0:T(8,128)(2,1)S(1)}, bf16[256,1408]{1,0:T(8,128)(2,1)S(1)}, u32[]{:S(2)}, u32[]{:S(2)}) collective-permute-start(bf16[256,1408]{1,0:T(8,128)(2,1)S(1)} %collective-permute-done.3), channel_id=1, source_target_pairs={{0,8},{8,0},{16,24},{24,16},{1,9},{9,1},{17,25},{25,17},{2,10},{10... | collective-permute-start | bytes 2162696 | tf_op jit(solution)/shard_map/ppermute | solution.py:430
  247.9 97.4 %all-to-all-start.1 = ((bf16[4,256,2048]{2,1,0:T(8,128)(2,1)}), bf16[4,256,2048]{2,1,0:T(8,128)(2,1)}, u32[]{:S(2)}, u32[]{:S(2)}) async-start(bf16[4,256,2048]{2,1,0:T(8,128)(2,1)} %pair_product.2), calls=%async_computation.2 | async-start | bytes 8388608 | tf_op jit(solution)/shard_map/all_to_all | solution.py:487
  252.8 118.9 %all-gather.8.cloned.1.call-start = ((), (), s32[]{:S(2)}) async-start(), calls=%async_computation.7 | async-start | bytes 5242880 | tf_op jit(solution)/shard_map/all_gather | solution.py:750
  345.2 26.4 %collective-permute-start.16 = (bf16[256,2048]{1,0:T(8,128)(2,1)}, bf16[256,2048]{1,0:T(8,128)(2,1)}, u32[]{:S(2)}, u32[]{:S(2)}) collective-permute-start(bf16[256,2048]{1,0:T(8,128)(2,1)} %get-tuple-element.94), channel_id=1, source_target_pairs={{0,2},{1,3},{2,4},{3,5},{4,6},{5,7},{6,0},{7,1},{8,10},{9,11},{10,... | collective-permute-start | bytes 3145736 | tf_op jit(solution)/shard_map/ppermute | solution.py:482
  371.6 31.8 %collective-permute-start.17 = (bf16[512,1408]{1,0:T(8,128)(2,1)}, bf16[512,1408]{1,0:T(8,128)(2,1)S(1)}, u32[]{:S(2)}, u32[]{:S(2)}) collective-permute-start(bf16[512,1408]{1,0:T(8,128)(2,1)} %pad_maximum_fusion.1), channel_id=1, source_target_pairs={{0,8},{8,0},{16,24},{24,16},{1,9},{9,1},{17,25},{25,17},{2,10},{10... | collective-permute-start | bytes 4325384 | tf_op jit(solution)/shard_map/ppermute | solution.py:430
  373.1 31.5 %collective-permute-start.18 = (bf16[512,1408]{1,0:T(8,128)(2,1)}, bf16[512,1408]{1,0:T(8,128)(2,1)S(1)}, u32[]{:S(2)}, u32[]{:S(2)}) collective-permute-start(bf16[512,1408]{1,0:T(8,128)(2,1)} %pad_maximum_fusion.2), channel_id=1, source_target_pairs={{0,16},{8,24},{16,0},{24,8},{1,17},{9,25},{17,1},{25,9},{2,18},{10... | collective-permute-start | bytes 4325384 | tf_op jit(solution)/shard_map/ppermute | solution.py:430
  375.2 22.1 %collective-permute-start.19 = (bf16[256,2048]{1,0:T(8,128)(2,1)S(1)}, bf16[256,2048]{1,0:T(8,128)(2,1)}, u32[]{:S(2)}, u32[]{:S(2)}) collective-permute-start(bf16[256,2048]{1,0:T(8,128)(2,1)S(1)} %copy-done.39), channel_id=1, source_target_pairs={{0,6},{1,7},{2,0},{3,1},{4,2},{5,3},{6,4},{7,5},{8,14},{9,15},{10,... | collective-permute-start | bytes 3145736 | tf_op jit(solution)/shard_map/ppermute | solution.py:482
  411.8 43.6 %collective-permute-start.22 = (bf16[256,2048]{1,0:T(8,128)(2,1)}, bf16[256,2048]{1,0:T(8,128)(2,1)S(1)}, u32[]{:S(2)}, u32[]{:S(2)}) collective-permute-start(bf16[256,2048]{1,0:T(8,128)(2,1)} %get-tuple-element.111), channel_id=1, source_target_pairs={{0,4},{1,5},{2,6},{3,7},{4,0},{5,1},{6,2},{7,3},{8,12},{9,13},{10,... | collective-permute-start | bytes 3145736 | tf_op jit(solution)/shard_map/ppermute | solution.py:482
  456.4 38.9 %all-to-all-start.2 = ((bf16[8,64,1408]{2,1,0:T(8,128)(2,1)}), bf16[8,64,1408]{2,1,0:T(8,128)(2,1)S(1)}, u32[]{:S(2)}, u32[]{:S(2)}) async-start(bf16[8,64,1408]{2,1,0:T(8,128)(2,1)} %bitcast.93), calls=%async_computation.3 | async-start | bytes 2883584 | tf_op jit(solution)/shard_map/all_to_all | solution.py:731
  501.0 20.7 %collective-permute-start.30 = (bf16[32,8512]{1,0:T(8,128)(2,1)}, bf16[32,8512]{1,0:T(8,128)(2,1)}, u32[]{:S(2)}, u32[]{:S(2)}) collective-permute-start(bf16[32,8512]{1,0:T(8,128)(2,1)} %get-tuple-element.170.refs_0_), channel_id=1, source_target_pairs={{0,8},{8,0},{16,24},{24,16},{1,9},{9,1},{17,25},{25,17},{2,10},{10... | collective-permute-start | bytes 1634312 | tf_op jit(solution)/shard_map/ppermute | solution.py:430
  502.4 20.2 %collective-permute-start.33 = (bf16[32,8512]{1,0:T(8,128)(2,1)}, bf16[32,8512]{1,0:T(8,128)(2,1)}, u32[]{:S(2)}, u32[]{:S(2)}) collective-permute-start(bf16[32,8512]{1,0:T(8,128)(2,1)} %get-tuple-element.169.refs_1_), channel_id=1, source_target_pairs={{0,16},{8,24},{16,0},{24,8},{1,17},{9,25},{17,1},{25,9},{2,18},{10... | collective-permute-start | bytes 1634312 | tf_op jit(solution)/shard_map/ppermute | solution.py:430
  517.5 15.6 %collective-permute-start.31 = (bf16[32,8512]{1,0:T(8,128)(2,1)}, bf16[32,8512]{1,0:T(8,128)(2,1)S(1)}, u32[]{:S(2)}, u32[]{:S(2)}) collective-permute-start(bf16[32,8512]{1,0:T(8,128)(2,1)} %get-tuple-element.169.refs_1_), channel_id=1, source_target_pairs={{0,8},{8,0},{16,24},{24,16},{1,9},{9,1},{17,25},{25,17},{2,10},{10... | collective-permute-start | bytes 1634312 | tf_op jit(solution)/shard_map/ppermute | solution.py:430
  518.0 15.6 %collective-permute-start.32 = (bf16[32,8512]{1,0:T(8,128)(2,1)}, bf16[32,8512]{1,0:T(8,128)(2,1)S(1)}, u32[]{:S(2)}, u32[]{:S(2)}) collective-permute-start(bf16[32,8512]{1,0:T(8,128)(2,1)} %get-tuple-element.170.refs_0_), channel_id=1, source_target_pairs={{0,16},{8,24},{16,0},{24,8},{1,17},{9,25},{17,1},{25,9},{2,18},{10... | collective-permute-start | bytes 1634312 | tf_op jit(solution)/shard_map/ppermute | solution.py:430
  521.6 22.0 %collective-permute-start.34 = (bf16[32,8512]{1,0:T(8,128)(2,1)}, bf16[32,8512]{1,0:T(8,128)(2,1)S(1)}, u32[]{:S(2)}, u32[]{:S(2)}) collective-permute-start(bf16[32,8512]{1,0:T(8,128)(2,1)} %collective-permute-done.30.refs_2_), channel_id=1, source_target_pairs={{0,16},{8,24},{16,0},{24,8},{1,17},{9,25},{17,1},{25,9},{2,18},{10... | collective-permute-start | bytes 1634312 | tf_op jit(solution)/shard_map/ppermute | solution.py:430
  522.6 20.9 %collective-permute-start.35 = (bf16[32,8512]{1,0:T(8,128)(2,1)}, bf16[32,8512]{1,0:T(8,128)(2,1)S(1)}, u32[]{:S(2)}, u32[]{:S(2)}) collective-permute-start(bf16[32,8512]{1,0:T(8,128)(2,1)} %collective-permute-done.33.refs_5_), channel_id=1, source_target_pairs={{0,8},{8,0},{16,24},{24,16},{1,9},{9,1},{17,25},{25,17},{2,10},{10... | collective-permute-start | bytes 1634312 | tf_op jit(solution)/shard_map/ppermute | solution.py:430
  (61 other events, 476.6 us)
Sparse Core Ops, SparseCore 0:
  55.0 80.9 all-gather.3
  137.6 80.9 all-gather.5
  248.0 52.3 reduce-scatter.1
  306.4 54.1 all-gather.7

commit v5 on v4

--- a/solution.py
+++ b/solution.py
@@ -234,8 +234,8 @@
     d_parts = halves(d_scores)
     d_c = mm3(d_parts, b_coef, TN) + mm3(ey_parts, old_parts, NT)
     d_b = mm3(d_parts, c_coef) + mm3(tail_parts, grown_parts, NT)
-    end_terms = head_sum(ey * mm3(c_coef, old_parts), ones)
-    start_terms = head_sum(tail * into_state, ones)
+    end_terms = mm((ey * mm3(c_coef, old_parts)).astype(BF16), ones)
+    start_terms = mm((tail * into_state).astype(BF16), ones)
     kept = jnp.sum(last_chan * grown * old, axis=0, keepdims=True)
     skip_part = jnp.sum(dy * values, axis=0, keepdims=True)
     kept_heads = mm_exact_left(jnp.concatenate([kept, skip_part, jnp.zeros((6, width), F32)], axis=0), ones)
@@ -768,7 +768,7 @@
         theirs = swap(for_sibling(d_proj, tokens), "mp", 1)
         d_shares = pair_product(d_proj, theirs, weight, sibling_weight, NT, depth, tokens, False)
         d_shares, d_proj, sent = lax.optimization_barrier((d_shares, d_proj, sent))
-        reaches = [1] + list(range(mp // 2 - 1, 1, -1))
+        reaches = list(range(1, mp // 2))
         d_blocks = [d_shares[0], line_permute(d_shares[1], 1)]
         share = mm(hidden, d_proj, TN)
         near_cut = reduce_cut(share, in_block, BF16)

time: 565 us -> 560 us (level)
  transfers between devices with their start and end apart: 43 -> 43, of which waited for: 32 -> 29; matrix products, arithmetic and copies ran while one was open for 19% -> 19% of each run, Pallas kernels for 23% -> 23%
where the time goes in v5:
time: 560 us; the launch traced here: 554 us
  waiting for transfers between devices  222 us (40%)
  Pallas kernels  147 us (26%)
  local copies, waits for them, and re-layouts  60.6 us (11%)
  starting transfers between devices  45.2 us (8%)
  other arithmetic  35.9 us (6%)
  matrix products  28.2 us (5%)
  between operations  15.5 us (3%)
    ppermute x33, waiting for transfers between devices, swap(): lax.ppermute(value, axis, [(place, place ^ bit) for place in range(size)])  110 us
    ppermute x3, waiting for transfers between devices, line_permute(): return lax.ppermute(block, 'mp', pairs)  53.9 us
    pallas_call x1, Pallas kernels, mixer_backward(): pl.pallas_call(lambda *refs: backward_kernel(*refs, state_dim=state_dim,...  48.2 us
    pallas_call x1, Pallas kernels, mixer_forward(): pl.pallas_call(lambda *refs: forward_kernel(*refs, state_dim=state_dim, w...  39.1 us
    pallas_call x2, Pallas kernels, pair_product(): pl.pallas_call(lambda *refs: pair_kernel(*refs, dims=dims), grid_spec=plt...  32.1 us
    dot_general x2, matrix products, mm(): return lax.dot_general(left, right, dims, preferred_element_type=F32)  28.2 us
    ppermute x33, starting transfers between devices, swap(): lax.ppermute(value, axis, [(place, place ^ bit) for place in range(size)])  27.4 us
    all_to_all x1, waiting for transfers between devices, on_device(): got = lax.all_to_all(send, 'mp', split_axis=0, concat_axis=0, tiled=True)  17.2 us
  transfers between devices with their start and end apart: 43, of which 29 were waited for; matrix products, arithmetic and copies ran while one was open for 19% of the time, Pallas kernels for 23%

profile of v5, /device:TPU:0, one launch (start us, length us, event | category | flops | bytes accessed | tf_op | source)
XLA Modules:
  0.0 554.1 jit_solution(11909729404876462702)
XLA Ops:
  13.4 6.5 %all-to-all-start = ((bf16[8,64,1408]{2,1,0:T(8,128)(2,1)}), bf16[8,64,1408]{2,1,0:T(8,128)(2,1)S(1)}, u32[]{:S(2)}, u32[]{:S(2)}) async-start(bf16[8,64,1408]{2,1,0:T(8,128)(2,1)} %fusion.9), calls=%async_computation | async-start | bytes 2883584 | tf_op jit(solution)/shard_map/all_to_all | solution.py:632
  37.7 17.2 %all-to-all-done = bf16[8,64,1408]{2,1,0:T(8,128)(2,1)S(1)} async-done(((bf16[8,64,1408]{2,1,0:T(8,128)(2,1)}), bf16[8,64,1408]{2,1,0:T(8,128)(2,1)S(1)}, u32[]{:S(2)}, u32[]{:S(2)}) %all-to-all-start) | async-done | bytes 1441824 | tf_op jit(solution)/shard_map/all_to_all | solution.py:632
  62.4 13.1 %collective-permute-done = bf16[256,1408]{1,0:T(8,128)(2,1)S(1)} collective-permute-done((bf16[256,1408]{1,0:T(8,128)(2,1)S(1)}, bf16[256,1408]{1,0:T(8,128)(2,1)S(1)}, u32[]{:S(2)}, u32[]{:S(2)}) %collective-permute-start) | collective-permute-done | bytes 720928 | tf_op jit(solution)/shard_map/ppermute | solution.py:430
  79.4 11.5 %collective-permute-done.1 = bf16[256,1408]{1,0:T(8,128)(2,1)S(1)} collective-permute-done((bf16[256,1408]{1,0:T(8,128)(2,1)S(1)}, bf16[256,1408]{1,0:T(8,128)(2,1)S(1)}, u32[]{:S(2)}, u32[]{:S(2)}) %collective-permute-start.1) | collective-permute-done | bytes 720928 | tf_op jit(solution)/shard_map/ppermute | solution.py:430
  94.3 11.9 %collective-permute-done.4 = bf16[256,1408]{1,0:T(8,128)(2,1)S(1)} collective-permute-done((bf16[256,1408]{1,0:T(8,128)(2,1)S(1)}, bf16[256,1408]{1,0:T(8,128)(2,1)S(1)}, u32[]{:S(2)}, u32[]{:S(2)}) %collective-permute-start.4) | collective-permute-done | bytes 720928 | tf_op jit(solution)/shard_map/ppermute | solution.py:430
  112.2 7.8 %collective-permute-done.6.refs_4_ = bf16[512,2048]{1,0:T(8,128)(2,1)} collective-permute-done((bf16[512,2048]{1,0:T(8,128)(2,1)S(1)}, bf16[512,2048]{1,0:T(8,128)(2,1)}, u32[]{:S(2)}, u32[]{:S(2)}) %collective-permute-start.6) | collective-permute-done | bytes 2097184 | tf_op jit(solution)/shard_map/ppermute | solution.py:430
  121.2 14.8 %all-gather.4.cloned.1.call-done.refs_1_ = bf16[2048,2048]{1,0:T(8,128)(2,1)} async-done(((bf16[256,2048]{1,0:T(8,128)(2,1)}), bf16[2048,2048]{1,0:T(8,128)(2,1)}) %all-gather.4.cloned.1.call-update) | async-done | bytes 8388624 | tf_op jit(solution)/shard_map/all_gather | solution.py:658
  136.0 39.1 %mixer_forward.1 = (bf16[2048,1408]{1,0:T(8,128)(2,1)}, bf16[2048,512]{1,0:T(8,128)(2,1)}, f32[8,128,512]{2,1,0:T(8,128)}, f32[8,8,256]{2,1,0:T(8,128)}, f32[2048,768]{1,0:T(8,128)}) custom-call(f32[1,1,512]{2,1,0:T(1,128)} %broadcast_in_dim.51.refs_0_, bf16[2048,2048]{1,0:T(8,128)(2,1)} %all-gather.4.cloned.1.call-done.refs_1_, ...), custom_call_target="tpu_custom_call" | custom-call | flops 1 | bytes 1 | tf_op jit(solution)/shard_map/mixer_forward/pallas_call | solution.py:286
  177.3 6.2 %collective-permute-done.9 = f32[8,256]{1,0:T(8,128)S(1)} collective-permute-done((f32[8,256]{1,0:T(8,128)S(1)}, f32[8,256]{1,0:T(8,128)S(1)}, u32[]{:S(2)}, u32[]{:S(2)}) %collective-permute-start.9) | collective-permute-done | bytes 8224 | tf_op jit(solution)/shard_map/ppermute | solution.py:430
  195.7 9.3 %pair_product.2 = bf16[4,256,2048]{2,1,0:T(8,128)(2,1)} custom-call(s32[2]{0:T(128)} %pad_add_fusion.refs_0_, bf16[2048,512]{1,0:T(8,128)(2,1)} %copy-done, bf16[1024,512]{1,0:T(8,128)(2,1)} %collective-permute-done.11.refs_2_, bf16[512,2048]{1,0:T(8,128)(2,1)} %weight_ref.1, bf16[512,2048]{1,0:T(8,128)(2,1)} %collective-permute-done.6.refs_4_), custom_call_target="tpu_custom_call" | custom-call | flops 1 | bytes 1 | tf_op jit(solution)/shard_map/pair_product/pallas_call | solution.py:509
  205.0 13.6 %all-gather.6.cloned.1.call-done.cot_ref = bf16[2048,2048]{1,0:T(8,128)(2,1)} async-done(((bf16[256,2048]{1,0:T(8,128)(2,1)}), bf16[2048,2048]{1,0:T(8,128)(2,1)}) %all-gather.6.cloned.1.call-update) | async-done | bytes 8388624 | tf_op jit(solution)/shard_map/all_gather | solution.py:699
  218.6 12.4 %pull_back.1 = (f32[2048,512]{1,0:T(8,128)}, f32[8,8,256]{2,1,0:T(8,128)}) custom-call(bf16[2048,2048]{1,0:T(8,128)(2,1)} %all-gather.6.cloned.1.call-done.cot_ref, bf16[512,2048]{1,0:T(8,128)(2,1)} %weight_ref.1, bf16[2048,1408]{1,0:T(8,128)(2,1)} %get-tuple-element.70.gate_ref.refs_1_, bf16[2048,512]{1,0:T(8,128)(2,1)} %get-tuple-element.72.y_ref.refs_3_, ...), custom_call_target="tpu_custom_call" | custom-call | flops 1 | bytes 1 | tf_op jit(solution)/shard_map/pull_back/pallas_call | solution.py:391
  237.7 9.4 %fusion.28 = f32[512,2048]{1,0:T(8,128)} fusion(bf16[2048,512]{1,0:T(8,128)(2,1)S(1)} %copy-done.1, bf16[2048,2048]{1,0:T(8,128)(2,1)} %all-gather.6.cloned.1.call-done.cot_ref), kind=kOutput, calls=%fused_computation.113 | convolution fusion | flops 4294967296 | bytes 14680064 | tf_op jit(solution)/shard_map/dot_general | solution.py:23
  253.0 48.2 %mixer_backward.1 = (bf16[2048,1408]{1,0:T(8,128)(2,1)}, f32[8,768]{1,0:T(8,128)}, f32[8,128]{1,0:T(8,128)}, f32[8,512]{1,0:T(8,128)}) custom-call(f32[1,8,512]{2,1,0:T(8,128)} %maximum_maximum_fusion.1.gain_ref.refs_0_, bf16[2048,1408]{1,0:T(8,128)(2,1)} %get-tuple-element.70.gate_ref.refs_1_, f32[2048,768]{1,0:T(8,128)} %get-tuple-element.71.refs_2_, ...), custom_call_target="tpu_custom_call" | custom-call | flops 1 | bytes 1 | tf_op jit(solution)/shard_map/mixer_backward/pallas_call | solution.py:332
  304.9 5.6 %collective-permute-done.15.refs_2_ = bf16[1024,1408]{1,0:T(8,128)(2,1)} collective-permute-done((bf16[1024,1408]{1,0:T(8,128)(2,1)}, bf16[1024,1408]{1,0:T(8,128)(2,1)}, u32[]{:S(2)}, u32[]{:S(2)}) %collective-permute-start.15) | collective-permute-done | bytes 2883616 | tf_op jit(solution)/shard_map/ppermute | solution.py:430
  310.5 22.8 %pair_product.3 = (bf16[256,2048]{1,0:T(8,128)(2,1)}, bf16[256,2048]{1,0:T(8,128)(2,1)}, bf16[256,2048]{1,0:T(8,128)(2,1)}, bf16[256,2048]{1,0:T(8,128)(2,1)}) custom-call(s32[2]{0:T(128)} %pad_add_fusion.refs_0_, bf16[2048,1408]{1,0:T(8,128)(2,1)} %get-tuple-element.92.refs_1_, bf16[1024,1408]{1,0:T(8,128)(2,1)} %collective-permute-done.15.refs_2_, ...), custom_call_target="tpu_custom_call" | custom-call | flops 1 | bytes 1 | tf_op jit(solution)/shard_map/pair_product/pallas_call | solution.py:509
  333.3 11.9 %all-to-all-done.1 = bf16[4,256,2048]{2,1,0:T(8,128)(2,1)} async-done(((bf16[4,256,2048]{2,1,0:T(8,128)(2,1)}), bf16[4,256,2048]{2,1,0:T(8,128)(2,1)}, u32[]{:S(2)}, u32[]{:S(2)}) %all-to-all-start.1) | async-done | bytes 4194336 | tf_op jit(solution)/shard_map/all_to_all | solution.py:487
  345.4 18.8 %fusion.27 = (bf16[2048,1408]{1,0:T(8,128)(2,1)S(1)}, f32[2048,1408]{1,0:T(8,128)}) fusion(bf16[2048,2048]{1,0:T(8,128)(2,1)} %all-gather.4.cloned.1.call-done.refs_1_, bf16[2048,1408]{1,0:T(8,128)(2,1)} %get-tuple-element.92.refs_1_), kind=kOutput, calls=%fused_computation.112 | convolution fusion | flops 11814043648 | bytes 31457280 | tf_op jit(solution)/shard_map/dot_general | solution.py:23
  374.6 44.3 %collective-permute-done.19 = bf16[256,2048]{1,0:T(8,128)(2,1)} collective-permute-done((bf16[256,2048]{1,0:T(8,128)(2,1)S(1)}, bf16[256,2048]{1,0:T(8,128)(2,1)}, u32[]{:S(2)}, u32[]{:S(2)}) %collective-permute-start.19) | collective-permute-done | bytes 1048608 | tf_op jit(solution)/shard_map/ppermute | solution.py:482
  427.3 13.7 %collective-permute-done.20 = bf16[256,1408]{1,0:T(8,128)(2,1)S(1)} collective-permute-done((bf16[256,1408]{1,0:T(8,128)(2,1)}, bf16[256,1408]{1,0:T(8,128)(2,1)S(1)}, u32[]{:S(2)}, u32[]{:S(2)}) %collective-permute-start.20) | collective-permute-done | bytes 720928 | tf_op jit(solution)/shard_map/ppermute | solution.py:430
  474.9 6.6 %keep.1 = f32[512,2048]{1,0:T(8,128)} custom-call(f32[512,2048]{1,0:T(8,128)} %all-gather.8.cloned.1.call-done.in_ref), custom_call_target="tpu_custom_call" | custom-call | flops 1 | bytes 1 | tf_op jit(solution)/shard_map/keep/pallas_call | solution.py:555
  521.4 6.2 %collective-permute-done.31.refs_3_ = bf16[32,8512]{1,0:T(8,128)(2,1)S(1)} collective-permute-done((bf16[32,8512]{1,0:T(8,128)(2,1)}, bf16[32,8512]{1,0:T(8,128)(2,1)S(1)}, u32[]{:S(2)}, u32[]{:S(2)}) %collective-permute-start.31) | collective-permute-done | bytes 544800 | tf_op jit(solution)/shard_map/ppermute | solution.py:430
  528.2 10.0 %collective-permute-done.34.refs_6_ = bf16[32,8512]{1,0:T(8,128)(2,1)S(1)} collective-permute-done((bf16[32,8512]{1,0:T(8,128)(2,1)}, bf16[32,8512]{1,0:T(8,128)(2,1)S(1)}, u32[]{:S(2)}, u32[]{:S(2)}) %collective-permute-start.34) | collective-permute-done | bytes 544800 | tf_op jit(solution)/shard_map/ppermute | solution.py:430
  539.2 8.1 %assemble.1 = f32[8512,256]{1,0:T(8,128)} custom-call(s32[1]{0:T(128)} %bitcast.47.place_ref, bf16[32,8512]{1,0:T(8,128)(2,1)} %get-tuple-element.170.refs_0_, bf16[32,8512]{1,0:T(8,128)(2,1)} %get-tuple-element.169.refs_1_, bf16[32,8512]{1,0:T(8,128)(2,1)} %collective-permute-done.30.refs_2_, bf16[32,8512]{1,0:T(8,128)(2,1)} %copy-done.22, ...), custom_call_target="tpu_custom_call" | custom-call | flops 1 | bytes 31457280 | tf_op jit(solution)/shard_map/assemble/pallas_call | solution.py:580
  (297 shorter events, 169.6 us)
Async XLA Ops:
  13.4 41.5 %all-to-all-start = ((bf16[8,64,1408]{2,1,0:T(8,128)(2,1)}), bf16[8,64,1408]{2,1,0:T(8,128)(2,1)S(1)}, u32[]{:S(2)}, u32[]{:S(2)}) async-start(bf16[8,64,1408]{2,1,0:T(8,128)(2,1)} %fusion.9), calls=%async_computation | async-start | bytes 2883584 | tf_op jit(solution)/shard_map/all_to_all | solution.py:632
  19.8 116.2 %all-gather.4.cloned.1.call-start = ((), (), s32[]{:S(2)}) async-start(), calls=%async_computation.4 | async-start | bytes 9437184 | tf_op jit(solution)/shard_map/all_gather | solution.py:658
  54.9 163.7 %all-gather.6.cloned.1.call-start = ((), (), s32[]{:S(2)}) async-start(), calls=%async_computation.5 | async-start | bytes 9437184 | tf_op jit(solution)/shard_map/all_gather | solution.py:699
  55.6 245.6 %reduce-scatter.2.cloned.1.call-start = ((), (), s32[]{:S(2)}) async-start(), calls=%async_computation.6 | async-start | bytes 5242880 | tf_op jit(solution)/shard_map/reduce_scatter | solution.py:734
  56.3 19.1 %collective-permute-start = (bf16[256,1408]{1,0:T(8,128)(2,1)S(1)}, bf16[256,1408]{1,0:T(8,128)(2,1)S(1)}, u32[]{:S(2)}, u32[]{:S(2)}) collective-permute-start(bf16[256,1408]{1,0:T(8,128)(2,1)S(1)} %bitcast.100), channel_id=1, source_target_pairs={{0,8},{8,0},{16,24},{24,16},{1,9},{9,1},{17,25},{25,17},{2,10},{10... | collective-permute-start | bytes 2162696 | tf_op jit(solution)/shard_map/ppermute | solution.py:430
  57.9 19.1 %collective-permute-start.3 = (bf16[256,1408]{1,0:T(8,128)(2,1)S(1)}, bf16[256,1408]{1,0:T(8,128)(2,1)S(1)}, u32[]{:S(2)}, u32[]{:S(2)}) collective-permute-start(bf16[256,1408]{1,0:T(8,128)(2,1)S(1)} %bitcast.103), channel_id=1, source_target_pairs={{0,16},{8,24},{16,0},{24,8},{1,17},{9,25},{17,1},{25,9},{2,18},{10... | collective-permute-start | bytes 2162696 | tf_op jit(solution)/shard_map/ppermute | solution.py:430
  59.4 31.5 %collective-permute-start.1 = (bf16[256,1408]{1,0:T(8,128)(2,1)S(1)}, bf16[256,1408]{1,0:T(8,128)(2,1)S(1)}, u32[]{:S(2)}, u32[]{:S(2)}) collective-permute-start(bf16[256,1408]{1,0:T(8,128)(2,1)S(1)} %bitcast.104), channel_id=1, source_target_pairs={{0,8},{8,0},{16,24},{24,16},{1,9},{9,1},{17,25},{25,17},{2,10},{10... | collective-permute-start | bytes 2162696 | tf_op jit(solution)/shard_map/ppermute | solution.py:430
  59.9 32.5 %collective-permute-start.2 = (bf16[256,1408]{1,0:T(8,128)(2,1)S(1)}, bf16[256,1408]{1,0:T(8,128)(2,1)S(1)}, u32[]{:S(2)}, u32[]{:S(2)}) collective-permute-start(bf16[256,1408]{1,0:T(8,128)(2,1)S(1)} %bitcast.101), channel_id=1, source_target_pairs={{0,16},{8,24},{16,0},{24,8},{1,17},{9,25},{17,1},{25,9},{2,18},{10... | collective-permute-start | bytes 2162696 | tf_op jit(solution)/shard_map/ppermute | solution.py:430
  75.5 30.7 %collective-permute-start.4 = (bf16[256,1408]{1,0:T(8,128)(2,1)S(1)}, bf16[256,1408]{1,0:T(8,128)(2,1)S(1)}, u32[]{:S(2)}, u32[]{:S(2)}) collective-permute-start(bf16[256,1408]{1,0:T(8,128)(2,1)S(1)} %collective-permute-done), channel_id=1, source_target_pairs={{0,16},{8,24},{16,0},{24,8},{1,17},{9,25},{17,1},{25,9},{2,18},{10... | collective-permute-start | bytes 2162696 | tf_op jit(solution)/shard_map/ppermute | solution.py:430
  77.0 30.1 %collective-permute-start.5 = (bf16[256,1408]{1,0:T(8,128)(2,1)S(1)}, bf16[256,1408]{1,0:T(8,128)(2,1)S(1)}, u32[]{:S(2)}, u32[]{:S(2)}) collective-permute-start(bf16[256,1408]{1,0:T(8,128)(2,1)S(1)} %collective-permute-done.3), channel_id=1, source_target_pairs={{0,8},{8,0},{16,24},{24,16},{1,9},{9,1},{17,25},{25,17},{2,10},{10... | collective-permute-start | bytes 2162696 | tf_op jit(solution)/shard_map/ppermute | solution.py:430
  247.9 97.4 %all-to-all-start.1 = ((bf16[4,256,2048]{2,1,0:T(8,128)(2,1)}), bf16[4,256,2048]{2,1,0:T(8,128)(2,1)}, u32[]{:S(2)}, u32[]{:S(2)}) async-start(bf16[4,256,2048]{2,1,0:T(8,128)(2,1)} %pair_product.2), calls=%async_computation.2 | async-start | bytes 8388608 | tf_op jit(solution)/shard_map/all_to_all | solution.py:487
  252.8 118.9 %all-gather.8.cloned.1.call-start = ((), (), s32[]{:S(2)}) async-start(), calls=%async_computation.7 | async-start | bytes 5242880 | tf_op jit(solution)/shard_map/all_gather | solution.py:750
  345.2 26.4 %collective-permute-start.16 = (bf16[256,2048]{1,0:T(8,128)(2,1)}, bf16[256,2048]{1,0:T(8,128)(2,1)}, u32[]{:S(2)}, u32[]{:S(2)}) collective-permute-start(bf16[256,2048]{1,0:T(8,128)(2,1)} %get-tuple-element.94), channel_id=1, source_target_pairs={{0,2},{1,3},{2,4},{3,5},{4,6},{5,7},{6,0},{7,1},{8,10},{9,11},{10,... | collective-permute-start | bytes 3145736 | tf_op jit(solution)/shard_map/ppermute | solution.py:482
  371.6 47.2 %collective-permute-start.17 = (bf16[512,1408]{1,0:T(8,128)(2,1)}, bf16[512,1408]{1,0:T(8,128)(2,1)S(1)}, u32[]{:S(2)}, u32[]{:S(2)}) collective-permute-start(bf16[512,1408]{1,0:T(8,128)(2,1)} %pad_maximum_fusion.1), channel_id=1, source_target_pairs={{0,8},{8,0},{16,24},{24,16},{1,9},{9,1},{17,25},{25,17},{2,10},{10... | collective-permute-start | bytes 4325384 | tf_op jit(solution)/shard_map/ppermute | solution.py:430
  373.1 45.8 %collective-permute-start.18 = (bf16[512,1408]{1,0:T(8,128)(2,1)}, bf16[512,1408]{1,0:T(8,128)(2,1)S(1)}, u32[]{:S(2)}, u32[]{:S(2)}) collective-permute-start(bf16[512,1408]{1,0:T(8,128)(2,1)} %pad_maximum_fusion.2), channel_id=1, source_target_pairs={{0,16},{8,24},{16,0},{24,8},{1,17},{9,25},{17,1},{25,9},{2,18},{10... | collective-permute-start | bytes 4325384 | tf_op jit(solution)/shard_map/ppermute | solution.py:430
  374.6 44.3 %collective-permute-start.19 = (bf16[256,2048]{1,0:T(8,128)(2,1)S(1)}, bf16[256,2048]{1,0:T(8,128)(2,1)}, u32[]{:S(2)}, u32[]{:S(2)}) collective-permute-start(bf16[256,2048]{1,0:T(8,128)(2,1)S(1)} %copy-done.39), channel_id=1, source_target_pairs={{0,4},{1,5},{2,6},{3,7},{4,0},{5,1},{6,2},{7,3},{8,12},{9,13},{10,... | collective-permute-start | bytes 3145736 | tf_op jit(solution)/shard_map/ppermute | solution.py:482
  422.7 18.3 %collective-permute-start.20 = (bf16[256,1408]{1,0:T(8,128)(2,1)}, bf16[256,1408]{1,0:T(8,128)(2,1)S(1)}, u32[]{:S(2)}, u32[]{:S(2)}) collective-permute-start(bf16[256,1408]{1,0:T(8,128)(2,1)} %get-tuple-element.103), channel_id=1, source_target_pairs={{0,16},{8,24},{16,0},{24,8},{1,17},{9,25},{17,1},{25,9},{2,18},{10... | collective-permute-start | bytes 2162696 | tf_op jit(solution)/shard_map/ppermute | solution.py:430
  423.2 18.1 %collective-permute-start.21 = (bf16[256,1408]{1,0:T(8,128)(2,1)}, bf16[256,1408]{1,0:T(8,128)(2,1)}, u32[]{:S(2)}, u32[]{:S(2)}) collective-permute-start(bf16[256,1408]{1,0:T(8,128)(2,1)} %get-tuple-element.104), channel_id=1, source_target_pairs={{0,8},{8,0},{16,24},{24,16},{1,9},{9,1},{17,25},{25,17},{2,10},{10... | collective-permute-start | bytes 2162696 | tf_op jit(solution)/shard_map/ppermute | solution.py:430
  425.1 24.8 %collective-permute-start.22 = (bf16[256,2048]{1,0:T(8,128)(2,1)}, bf16[256,2048]{1,0:T(8,128)(2,1)S(1)}, u32[]{:S(2)}, u32[]{:S(2)}) collective-permute-start(bf16[256,2048]{1,0:T(8,128)(2,1)} %get-tuple-element.111), channel_id=1, source_target_pairs={{0,6},{1,7},{2,0},{3,1},{4,2},{5,3},{6,4},{7,5},{8,14},{9,15},{10,... | collective-permute-start | bytes 3145736 | tf_op jit(solution)/shard_map/ppermute | solution.py:482
  451.0 39.1 %all-to-all-start.2 = ((bf16[8,64,1408]{2,1,0:T(8,128)(2,1)}), bf16[8,64,1408]{2,1,0:T(8,128)(2,1)S(1)}, u32[]{:S(2)}, u32[]{:S(2)}) async-start(bf16[8,64,1408]{2,1,0:T(8,128)(2,1)} %bitcast.93), calls=%async_computation.3 | async-start | bytes 2883584 | tf_op jit(solution)/shard_map/all_to_all | solution.py:731
  495.7 20.9 %collective-permute-start.30 = (bf16[32,8512]{1,0:T(8,128)(2,1)}, bf16[32,8512]{1,0:T(8,128)(2,1)}, u32[]{:S(2)}, u32[]{:S(2)}) collective-permute-start(bf16[32,8512]{1,0:T(8,128)(2,1)} %get-tuple-element.170.refs_0_), channel_id=1, source_target_pairs={{0,8},{8,0},{16,24},{24,16},{1,9},{9,1},{17,25},{25,17},{2,10},{10... | collective-permute-start | bytes 1634312 | tf_op jit(solution)/shard_map/ppermute | solution.py:430
  497.1 20.6 %collective-permute-start.33 = (bf16[32,8512]{1,0:T(8,128)(2,1)}, bf16[32,8512]{1,0:T(8,128)(2,1)}, u32[]{:S(2)}, u32[]{:S(2)}) collective-permute-start(bf16[32,8512]{1,0:T(8,128)(2,1)} %get-tuple-element.169.refs_1_), channel_id=1, source_target_pairs={{0,16},{8,24},{16,0},{24,8},{1,17},{9,25},{17,1},{25,9},{2,18},{10... | collective-permute-start | bytes 1634312 | tf_op jit(solution)/shard_map/ppermute | solution.py:430
  516.6 21.6 %collective-permute-start.34 = (bf16[32,8512]{1,0:T(8,128)(2,1)}, bf16[32,8512]{1,0:T(8,128)(2,1)S(1)}, u32[]{:S(2)}, u32[]{:S(2)}) collective-permute-start(bf16[32,8512]{1,0:T(8,128)(2,1)} %collective-permute-done.30.refs_2_), channel_id=1, source_target_pairs={{0,16},{8,24},{16,0},{24,8},{1,17},{9,25},{17,1},{25,9},{2,18},{10... | collective-permute-start | bytes 1634312 | tf_op jit(solution)/shard_map/ppermute | solution.py:430
  517.7 20.4 %collective-permute-start.35 = (bf16[32,8512]{1,0:T(8,128)(2,1)}, bf16[32,8512]{1,0:T(8,128)(2,1)S(1)}, u32[]{:S(2)}, u32[]{:S(2)}) collective-permute-start(bf16[32,8512]{1,0:T(8,128)(2,1)} %collective-permute-done.33.refs_5_), channel_id=1, source_target_pairs={{0,8},{8,0},{16,24},{24,16},{1,9},{9,1},{17,25},{25,17},{2,10},{10... | collective-permute-start | bytes 1634312 | tf_op jit(solution)/shard_map/ppermute | solution.py:430
  (61 other events, 484.8 us)
Sparse Core Ops, SparseCore 0:
  55.0 80.9 all-gather.3
  137.6 80.9 all-gather.5
  248.0 52.3 reduce-scatter.1
  305.0 54.1 all-gather.7

commit v6 on v5

--- a/solution.py
+++ b/solution.py
@@ -376,7 +376,7 @@
 
 
 def pull_kernel(cot_ref, weight_ref, gate_ref, y_ref, gain_ref, d_normed_ref, dot_ref):
-    d_normed = mm(cot_ref[...], weight_ref[...], NT)
+    d_normed = mm(cot_ref[...], weight_ref[...])
     d_normed_ref[...] = d_normed
     gate = gate_ref[...].astype(F32)
     gated = y_ref[...].astype(F32) * (gate * jax.nn.sigmoid(gate))
@@ -393,7 +393,7 @@
         grid=(seqs, blocks),
         in_specs=[
             pl.BlockSpec((BLOCK, depth), row),
-            pl.BlockSpec((width, depth), lambda s, c: (0, 0)),
+            pl.BlockSpec((depth, width), lambda s, c: (0, 0)),
             pl.BlockSpec((BLOCK, width), lambda s, c: (s * blocks + c, gate_place)),
             pl.BlockSpec((BLOCK, width), row),
             pl.BlockSpec((1, 8, width), lambda s, c: (s, 0, 0)),
@@ -680,6 +680,8 @@
     if line:
         sibling_out, sibling_weight = swap(out_weight, "mp", 1), swap(weight, "mp", 1)
         weight, sibling_out, sibling_weight = lax.optimization_barrier((weight, sibling_out, sibling_weight))
+    out_turned = pad_rows(out_weight, width).T
+    weight, out_turned = lax.optimization_barrier((weight, out_turned))
     projected, y_all, states, squares, pre = mixer_forward(
         mask, hidden, weight, taps, head_params, skip, state_dim, width
     )
@@ -714,8 +716,7 @@
         ],
         axis=1,
     )
-    out_padded = pad_rows(out_weight, width)
-    d_normed, dots = pull_back(cot_all, out_padded, projected, y_all, gains, 0)
+    d_normed, dots = pull_back(cot_all, out_turned, projected, y_all, gains, 0)
     dot_rows = all_sum(dots[:, 0, :], "mp")
     out_part = mm(normed_out, cot_all, TN)
     if line:

time: 560 us -> 560 us (level)
    unnamed x97 -> x98, local copies, waits for them, and re-layouts: 12.8 us -> 15.4 us
  transfers between devices with their start and end apart: 43 -> 43, of which waited for: 29 -> 29; matrix products, arithmetic and copies ran while one was open for 19% -> 20% of each run, Pallas kernels for 23% -> 23%
where the time goes in v6:
time: 560 us; the launch traced here: 554 us
  waiting for transfers between devices  219 us (39%)
  Pallas kernels  146 us (26%)
  local copies, waits for them, and re-layouts  63.2 us (11%)
  starting transfers between devices  44.9 us (8%)
  other arithmetic  35.9 us (6%)
  matrix products  28.2 us (5%)
  between operations  15.6 us (3%)
    ppermute x33, waiting for transfers between devices, swap(): lax.ppermute(value, axis, [(place, place ^ bit) for place in range(size)])  107 us
    ppermute x3, waiting for transfers between devices, line_permute(): return lax.ppermute(block, 'mp', pairs)  54 us
    pallas_call x1, Pallas kernels, mixer_backward(): pl.pallas_call(lambda *refs: backward_kernel(*refs, state_dim=state_dim,...  48.3 us
    pallas_call x1, Pallas kernels, mixer_forward(): pl.pallas_call(lambda *refs: forward_kernel(*refs, state_dim=state_dim, w...  39.1 us
    pallas_call x2, Pallas kernels, pair_product(): pl.pallas_call(lambda *refs: pair_kernel(*refs, dims=dims), grid_spec=plt...  32.1 us
    dot_general x2, matrix products, mm(): return lax.dot_general(left, right, dims, preferred_element_type=F32)  28.2 us
    ppermute x33, starting transfers between devices, swap(): lax.ppermute(value, axis, [(place, place ^ bit) for place in range(size)])  27.5 us
    all_to_all x1, waiting for transfers between devices, on_device(): got = lax.all_to_all(send, 'mp', split_axis=0, concat_axis=0, tiled=True)  17.2 us
  transfers between devices with their start and end apart: 43, of which 29 were waited for; matrix products, arithmetic and copies ran while one was open for 20% of the time, Pallas kernels for 23%

profile of v6, /device:TPU:0, one launch (start us, length us, event | category | flops | bytes accessed | tf_op | source)
XLA Modules:
  0.0 553.5 jit_solution(8250968859347323774)
XLA Ops:
  13.4 6.5 %all-to-all-start = ((bf16[8,64,1408]{2,1,0:T(8,128)(2,1)}), bf16[8,64,1408]{2,1,0:T(8,128)(2,1)S(1)}, u32[]{:S(2)}, u32[]{:S(2)}) async-start(bf16[8,64,1408]{2,1,0:T(8,128)(2,1)} %fusion.9), calls=%async_computation | async-start | bytes 2883584 | tf_op jit(solution)/shard_map/all_to_all | solution.py:632
  37.6 17.2 %all-to-all-done = bf16[8,64,1408]{2,1,0:T(8,128)(2,1)S(1)} async-done(((bf16[8,64,1408]{2,1,0:T(8,128)(2,1)}), bf16[8,64,1408]{2,1,0:T(8,128)(2,1)S(1)}, u32[]{:S(2)}, u32[]{:S(2)}) %all-to-all-start) | async-done | bytes 1441824 | tf_op jit(solution)/shard_map/all_to_all | solution.py:632
  62.0 13.1 %collective-permute-done = bf16[256,1408]{1,0:T(8,128)(2,1)S(1)} collective-permute-done((bf16[256,1408]{1,0:T(8,128)(2,1)S(1)}, bf16[256,1408]{1,0:T(8,128)(2,1)S(1)}, u32[]{:S(2)}, u32[]{:S(2)}) %collective-permute-start) | collective-permute-done | bytes 720928 | tf_op jit(solution)/shard_map/ppermute | solution.py:430
  79.0 11.5 %collective-permute-done.1 = bf16[256,1408]{1,0:T(8,128)(2,1)S(1)} collective-permute-done((bf16[256,1408]{1,0:T(8,128)(2,1)S(1)}, bf16[256,1408]{1,0:T(8,128)(2,1)S(1)}, u32[]{:S(2)}, u32[]{:S(2)}) %collective-permute-start.1) | collective-permute-done | bytes 720928 | tf_op jit(solution)/shard_map/ppermute | solution.py:430
  93.9 11.9 %collective-permute-done.4 = bf16[256,1408]{1,0:T(8,128)(2,1)S(1)} collective-permute-done((bf16[256,1408]{1,0:T(8,128)(2,1)S(1)}, bf16[256,1408]{1,0:T(8,128)(2,1)S(1)}, u32[]{:S(2)}, u32[]{:S(2)}) %collective-permute-start.4) | collective-permute-done | bytes 720928 | tf_op jit(solution)/shard_map/ppermute | solution.py:430
  120.9 15.1 %all-gather.4.cloned.1.call-done.refs_1_ = bf16[2048,2048]{1,0:T(8,128)(2,1)} async-done(((bf16[256,2048]{1,0:T(8,128)(2,1)}), bf16[2048,2048]{1,0:T(8,128)(2,1)}) %all-gather.4.cloned.1.call-update) | async-done | bytes 8388624 | tf_op jit(solution)/shard_map/all_gather | solution.py:658
  136.0 39.1 %mixer_forward.1 = (bf16[2048,1408]{1,0:T(8,128)(2,1)}, bf16[2048,512]{1,0:T(8,128)(2,1)}, f32[8,128,512]{2,1,0:T(8,128)}, f32[8,8,256]{2,1,0:T(8,128)}, f32[2048,768]{1,0:T(8,128)}) custom-call(f32[1,1,512]{2,1,0:T(1,128)} %broadcast_in_dim.51.refs_0_, bf16[2048,2048]{1,0:T(8,128)(2,1)} %all-gather.4.cloned.1.call-done.refs_1_, ...), custom_call_target="tpu_custom_call" | custom-call | flops 1 | bytes 1 | tf_op jit(solution)/shard_map/mixer_forward/pallas_call | solution.py:286
  177.3 6.2 %collective-permute-done.9 = f32[8,256]{1,0:T(8,128)S(1)} collective-permute-done((f32[8,256]{1,0:T(8,128)S(1)}, f32[8,256]{1,0:T(8,128)S(1)}, u32[]{:S(2)}, u32[]{:S(2)}) %collective-permute-start.9) | collective-permute-done | bytes 8224 | tf_op jit(solution)/shard_map/ppermute | solution.py:430
  195.7 9.3 %pair_product.2 = bf16[4,256,2048]{2,1,0:T(8,128)(2,1)} custom-call(s32[2]{0:T(128)} %pad_add_fusion.refs_0_, bf16[2048,512]{1,0:T(8,128)(2,1)} %copy-done, bf16[1024,512]{1,0:T(8,128)(2,1)} %collective-permute-done.11.refs_2_, bf16[512,2048]{1,0:T(8,128)(2,1)} %refs_3_.1, bf16[512,2048]{1,0:T(8,128)(2,1)} %collective-permute-done.6.refs_4_), custom_call_target="tpu_custom_call" | custom-call | flops 1 | bytes 1 | tf_op jit(solution)/shard_map/pair_product/pallas_call | solution.py:509
  205.0 13.6 %all-gather.6.cloned.1.call-done.cot_ref = bf16[2048,2048]{1,0:T(8,128)(2,1)} async-done(((bf16[256,2048]{1,0:T(8,128)(2,1)}), bf16[2048,2048]{1,0:T(8,128)(2,1)}) %all-gather.6.cloned.1.call-update) | async-done | bytes 8388624 | tf_op jit(solution)/shard_map/all_gather | solution.py:701
  218.6 12.3 %pull_back.1 = (f32[2048,512]{1,0:T(8,128)}, f32[8,8,256]{2,1,0:T(8,128)}) custom-call(bf16[2048,2048]{1,0:T(8,128)(2,1)} %all-gather.6.cloned.1.call-done.cot_ref, bf16[2048,512]{1,0:T(8,128)(2,1)} %bitcast.94, bf16[2048,1408]{1,0:T(8,128)(2,1)} %get-tuple-element.73.gate_ref.refs_1_, bf16[2048,512]{1,0:T(8,128)(2,1)} %get-tuple-element.75.y_ref.refs_3_, ...), custom_call_target="tpu_custom_call" | custom-call | flops 1 | bytes 1 | tf_op jit(solution)/shard_map/pull_back/pallas_call | solution.py:391
  237.6 9.4 %fusion.28 = f32[512,2048]{1,0:T(8,128)} fusion(bf16[2048,512]{1,0:T(8,128)(2,1)S(1)} %copy-done.1, bf16[2048,2048]{1,0:T(8,128)(2,1)} %all-gather.6.cloned.1.call-done.cot_ref), kind=kOutput, calls=%fused_computation.113 | convolution fusion | flops 4294967296 | bytes 14680064 | tf_op jit(solution)/shard_map/dot_general | solution.py:23
  247.7 4.9 all-to-all-start.1
  252.9 48.3 %mixer_backward.1 = (bf16[2048,1408]{1,0:T(8,128)(2,1)}, f32[8,768]{1,0:T(8,128)}, f32[8,128]{1,0:T(8,128)}, f32[8,512]{1,0:T(8,128)}) custom-call(f32[1,8,512]{2,1,0:T(8,128)} %maximum_maximum_fusion.1.gain_ref.refs_0_, bf16[2048,1408]{1,0:T(8,128)(2,1)} %get-tuple-element.73.gate_ref.refs_1_, f32[2048,768]{1,0:T(8,128)} %get-tuple-element.74.refs_2_, ...), custom_call_target="tpu_custom_call" | custom-call | flops 1 | bytes 1 | tf_op jit(solution)/shard_map/mixer_backward/pallas_call | solution.py:332
  304.8 5.6 %collective-permute-done.15.refs_2_ = bf16[1024,1408]{1,0:T(8,128)(2,1)} collective-permute-done((bf16[1024,1408]{1,0:T(8,128)(2,1)}, bf16[1024,1408]{1,0:T(8,128)(2,1)}, u32[]{:S(2)}, u32[]{:S(2)}) %collective-permute-start.15) | collective-permute-done | bytes 2883616 | tf_op jit(solution)/shard_map/ppermute | solution.py:430
  310.4 22.8 %pair_product.3 = (bf16[256,2048]{1,0:T(8,128)(2,1)}, bf16[256,2048]{1,0:T(8,128)(2,1)}, bf16[256,2048]{1,0:T(8,128)(2,1)}, bf16[256,2048]{1,0:T(8,128)(2,1)}) custom-call(s32[2]{0:T(128)} %pad_add_fusion.refs_0_, bf16[2048,1408]{1,0:T(8,128)(2,1)} %get-tuple-element.96.refs_1_, bf16[1024,1408]{1,0:T(8,128)(2,1)} %collective-permute-done.15.refs_2_, ...), custom_call_target="tpu_custom_call" | custom-call | flops 1 | bytes 1 | tf_op jit(solution)/shard_map/pair_product/pallas_call | solution.py:509
  333.2 11.9 %all-to-all-done.1 = bf16[4,256,2048]{2,1,0:T(8,128)(2,1)} async-done(((bf16[4,256,2048]{2,1,0:T(8,128)(2,1)}), bf16[4,256,2048]{2,1,0:T(8,128)(2,1)}, u32[]{:S(2)}, u32[]{:S(2)}) %all-to-all-start.1) | async-done | bytes 4194336 | tf_op jit(solution)/shard_map/all_to_all | solution.py:487
  345.1 18.7 %fusion.27 = (bf16[2048,1408]{1,0:T(8,128)(2,1)S(1)}, f32[2048,1408]{1,0:T(8,128)}) fusion(bf16[2048,2048]{1,0:T(8,128)(2,1)} %all-gather.4.cloned.1.call-done.refs_1_, bf16[2048,1408]{1,0:T(8,128)(2,1)} %get-tuple-element.96.refs_1_), kind=kOutput, calls=%fused_computation.112 | convolution fusion | flops 11814043648 | bytes 31457280 | tf_op jit(solution)/shard_map/dot_general | solution.py:23
  374.3 44.3 %collective-permute-done.19 = bf16[256,2048]{1,0:T(8,128)(2,1)} collective-permute-done((bf16[256,2048]{1,0:T(8,128)(2,1)S(1)}, bf16[256,2048]{1,0:T(8,128)(2,1)}, u32[]{:S(2)}, u32[]{:S(2)}) %collective-permute-start.19) | collective-permute-done | bytes 1048608 | tf_op jit(solution)/shard_map/ppermute | solution.py:482
  427.0 13.6 %collective-permute-done.20 = bf16[256,1408]{1,0:T(8,128)(2,1)S(1)} collective-permute-done((bf16[256,1408]{1,0:T(8,128)(2,1)}, bf16[256,1408]{1,0:T(8,128)(2,1)S(1)}, u32[]{:S(2)}, u32[]{:S(2)}) %collective-permute-start.20) | collective-permute-done | bytes 720928 | tf_op jit(solution)/shard_map/ppermute | solution.py:430
  474.6 6.6 %keep.1 = f32[512,2048]{1,0:T(8,128)} custom-call(f32[512,2048]{1,0:T(8,128)} %all-gather.8.cloned.1.call-done.in_ref), custom_call_target="tpu_custom_call" | custom-call | flops 1 | bytes 1 | tf_op jit(solution)/shard_map/keep/pallas_call | solution.py:555
  520.1 6.7 %collective-permute-done.31.refs_3_ = bf16[32,8512]{1,0:T(8,128)(2,1)S(1)} collective-permute-done((bf16[32,8512]{1,0:T(8,128)(2,1)}, bf16[32,8512]{1,0:T(8,128)(2,1)S(1)}, u32[]{:S(2)}, u32[]{:S(2)}) %collective-permute-start.31) | collective-permute-done | bytes 544800 | tf_op jit(solution)/shard_map/ppermute | solution.py:430
  527.7 9.7 %collective-permute-done.34.refs_6_ = bf16[32,8512]{1,0:T(8,128)(2,1)S(1)} collective-permute-done((bf16[32,8512]{1,0:T(8,128)(2,1)}, bf16[32,8512]{1,0:T(8,128)(2,1)S(1)}, u32[]{:S(2)}, u32[]{:S(2)}) %collective-permute-start.34) | collective-permute-done | bytes 544800 | tf_op jit(solution)/shard_map/ppermute | solution.py:430
  538.4 8.1 %assemble.1 = f32[8512,256]{1,0:T(8,128)} custom-call(s32[1]{0:T(128)} %bitcast.48.place_ref, bf16[32,8512]{1,0:T(8,128)(2,1)} %get-tuple-element.174.refs_0_, bf16[32,8512]{1,0:T(8,128)(2,1)} %get-tuple-element.173.refs_1_, bf16[32,8512]{1,0:T(8,128)(2,1)} %collective-permute-done.30.refs_2_, bf16[32,8512]{1,0:T(8,128)(2,1)} %copy-done.22, ...), custom_call_target="tpu_custom_call" | custom-call | flops 1 | bytes 31457280 | tf_op jit(solution)/shard_map/assemble/pallas_call | solution.py:580
  (298 shorter events, 171.4 us)
Async XLA Ops:
  13.4 41.5 %all-to-all-start = ((bf16[8,64,1408]{2,1,0:T(8,128)(2,1)}), bf16[8,64,1408]{2,1,0:T(8,128)(2,1)S(1)}, u32[]{:S(2)}, u32[]{:S(2)}) async-start(bf16[8,64,1408]{2,1,0:T(8,128)(2,1)} %fusion.9), calls=%async_computation | async-start | bytes 2883584 | tf_op jit(solution)/shard_map/all_to_all | solution.py:632
  19.8 116.2 %all-gather.4.cloned.1.call-start = ((), (), s32[]{:S(2)}) async-start(), calls=%async_computation.4 | async-start | bytes 9437184 | tf_op jit(solution)/shard_map/all_gather | solution.py:658
  54.9 163.7 %all-gather.6.cloned.1.call-start = ((), (), s32[]{:S(2)}) async-start(), calls=%async_computation.5 | async-start | bytes 9437184 | tf_op jit(solution)/shard_map/all_gather | solution.py:701
  55.6 245.5 %reduce-scatter.2.cloned.1.call-start = ((), (), s32[]{:S(2)}) async-start(), calls=%async_computation.6 | async-start | bytes 5242880 | tf_op jit(solution)/shard_map/reduce_scatter | solution.py:735
  56.0 19.1 %collective-permute-start = (bf16[256,1408]{1,0:T(8,128)(2,1)S(1)}, bf16[256,1408]{1,0:T(8,128)(2,1)S(1)}, u32[]{:S(2)}, u32[]{:S(2)}) collective-permute-start(bf16[256,1408]{1,0:T(8,128)(2,1)S(1)} %bitcast.102), channel_id=1, source_target_pairs={{0,8},{8,0},{16,24},{24,16},{1,9},{9,1},{17,25},{25,17},{2,10},{10... | collective-permute-start | bytes 2162696 | tf_op jit(solution)/shard_map/ppermute | solution.py:430
  57.5 19.1 %collective-permute-start.3 = (bf16[256,1408]{1,0:T(8,128)(2,1)S(1)}, bf16[256,1408]{1,0:T(8,128)(2,1)S(1)}, u32[]{:S(2)}, u32[]{:S(2)}) collective-permute-start(bf16[256,1408]{1,0:T(8,128)(2,1)S(1)} %bitcast.105), channel_id=1, source_target_pairs={{0,16},{8,24},{16,0},{24,8},{1,17},{9,25},{17,1},{25,9},{2,18},{10... | collective-permute-start | bytes 2162696 | tf_op jit(solution)/shard_map/ppermute | solution.py:430
  59.1 31.5 %collective-permute-start.1 = (bf16[256,1408]{1,0:T(8,128)(2,1)S(1)}, bf16[256,1408]{1,0:T(8,128)(2,1)S(1)}, u32[]{:S(2)}, u32[]{:S(2)}) collective-permute-start(bf16[256,1408]{1,0:T(8,128)(2,1)S(1)} %bitcast.106), channel_id=1, source_target_pairs={{0,8},{8,0},{16,24},{24,16},{1,9},{9,1},{17,25},{25,17},{2,10},{10... | collective-permute-start | bytes 2162696 | tf_op jit(solution)/shard_map/ppermute | solution.py:430
  59.6 32.5 %collective-permute-start.2 = (bf16[256,1408]{1,0:T(8,128)(2,1)S(1)}, bf16[256,1408]{1,0:T(8,128)(2,1)S(1)}, u32[]{:S(2)}, u32[]{:S(2)}) collective-permute-start(bf16[256,1408]{1,0:T(8,128)(2,1)S(1)} %bitcast.103), channel_id=1, source_target_pairs={{0,16},{8,24},{16,0},{24,8},{1,17},{9,25},{17,1},{25,9},{2,18},{10... | collective-permute-start | bytes 2162696 | tf_op jit(solution)/shard_map/ppermute | solution.py:430
  75.1 30.7 %collective-permute-start.4 = (bf16[256,1408]{1,0:T(8,128)(2,1)S(1)}, bf16[256,1408]{1,0:T(8,128)(2,1)S(1)}, u32[]{:S(2)}, u32[]{:S(2)}) collective-permute-start(bf16[256,1408]{1,0:T(8,128)(2,1)S(1)} %collective-permute-done), channel_id=1, source_target_pairs={{0,16},{8,24},{16,0},{24,8},{1,17},{9,25},{17,1},{25,9},{2,18},{10... | collective-permute-start | bytes 2162696 | tf_op jit(solution)/shard_map/ppermute | solution.py:430
  76.6 30.1 %collective-permute-start.5 = (bf16[256,1408]{1,0:T(8,128)(2,1)S(1)}, bf16[256,1408]{1,0:T(8,128)(2,1)S(1)}, u32[]{:S(2)}, u32[]{:S(2)}) collective-permute-start(bf16[256,1408]{1,0:T(8,128)(2,1)S(1)} %collective-permute-done.3), channel_id=1, source_target_pairs={{0,8},{8,0},{16,24},{24,16},{1,9},{9,1},{17,25},{25,17},{2,10},{10... | collective-permute-start | bytes 2162696 | tf_op jit(solution)/shard_map/ppermute | solution.py:430
  247.7 97.4 %all-to-all-start.1 = ((bf16[4,256,2048]{2,1,0:T(8,128)(2,1)}), bf16[4,256,2048]{2,1,0:T(8,128)(2,1)}, u32[]{:S(2)}, u32[]{:S(2)}) async-start(bf16[4,256,2048]{2,1,0:T(8,128)(2,1)} %pair_product.2), calls=%async_computation.2 | async-start | bytes 8388608 | tf_op jit(solution)/shard_map/all_to_all | solution.py:487
  252.6 118.7 %all-gather.8.cloned.1.call-start = ((), (), s32[]{:S(2)}) async-start(), calls=%async_computation.7 | async-start | bytes 5242880 | tf_op jit(solution)/shard_map/all_gather | solution.py:751
  345.1 26.2 %collective-permute-start.16 = (bf16[256,2048]{1,0:T(8,128)(2,1)}, bf16[256,2048]{1,0:T(8,128)(2,1)}, u32[]{:S(2)}, u32[]{:S(2)}) collective-permute-start(bf16[256,2048]{1,0:T(8,128)(2,1)} %get-tuple-element.98), channel_id=1, source_target_pairs={{0,2},{1,3},{2,4},{3,5},{4,6},{5,7},{6,0},{7,1},{8,10},{9,11},{10,... | collective-permute-start | bytes 3145736 | tf_op jit(solution)/shard_map/ppermute | solution.py:482
  371.3 47.3 %collective-permute-start.17 = (bf16[512,1408]{1,0:T(8,128)(2,1)}, bf16[512,1408]{1,0:T(8,128)(2,1)S(1)}, u32[]{:S(2)}, u32[]{:S(2)}) collective-permute-start(bf16[512,1408]{1,0:T(8,128)(2,1)} %pad_maximum_fusion.1), channel_id=1, source_target_pairs={{0,8},{8,0},{16,24},{24,16},{1,9},{9,1},{17,25},{25,17},{2,10},{10... | collective-permute-start | bytes 4325384 | tf_op jit(solution)/shard_map/ppermute | solution.py:430
  372.8 45.8 %collective-permute-start.18 = (bf16[512,1408]{1,0:T(8,128)(2,1)}, bf16[512,1408]{1,0:T(8,128)(2,1)S(1)}, u32[]{:S(2)}, u32[]{:S(2)}) collective-permute-start(bf16[512,1408]{1,0:T(8,128)(2,1)} %pad_maximum_fusion.2), channel_id=1, source_target_pairs={{0,16},{8,24},{16,0},{24,8},{1,17},{9,25},{17,1},{25,9},{2,18},{10... | collective-permute-start | bytes 4325384 | tf_op jit(solution)/shard_map/ppermute | solution.py:430
  374.3 44.3 %collective-permute-start.19 = (bf16[256,2048]{1,0:T(8,128)(2,1)S(1)}, bf16[256,2048]{1,0:T(8,128)(2,1)}, u32[]{:S(2)}, u32[]{:S(2)}) collective-permute-start(bf16[256,2048]{1,0:T(8,128)(2,1)S(1)} %copy-done.39), channel_id=1, source_target_pairs={{0,4},{1,5},{2,6},{3,7},{4,0},{5,1},{6,2},{7,3},{8,12},{9,13},{10,... | collective-permute-start | bytes 3145736 | tf_op jit(solution)/shard_map/ppermute | solution.py:482
  422.3 18.3 %collective-permute-start.20 = (bf16[256,1408]{1,0:T(8,128)(2,1)}, bf16[256,1408]{1,0:T(8,128)(2,1)S(1)}, u32[]{:S(2)}, u32[]{:S(2)}) collective-permute-start(bf16[256,1408]{1,0:T(8,128)(2,1)} %get-tuple-element.107), channel_id=1, source_target_pairs={{0,16},{8,24},{16,0},{24,8},{1,17},{9,25},{17,1},{25,9},{2,18},{10... | collective-permute-start | bytes 2162696 | tf_op jit(solution)/shard_map/ppermute | solution.py:430
  424.8 24.8 %collective-permute-start.22 = (bf16[256,2048]{1,0:T(8,128)(2,1)}, bf16[256,2048]{1,0:T(8,128)(2,1)S(1)}, u32[]{:S(2)}, u32[]{:S(2)}) collective-permute-start(bf16[256,2048]{1,0:T(8,128)(2,1)} %get-tuple-element.115), channel_id=1, source_target_pairs={{0,6},{1,7},{2,0},{3,1},{4,2},{5,3},{6,4},{7,5},{8,14},{9,15},{10,... | collective-permute-start | bytes 3145736 | tf_op jit(solution)/shard_map/ppermute | solution.py:482
  450.6 39.0 %all-to-all-start.2 = ((bf16[8,64,1408]{2,1,0:T(8,128)(2,1)}), bf16[8,64,1408]{2,1,0:T(8,128)(2,1)S(1)}, u32[]{:S(2)}, u32[]{:S(2)}) async-start(bf16[8,64,1408]{2,1,0:T(8,128)(2,1)} %bitcast.95), calls=%async_computation.3 | async-start | bytes 2883584 | tf_op jit(solution)/shard_map/all_to_all | solution.py:732
  461.8 21.5 %collective-permute-start.23 = (f32[208,128]{1,0:T(8,128)}, f32[208,128]{1,0:T(8,128)}, u32[]{:S(2)}, u32[]{:S(2)}) collective-permute-start(f32[208,128]{1,0:T(8,128)} %pad_bitcast_fusion), channel_id=1, source_target_pairs={{0,8},{8,0},{16,24},{24,16},{1,9},{9,1},{17,25},{25,17},{2,10},{10... | collective-permute-start | bytes 319496 | tf_op jit(solution)/shard_map/ppermute | solution.py:430
  495.6 19.6 %collective-permute-start.30 = (bf16[32,8512]{1,0:T(8,128)(2,1)}, bf16[32,8512]{1,0:T(8,128)(2,1)}, u32[]{:S(2)}, u32[]{:S(2)}) collective-permute-start(bf16[32,8512]{1,0:T(8,128)(2,1)} %get-tuple-element.174.refs_0_), channel_id=1, source_target_pairs={{0,8},{8,0},{16,24},{24,16},{1,9},{9,1},{17,25},{25,17},{2,10},{10... | collective-permute-start | bytes 1634312 | tf_op jit(solution)/shard_map/ppermute | solution.py:430
  497.0 19.4 %collective-permute-start.33 = (bf16[32,8512]{1,0:T(8,128)(2,1)}, bf16[32,8512]{1,0:T(8,128)(2,1)}, u32[]{:S(2)}, u32[]{:S(2)}) collective-permute-start(bf16[32,8512]{1,0:T(8,128)(2,1)} %get-tuple-element.173.refs_1_), channel_id=1, source_target_pairs={{0,16},{8,24},{16,0},{24,8},{1,17},{9,25},{17,1},{25,9},{2,18},{10... | collective-permute-start | bytes 1634312 | tf_op jit(solution)/shard_map/ppermute | solution.py:430
  515.2 22.2 %collective-permute-start.34 = (bf16[32,8512]{1,0:T(8,128)(2,1)}, bf16[32,8512]{1,0:T(8,128)(2,1)S(1)}, u32[]{:S(2)}, u32[]{:S(2)}) collective-permute-start(bf16[32,8512]{1,0:T(8,128)(2,1)} %collective-permute-done.30.refs_2_), channel_id=1, source_target_pairs={{0,16},{8,24},{16,0},{24,8},{1,17},{9,25},{17,1},{25,9},{2,18},{10... | collective-permute-start | bytes 1634312 | tf_op jit(solution)/shard_map/ppermute | solution.py:430
  516.4 21.0 %collective-permute-start.35 = (bf16[32,8512]{1,0:T(8,128)(2,1)}, bf16[32,8512]{1,0:T(8,128)(2,1)S(1)}, u32[]{:S(2)}, u32[]{:S(2)}) collective-permute-start(bf16[32,8512]{1,0:T(8,128)(2,1)} %collective-permute-done.33.refs_5_), channel_id=1, source_target_pairs={{0,8},{8,0},{16,24},{24,16},{1,9},{9,1},{17,25},{25,17},{2,10},{10... | collective-permute-start | bytes 1634312 | tf_op jit(solution)/shard_map/ppermute | solution.py:430
  (61 other events, 429.6 us)
Sparse Core Ops, SparseCore 0:
  55.0 80.9 all-gather.3
  137.6 80.9 all-gather.5
  247.8 52.3 reduce-scatter.1
  305.0 54.1 all-gather.7
